TPU v7x, 32 devices: a whole 2x2x4 slice. The times are simulated.
32 devices in a mesh: dp: 4 (over y, x), space: 8 (over z, core).
Axes of the slice: x: 2, y: 2, z: 4, core: 2. Of those that a mesh axis runs over, the one named last changes fastest.
Arguments:
- block_input: bfloat16 [4, 2304, 8, 192], P('dp', 'space'), may hold values from -6 to 6
- cotangent: bfloat16 [4, 2304, 8, 192], P('dp', 'space'), may hold values from -6 to 6
- params: float32 [1216512], P(('dp', 'space')), as said below
- send_rows: int32 [4, 8, 8, 288], P('dp', None, 'space'), may hold values from 0 to 2303, as said below
- window_band: int32 [4, 256], P('dp', 'space'), may hold values from 0 to 19
- level_count: int32 [4, 2304], P('dp', 'space'), may hold values from 1 to 8
Outputs:
- block_output: bfloat16 [4, 2304, 8, 192], P('dp', 'space')
- input_grad: float32 [4, 2304, 8, 192], P('dp', 'space')
- param_grad: float32 [1216512], P(('dp', 'space'))
Inputs may be any that keep to these rules, and one draw needn't show every extreme that they name: For each sample and each source device e, the entries send_rows[s, :, e, :] are a permutation of 0 to 2303. `params`: laid out in the order of the statement's segments; the padding is unused.
All inputs are finite; a program needn't handle non-finite values.
Results may differ from a plain program's by a relative error of at most 0.013.
The roundings to bfloat16 on the way count: a program that leaves them out, or rounds other values in their place, can miss the bound.
Values may be sent and summed in bfloat16 or wider, within the bound.
No kernel may reach another device: no remote copies, remote signals or barrier semaphores. Data moves between devices by JAX's collectives and lax.ppermute only.
A program may use at most 192 MiB of HBM per device.

v0:
```python
import jax
import jax.numpy as jnp
from jax import lax
from jax.sharding import PartitionSpec as P

D = 192
HEADS = 6
HEAD_DIM = 32
FF = 768
LEVELS = 8
WIN = 72
LAT_BANDS = 20


norm_eps = 1e-05


def param_layout():
    return [
        ("norm1_gain", (D,)),
        ("norm1_shift", (D,)),
        ("qkv1", (D, 3 * D)),
        ("proj1", (D, D)),
        ("proj1_bias", (D,)),
        ("norm2_gain", (D,)),
        ("norm2_shift", (D,)),
        ("qkv2", (D, 3 * D)),
        ("proj2", (D, D)),
        ("proj2_bias", (D,)),
        ("norm3_gain", (D,)),
        ("norm3_shift", (D,)),
        ("mlp_in", (D, FF)),
        ("mlp_in_bias", (FF,)),
        ("mlp_out", (FF, D)),
        ("mlp_out_bias", (D,)),
        ("earth_bias", (LAT_BANDS, HEADS, WIN, WIN)),
    ]


def unpack_params(flat_values):
    pieces = {}
    offset = 0
    for entry_name, entry_shape in param_layout():
        entry_size = 1
        for extent in entry_shape:
            entry_size = entry_size * extent
        pieces[entry_name] = flat_values[offset : offset + entry_size].reshape(entry_shape)
        offset = offset + entry_size
    return pieces


def layer_norm(rows_in, norm_gain, norm_shift):
    row_mean = jnp.mean(rows_in, axis=-1, keepdims=True)
    centered = rows_in - row_mean
    row_var = jnp.mean(centered * centered, axis=-1, keepdims=True)
    return centered * lax.rsqrt(row_var + norm_eps) * norm_gain + norm_shift


def plain_product(left, right):
    return jnp.dot(left, right, preferred_element_type=jnp.float32)


def left_product(left, right):
    return lax.dot_general(
        left, right, (((0,), (0,)), ((), ())), preferred_element_type=jnp.float32
    )


def right_product(left, right):
    return lax.dot_general(
        left, right, (((1,), (1,)), ((), ())), preferred_element_type=jnp.float32
    )


def as_float(value):
    return value.astype(jnp.float32)


def window_forward(pieces, shifted, selector):
    score_scale = HEAD_DIM ** (-0.5)
    normed, norm_back = jax.vjp(
        layer_norm,
        as_float(shifted),
        as_float(pieces["norm1_gain"]),
        as_float(pieces["norm1_shift"]),
    )
    normed_bf = normed.astype(jnp.bfloat16)
    packed = (
        plain_product(normed_bf, pieces["qkv1"])
        .astype(jnp.bfloat16)
        .reshape(-1, WIN, 3, HEADS, HEAD_DIM)
    )
    bias_rows = plain_product(selector, pieces["earth_bias"].reshape(LAT_BANDS, -1)).reshape(
        -1, HEADS, WIN, WIN
    )
    scores = (
        jnp.einsum(
            "uqhe,ukhe->uhqk", packed[:, :, 0], packed[:, :, 1], preferred_element_type=jnp.float32
        )
        * score_scale
        + bias_rows
    )
    attn_prob = jax.nn.softmax(scores, axis=-1)
    attn_bf = attn_prob.astype(jnp.bfloat16)
    mixed_heads = (
        jnp.einsum("uhqk,ukhe->uqhe", attn_bf, packed[:, :, 2], preferred_element_type=jnp.float32)
        .reshape(-1, D)
        .astype(jnp.bfloat16)
    )
    window_out = plain_product(mixed_heads, pieces["proj1"]) + as_float(pieces["proj1_bias"])
    return (window_out, (norm_back, normed_bf, packed, attn_prob, attn_bf, mixed_heads))


def window_backward(pieces, saved, grad_out, selector):
    score_scale = HEAD_DIM ** (-0.5)
    norm_back, normed_bf, packed, attn_prob, attn_bf, mixed_heads = saved
    gradient = {}
    gradient["proj1"] = left_product(mixed_heads, grad_out)
    gradient["proj1_bias"] = jnp.sum(as_float(grad_out), axis=0)
    grad_mixed = (
        right_product(grad_out, pieces["proj1"])
        .astype(jnp.bfloat16)
        .reshape(-1, WIN, HEADS, HEAD_DIM)
    )
    grad_prob = jnp.einsum(
        "uqhe,ukhe->uhqk", grad_mixed, packed[:, :, 2], preferred_element_type=jnp.float32
    )
    grad_value = jnp.einsum(
        "uhqk,uqhe->ukhe", attn_bf, grad_mixed, preferred_element_type=jnp.float32
    )
    grad_scores = (
        attn_prob * (grad_prob - jnp.sum(attn_prob * grad_prob, axis=-1, keepdims=True))
    ).astype(jnp.bfloat16)
    gradient["earth_bias"] = left_product(
        selector, grad_scores.reshape(selector.shape[0], -1)
    ).reshape(LAT_BANDS, HEADS, WIN, WIN)
    grad_query = (
        jnp.einsum(
            "uhqk,ukhe->uqhe", grad_scores, packed[:, :, 1], preferred_element_type=jnp.float32
        )
        * score_scale
    )
    grad_key = (
        jnp.einsum(
            "uhqk,uqhe->ukhe", grad_scores, packed[:, :, 0], preferred_element_type=jnp.float32
        )
        * score_scale
    )
    grad_packed = (
        jnp.stack([grad_query, grad_key, grad_value], axis=2)
        .astype(jnp.bfloat16)
        .reshape(-1, 3 * D)
    )
    gradient["qkv1"] = left_product(normed_bf, grad_packed)
    grad_tokens, gradient["norm1_gain"], gradient["norm1_shift"] = norm_back(
        right_product(grad_packed, pieces["qkv1"])
    )
    return (grad_tokens, gradient)


def column_forward(pieces, after_window, level_rows):
    score_scale = HEAD_DIM ** (-0.5)
    normed, norm2_back = jax.vjp(
        layer_norm, after_window, as_float(pieces["norm2_gain"]), as_float(pieces["norm2_shift"])
    )
    normed_bf = normed.astype(jnp.bfloat16)
    packed = (
        plain_product(normed_bf, pieces["qkv2"])
        .astype(jnp.bfloat16)
        .reshape(-1, LEVELS, 3, HEADS, HEAD_DIM)
    )
    scores = (
        jnp.einsum(
            "cqhe,ckhe->hqkc", packed[:, :, 0], packed[:, :, 1], preferred_element_type=jnp.float32
        )
        * score_scale
    )
    valid_keys = jnp.arange(LEVELS, dtype=jnp.int32)[:, None] < level_rows[None, :]
    scores = jnp.where(valid_keys, scores, -jnp.inf)
    attn_prob = jax.nn.softmax(scores, axis=2)
    attn_bf = attn_prob.astype(jnp.bfloat16)
    mixed_heads = (
        jnp.einsum("hqkc,ckhe->cqhe", attn_bf, packed[:, :, 2], preferred_element_type=jnp.float32)
        .reshape(-1, D)
        .astype(jnp.bfloat16)
    )
    middle = after_window + (
        plain_product(mixed_heads, pieces["proj2"]) + as_float(pieces["proj2_bias"])
    )
    normed3, norm3_back = jax.vjp(
        layer_norm, middle, as_float(pieces["norm3_gain"]), as_float(pieces["norm3_shift"])
    )
    normed3_bf = normed3.astype(jnp.bfloat16)
    pre_gelu = plain_product(normed3_bf, pieces["mlp_in"]) + as_float(pieces["mlp_in_bias"])
    activation, gelu_back = jax.vjp(jax.nn.gelu, pre_gelu)
    active_bf = activation.astype(jnp.bfloat16)
    output = middle + (
        plain_product(active_bf, pieces["mlp_out"]) + as_float(pieces["mlp_out_bias"])
    )
    saved = (
        norm2_back,
        normed_bf,
        packed,
        attn_prob,
        attn_bf,
        mixed_heads,
        norm3_back,
        normed3_bf,
        gelu_back,
        active_bf,
    )
    return (output, saved)


def column_backward(pieces, saved, grad_out):
    score_scale = HEAD_DIM ** (-0.5)
    (
        norm2_back,
        normed_bf,
        packed,
        attn_prob,
        attn_bf,
        mixed_heads,
        norm3_back,
        normed3_bf,
        gelu_back,
        active_bf,
    ) = saved
    gradient = {}
    grad_mlp = grad_out.astype(jnp.bfloat16)
    gradient["mlp_out"] = left_product(active_bf, grad_mlp)
    gradient["mlp_out_bias"] = jnp.sum(as_float(grad_mlp), axis=0)
    grad_pre = gelu_back(right_product(grad_mlp, pieces["mlp_out"]))[0].astype(jnp.bfloat16)
    gradient["mlp_in"] = left_product(normed3_bf, grad_pre)
    gradient["mlp_in_bias"] = jnp.sum(as_float(grad_pre), axis=0)
    grad_norm3, gradient["norm3_gain"], gradient["norm3_shift"] = norm3_back(
        right_product(grad_pre, pieces["mlp_in"])
    )
    grad_middle = grad_out + grad_norm3
    grad_attn = grad_middle.astype(jnp.bfloat16)
    gradient["proj2"] = left_product(mixed_heads, grad_attn)
    gradient["proj2_bias"] = jnp.sum(as_float(grad_attn), axis=0)
    grad_mixed = (
        right_product(grad_attn, pieces["proj2"])
        .astype(jnp.bfloat16)
        .reshape(-1, LEVELS, HEADS, HEAD_DIM)
    )
    grad_prob = jnp.einsum(
        "cqhe,ckhe->hqkc", grad_mixed, packed[:, :, 2], preferred_element_type=jnp.float32
    )
    grad_value = jnp.einsum(
        "hqkc,cqhe->ckhe", attn_bf, grad_mixed, preferred_element_type=jnp.float32
    )
    grad_scores = (
        attn_prob * (grad_prob - jnp.sum(attn_prob * grad_prob, axis=2, keepdims=True))
    ).astype(jnp.bfloat16)
    grad_query = (
        jnp.einsum(
            "hqkc,ckhe->cqhe", grad_scores, packed[:, :, 1], preferred_element_type=jnp.float32
        )
        * score_scale
    )
    grad_key = (
        jnp.einsum(
            "hqkc,cqhe->ckhe", grad_scores, packed[:, :, 0], preferred_element_type=jnp.float32
        )
        * score_scale
    )
    grad_packed = (
        jnp.stack([grad_query, grad_key, grad_value], axis=2)
        .astype(jnp.bfloat16)
        .reshape(-1, 3 * D)
    )
    gradient["qkv2"] = left_product(normed_bf, grad_packed)
    grad_norm2, gradient["norm2_gain"], gradient["norm2_shift"] = norm2_back(
        right_product(grad_packed, pieces["qkv2"])
    )
    return (grad_middle + grad_norm2, gradient)


def body(block_input, cotangent, params, send_rows, window_band, level_count):
    model_width = block_input.shape[-1]
    rows_dev = block_input.shape[1] * block_input.shape[2]
    flat_in = block_input[0].reshape(rows_dev, model_width)
    routes = send_rows[0, :, 0, :]
    route_flat = routes.reshape(-1)
    level_rows = level_count[0]
    selector = (window_band[0][:, None] == jnp.arange(LAT_BANDS, dtype=jnp.int32)[None, :]).astype(
        jnp.bfloat16
    )
    gathered = lax.all_gather(params.astype(jnp.bfloat16), ("dp", "space"), axis=0, tiled=True)
    pieces = unpack_params(gathered)
    shifted = lax.all_to_all(
        flat_in[routes], "space", split_axis=0, concat_axis=0, tiled=True
    ).reshape(rows_dev, model_width)
    window_out, window_saved = window_forward(pieces, shifted, selector)
    returned = lax.all_to_all(
        window_out.astype(jnp.bfloat16).reshape(routes.shape[0], routes.shape[1], model_width),
        "space",
        split_axis=0,
        concat_axis=0,
        tiled=True,
    )
    branch = (
        jnp.zeros((rows_dev, model_width), jnp.bfloat16)
        .at[route_flat]
        .set(returned.reshape(-1, model_width))
    )
    after_window = as_float(flat_in) + as_float(branch)
    output, column_saved = column_forward(pieces, after_window, level_rows)
    again = unpack_params(
        lax.all_gather(params.astype(jnp.bfloat16), ("dp", "space"), axis=0, tiled=True)
    )
    output_again, column_saved = column_forward(again, after_window, level_rows)
    grad_after, column_grads = column_backward(
        again, column_saved, as_float(cotangent[0].reshape(rows_dev, model_width))
    )
    grad_branch = grad_after.astype(jnp.bfloat16)
    grad_window = lax.all_to_all(
        grad_branch[routes], "space", split_axis=0, concat_axis=0, tiled=True
    ).reshape(rows_dev, model_width)
    window_again, window_saved = window_forward(again, shifted, selector)
    grad_shifted, window_grads = window_backward(again, window_saved, grad_window, selector)
    sent_back = lax.all_to_all(
        grad_shifted.astype(jnp.bfloat16).reshape(routes.shape[0], routes.shape[1], model_width),
        "space",
        split_axis=0,
        concat_axis=0,
        tiled=True,
    )
    input_grad = grad_after + jnp.zeros((rows_dev, model_width), jnp.float32).at[route_flat].set(
        as_float(sent_back.reshape(-1, model_width))
    )
    gradient = dict(column_grads)
    gradient.update(window_grads)
    flat_grad = jnp.concatenate(
        [gradient[entry_name].reshape(-1) for entry_name, entry_shape in param_layout()]
    )
    flat_grad = jnp.pad(flat_grad, (0, gathered.shape[0] - flat_grad.shape[0]))
    owned = lax.psum_scatter(flat_grad, ("dp", "space"), scatter_dimension=0, tiled=True)
    return (
        output.astype(jnp.bfloat16).reshape(block_input.shape),
        input_grad.reshape(block_input.shape),
        owned,
    )


def solution(mesh):
    return jax.shard_map(
        body,
        mesh=mesh,
        in_specs=(
            P("dp", "space", None, None),
            P("dp", "space", None, None),
            P(("dp", "space")),
            P("dp", None, "space", None),
            P("dp", "space"),
            P("dp", "space"),
        ),
        out_specs=(P("dp", "space", None, None), P("dp", "space", None, None), P(("dp", "space"))),
        check_vma=False,
    )
```

profile of v0, /device:TPU:0, one launch (start us, length us, event | category | flops | bytes accessed | tf_op | source)
XLA Modules:
  0.0 775.5 jit_solution(8683210609197429767)
XLA Ops:
  9.8 6.6 gather_fusion
  27.7 34.8 %all-to-all-done = bf16[8,288,192]{1,2,0:T(8,128)(2,1)S(1)} async-done(((bf16[8,288,192]{1,2,0:T(8,128)(2,1)}), bf16[8,288,192]{1,2,0:T(8,128)(2,1)S(1)}, u32[]{:S(2)}, u32[]{:S(2)}) %all-to-all-start) | async-done | bytes 884768 | tf_op jit(solution)/shard_map/all_to_all | solution.py:293
  63.7 23.6 %all-gather.3.cloned.1.call-done = bf16[32,1,38016]{2,1,0:T(2,128)(2,1)} async-done(((bf16[1,1,38016]{2,1,0:T(2,128)(2,1)}), bf16[32,1,38016]{2,1,0:T(2,128)(2,1)}) %all-gather.3.cloned.1.call-update) | async-done | bytes 2433040 | tf_op jit(solution)/shard_map/all_gather | solution.py:291
  87.3 16.6 %reduce.7 = bf16[32,38016]{1,0:T(8,128)(2,1)} reduce(bf16[32,1,38016]{2,1,0:T(2,128)(2,1)} %all-gather.3.cloned.1.call-done, bf16[]{:T(256)} %constant.65), dimensions={1}, to_apply=%all-gather.reduce_sub_computation | reduce | bytes 4866050 | tf_op jit(solution)/shard_map/all_gather | solution.py:291
  133.4 12.4 %reshape.376 = bf16[32,72,3,6,32]{1,0,4,3,2:T(8,128)(2,1)} reshape(bf16[2304,576]{0,1:T(8,128)(2,1)} %convolution_convert_fusion.1) | data formatting | bytes 5308416 | tf_op jit(solution)/shard_map/reshape | solution.py:91
  155.1 9.1 %copy.181 = f32[32,6,72,72]{2,3,1,0:T(8,128)} copy(f32[32,6,72,72]{3,0,2,1:T(8,128)} %fusion.32) | data formatting | bytes 7962624 | tf_op jit(solution)/shard_map/dot_general | solution.py:60
  164.2 6.6 multiply_add_fusion
  175.8 8.9 %fusion.51 = bf16[32,72,6,32]{1,3,2,0:T(8,128)(2,1)} fusion(bf16[32,72,1,6,32]{1,0,4,3,2:T(8,128)(2,1)S(1)} %copy-done.37, f32[32,6,72]{2,1,0:T(8,128)S(1)} %get-tuple-element.50, f32[32,6,72,72]{2,3,1,0:T(8,128)} %copy-done.8), kind=kOutput, calls=%fused_computation.95 | convolution fusion | flops 67143240 | bytes 5806080 | tf_op jit(solution)/shard_map/uhqk,ukhe->uqhe/dot_general | solution.py:106
  206.2 24.4 %all-to-all-done.1 = bf16[8,288,192]{1,2,0:T(8,128)(2,1)S(1)} async-done(((bf16[8,288,192]{1,2,0:T(8,128)(2,1)}), bf16[8,288,192]{1,2,0:T(8,128)(2,1)S(1)}, u32[]{:S(2)}, u32[]{:S(2)}) %all-to-all-start.1) | async-done | bytes 884768 | tf_op jit(solution)/shard_map/all_to_all | solution.py:297
  232.2 13.5 %scatter_custom_fusion = bf16[2304,192]{1,0:T(8,128)(2,1)S(1)} fusion(s32[2304]{0:T(1024)S(1)} %fusion.80, bf16[2304,192]{1,0:T(8,128)(2,1)} %bitcast.172, bf16[]{:T(256)} %constant.15.clone.1), kind=kCustom, calls=%fused_computation.110 | custom fusion | bytes 885248 | tf_op jit(solution)/shard_map/scatter | solution.py:307
  254.4 13.6 %reshape.381 = bf16[288,8,3,6,32]{4,3,2,1,0:T(8,128)(2,1)} reshape(bf16[2304,576]{1,0:T(8,128)(2,1)S(1)} %copy.188) | data formatting | bytes 5308416 | tf_op jit(solution)/shard_map/reshape | solution.py:170
  268.0 14.1 %slice_bitcast_fusion.1 = (bf16[288,8,6,32]{3,2,1,0:T(8,128)(2,1)}, bf16[288,8,6,32]{3,2,1,0:T(8,128)(2,1)}, bf16[288,8,6,32]{3,2,1,0:T(8,128)(2,1)}, bf16[288,8...) fusion(bf16[288,8,3,6,32]{4,3,2,1,0:T(8,128)(2,1)} %reshape.381), kind=kLoop, calls=%fused_computation.163 | loop fusion | bytes 7962624 | tf_op jit(solution)/shard_map/squeeze | solution.py:174
  308.8 6.6 convert_element_type.228
  350.5 7.2 fusion.16
  399.2 14.4 %copy.210 = bf16[288,8,3,6,32]{4,3,2,1,0:T(8,128)(2,1)} copy(bf16[288,8,3,6,32]{0,4,3,2,1:T(8,128)(2,1)S(1)} %maximum_convert_fusion) | data formatting | bytes 5308416 | tf_op jit(solution)/shard_map/convert_element_type | solution.py:271
  413.6 16.1 %convert_element_type.243 = bf16[2304,576]{1,0:T(8,128)(2,1)} reshape(bf16[288,8,3,6,32]{4,3,2,1,0:T(8,128)(2,1)} %copy.210) | data formatting | bytes 5308416 | tf_op jit(solution)/shard_map/convert_element_type | solution.py:271
  438.3 7.4 gather_fusion.1
  487.6 8.8 %fusion.48 = bf16[32,72,1,6,32]{1,4,3,0,2:T(8,128)(2,1)} fusion(bf16[32,72,6,32]{1,0,3,2:T(8,128)(2,1)S(1)} %reshape.387, f32[32,6,72]{2,1,0:T(8,128)S(1)} %copy-done.47, f32[32,6,72,72]{2,3,1,0:T(8,128)} %copy-done.8), kind=kOutput, calls=%fused_computation.94 | convolution fusion | flops 67143240 | bytes 5806080 | tf_op jit(solution)/shard_map/uhqk,uqhe->ukhe/dot_general | solution.py:128
  496.4 9.2 %multiply_reduce_fusion = (f32[32,6,72]{2,1,0:T(8,128)S(1)}, f32[32,6,72,72]{2,3,1,0:T(8,128)}) fusion(f32[32,6,72,72]{2,3,1,0:T(8,128)} %get-tuple-element.51, f32[32,6,72]{2,1,0:T(8,128)S(1)} %copy-done.47, bf16[32,72,1,6,32]{1,0,4,3,2:T(8,128)(2,1)S(1)} %copy-done.38, bf16[32,72,6,32]{1,0,3,2:T(8,128)(2,1)S(1)} %reshape.387), kind=kOutput, calls=%fused_computation.19 | convolution fusion | flops 66673152 | bytes 9842688 | tf_op jit(solution)/shard_map/uqhe,ukhe->uhqk/dot_general | solution.py:125
  522.6 6.6 reshape.396
  536.8 8.1 %convert_element_type.247 = bf16[2304,576]{0,1:T(8,128)(2,1)S(1)} reshape(bf16[32,72,3,6,32]{1,0,4,3,2:T(8,128)(2,1)} %copy.217) | data formatting | bytes 5308416 | tf_op jit(solution)/shard_map/convert_element_type | solution.py:151
  565.5 51.6 %concatenate.3 = f32[1214400]{0:T(1024)} concatenate(f32[192]{0:T(256)S(1)} %get-tuple-element.6, f32[192]{0:T(256)S(1)} %get-tuple-element.14, f32[110592]{0:T(1024)} %reshape.390, f32[36864]{0:T(1024)} %reshape.391, f32[192]{0:T(256)S(1)} %convert_reduce_fusion.2, f32[192]{0:T(256)S(1)} %copy-done.89, f32[192]{0:T(256)S(1)} %copy-done.90, f32[110592]{0:T(1024)S(1)} %copy-done.36, ...), dimensions={0} | concatenate | bytes 9715200 | tf_op jit(solution)/shard_map/concatenate | solution.py:336
  629.3 14.6 %scatter_custom_fusion.1 = f32[2304,192]{1,0:T(8,128)} fusion(s32[2304]{0:T(1024)} %copy-done.76, f32[2304,192]{1,0:T(8,128)S(1)} %bitcast.170, f32[]{:T(128)} %constant.18.clone.1), kind=kCustom, calls=%fused_computation.104 | custom fusion | bytes 1769984 | tf_op jit(solution)/shard_map/scatter | solution.py:331
  653.4 113.4 %all-reduce.4.cloned.1.call-done = f32[1216512]{0:T(1024)} async-done(((f32[1216512]{0:T(1024)}), f32[1216512]{0:T(1024)}) %all-reduce.4.cloned.1.call-update) | async-done | bytes 4866064
  (337 shorter events, 311.7 us)
Async XLA Ops:
  7.2 80.1 %all-gather.3.cloned.1.call-start = ((), (), s32[]{:S(2)}) async-start(), calls=%async_computation.4 | async-start | bytes 5018112 | tf_op jit(solution)/shard_map/all_gather | solution.py:291
  17.9 44.7 %all-to-all-start = ((bf16[8,288,192]{1,2,0:T(8,128)(2,1)}), bf16[8,288,192]{1,2,0:T(8,128)(2,1)S(1)}, u32[]{:S(2)}, u32[]{:S(2)}) async-start(bf16[8,288,192]{1,2,0:T(8,128)(2,1)} %copy.175), calls=%async_computation | async-start | bytes 2359296 | tf_op jit(solution)/shard_map/all_to_all | solution.py:293
  25.0 222.2 %copy-start.12 = (bf16[2304,192]{0,1:T(8,128)(2,1)}, bf16[2304,192]{0,1:T(8,128)(2,1)S(1)}, u32[]{:S(2)}) copy-start(bf16[2304,192]{0,1:T(8,128)(2,1)S(1)} %copy.174) | copy-start | bytes 2654212
  27.7 204.5 %copy-start.76 = (s32[2304]{0:T(1024)}, s32[2304]{0:T(1024)S(1)}, u32[]{:S(2)}) copy-start(s32[2304]{0:T(1024)S(1)} %fusion.80) | copy-start | bytes 27652
  62.6 66.2 %copy-start.3 = (bf16[8,288,192]{1,2,0:T(8,128)(2,1)}, bf16[8,288,192]{1,2,0:T(8,128)(2,1)S(1)}, u32[]{:S(2)}) copy-start(bf16[8,288,192]{1,2,0:T(8,128)(2,1)S(1)} %all-to-all-done) | copy-start | bytes 2654212
  62.8 65.9 %copy-start.53 = (f32[8,288]{1,0:T(8,128)}, f32[8,288]{1,0:T(8,128)S(1)}, u32[]{:S(2)}) copy-start(f32[8,288]{1,0:T(8,128)S(1)} %broadcast_multiply_fusion.2) | copy-start | bytes 27652
  111.3 17.5 %copy-start.67 = (f32[192]{0:T(256)}, f32[192]{0:T(256)S(1)}, u32[]{:S(2)}) copy-start(f32[192]{0:T(256)S(1)} %get-tuple-element.39) | copy-start | bytes 2308
  111.3 135.9 %copy-start.78 = (f32[192]{0:T(256)}, f32[192]{0:T(256)S(1)}, u32[]{:S(2)}) copy-start(f32[192]{0:T(256)S(1)} %get-tuple-element.36) | copy-start | bytes 2308
  111.3 135.9 %copy-start.91 = (f32[192]{0:T(256)}, f32[192]{0:T(256)S(1)}, u32[]{:S(2)}) copy-start(f32[192]{0:T(256)S(1)} %get-tuple-element.35) | copy-start | bytes 2308
  111.3 206.9 %copy-start.93 = (f32[192]{0:T(256)}, f32[192]{0:T(256)S(1)}, u32[]{:S(2)}) copy-start(f32[192]{0:T(256)S(1)} %get-tuple-element.32) | copy-start | bytes 2308
  111.3 220.2 %copy-start.81 = (f32[192]{0:T(256)}, f32[192]{0:T(256)S(1)}, u32[]{:S(2)}) copy-start(f32[192]{0:T(256)S(1)} %get-tuple-element.33) | copy-start | bytes 2308
  197.6 33.0 %all-to-all-start.1 = ((bf16[8,288,192]{1,2,0:T(8,128)(2,1)}), bf16[8,288,192]{1,2,0:T(8,128)(2,1)S(1)}, u32[]{:S(2)}, u32[]{:S(2)}) async-start(bf16[8,288,192]{1,2,0:T(8,128)(2,1)} %copy.184), calls=%async_computation.1 | async-start | bytes 2359296 | tf_op jit(solution)/shard_map/all_to_all | solution.py:297
  203.5 43.7 %copy-start.51 = (bf16[192,576]{1,0:T(8,128)(2,1)}, bf16[192,576]{1,0:T(8,128)(2,1)S(1)}, u32[]{:S(2)}) copy-start(bf16[192,576]{1,0:T(8,128)(2,1)S(1)} %reshape.380) | copy-start | bytes 663556
  317.9 13.5 %copy-start.5 = (f32[2304,192]{0,1:T(8,128)}, f32[2304,192]{0,1:T(8,128)S(1)}, u32[]{:S(2)}) copy-start(f32[2304,192]{0,1:T(8,128)S(1)} %get-tuple-element.55) | copy-start | bytes 5308420
  332.0 102.2 %copy-start.55 = (f32[2304]{0:T(1024)}, f32[2304]{0:T(1024)S(1)}, u32[]{:S(2)}) copy-start(f32[2304]{0:T(1024)S(1)} %negate_multiply_fusion.2) | copy-start | bytes 27652
  413.6 16.2 %copy-start.13 = (bf16[2304,192]{0,1:T(8,128)(2,1)S(1)}, bf16[2304,192]{0,1:T(8,128)(2,1)}, u32[]{:S(2)}) copy-start(bf16[2304,192]{0,1:T(8,128)(2,1)} %copy-done.12) | copy-start | bytes 2654212
  413.6 16.2 %copy-start.15 = (bf16[2304,192]{0,1:T(8,128)(2,1)S(1)}, bf16[2304,192]{0,1:T(8,128)(2,1)}, u32[]{:S(2)}) copy-start(bf16[2304,192]{0,1:T(8,128)(2,1)} %copy-done.14) | copy-start | bytes 2654212
  413.6 16.2 %copy-start.52 = (bf16[192,576]{1,0:T(8,128)(2,1)S(1)}, bf16[192,576]{1,0:T(8,128)(2,1)}, u32[]{:S(2)}) copy-start(bf16[192,576]{1,0:T(8,128)(2,1)} %copy-done.51) | copy-start | bytes 663556
  413.6 16.2 %copy-start.63 = (f32[2304]{0:T(1024)S(1)}, f32[2304]{0:T(1024)}, u32[]{:S(2)}) copy-start(f32[2304]{0:T(1024)} %copy-done.62) | copy-start | bytes 27652
  413.6 16.2 %copy-start.73 = (f32[2304]{0:T(1024)S(1)}, f32[2304]{0:T(1024)}, u32[]{:S(2)}) copy-start(f32[2304]{0:T(1024)} %copy-done.72) | copy-start | bytes 27652
  413.6 16.2 %copy-start.79 = (f32[192]{0:T(256)S(1)}, f32[192]{0:T(256)}, u32[]{:S(2)}) copy-start(f32[192]{0:T(256)} %copy-done.78) | copy-start | bytes 2308
  445.8 34.0 %all-to-all-start.2 = ((bf16[8,288,192]{2,1,0:T(8,128)(2,1)}), bf16[8,288,192]{2,1,0:T(8,128)(2,1)}, u32[]{:S(2)}, u32[]{:S(2)}) async-start(bf16[8,288,192]{2,1,0:T(8,128)(2,1)} %bitcast.168), calls=%async_computation.2 | async-start | bytes 2359296 | tf_op jit(solution)/shard_map/all_to_all | solution.py:319
  553.0 74.6 %all-to-all-start.3 = ((bf16[8,288,192]{1,2,0:T(8,128)(2,1)}), bf16[8,288,192]{1,2,0:T(8,128)(2,1)}, u32[]{:S(2)}, u32[]{:S(2)}) async-start(bf16[8,288,192]{1,2,0:T(8,128)(2,1)} %copy.219), calls=%async_computation.3 | async-start | bytes 2359296 | tf_op jit(solution)/shard_map/all_to_all | solution.py:324
  557.2 209.5 %all-reduce.4.cloned.1.call-start = ((), (), s32[]{:S(2)}) async-start(), calls=%async_computation.5 | async-start | bytes 9732096
  (79 other events, 348.2 us)
Sparse Core Ops, SparseCore 0:
  11.5 75.7 all-gather.2
  621.5 145.2 all-reduce.3
where the time goes:
time: 789 us; the launch traced here: 776 us
  local copies, waits for them, and re-layouts  356 us (45%)
  waiting for transfers between devices  198 us (25%)
  matrix products  131 us (17%)
  other arithmetic  55.3 us (7%)
  starting transfers between devices  19.1 us (2%)
  between operations  15.5 us (2%)
    unnamed x3, waiting for transfers between devices  113 us
    concatenate x1, local copies, waits for them, and re-layouts, body(): jnp.concatenate([gradient[entry_name].reshape(-1) for entry_name, entry_s...  51.6 us
    all_to_all x1, waiting for transfers between devices, body(): lax.all_to_all(flat_in[routes], 'space', split_axis=0, concat_axis=0, til...  34.8 us
    convert_element_type x2, local copies, waits for them, and re-layouts, column_backward(): grad_packed = jnp.stack([grad_query, grad_key, grad_value], axis=2).astyp...  30.5 us
    all_to_all x1, waiting for transfers between devices, body(): lax.all_to_all(window_out.astype(jnp.bfloat16).reshape(routes.shape[0], r...  24.4 us
    all_gather x1, waiting for transfers between devices, body(): lax.all_gather(params.astype(jnp.bfloat16), ('dp', 'space'), axis=0, tile...  23.6 us
    dot_general x7, matrix products, plain_product(): return jnp.dot(left, right, preferred_element_type=jnp.float32)  20.4 us
    dot_general x7, matrix products, left_product(): lax.dot_general(left, right, (((0,), (0,)), ((), ())), preferred_element_...  19.5 us
  transfers between devices with their start and end apart: 6, of which 5 were waited for; matrix products, arithmetic and copies ran while one was open for 18% of the time, Pallas kernels for 0%

commit v1 on v0

--- a/solution.py
+++ b/solution.py
@@ -1,3 +1,5 @@
+import math
+
 import jax
 import jax.numpy as jnp
 from jax import lax
@@ -281,56 +283,57 @@
 def body(block_input, cotangent, params, send_rows, window_band, level_count):
     model_width = block_input.shape[-1]
     rows_dev = block_input.shape[1] * block_input.shape[2]
+    n_space, per_peer = send_rows.shape[1], send_rows.shape[3]
+    group = WIN // math.gcd(per_peer, WIN)
+    if n_space % group:
+        group = n_space
+    dest = n_space // group
+    per_dest = group * per_peer // WIN
+    member_groups = [[first + k for k in range(group)] for first in range(0, n_space, group)]
+    me = lax.axis_index("space")
     flat_in = block_input[0].reshape(rows_dev, model_width)
     routes = send_rows[0, :, 0, :]
     route_flat = routes.reshape(-1)
     level_rows = level_count[0]
-    selector = (window_band[0][:, None] == jnp.arange(LAT_BANDS, dtype=jnp.int32)[None, :]).astype(
+
+    def exchange(value):
+        return lax.all_to_all(
+            value, "space", split_axis=0, concat_axis=0, tiled=True, axis_index_groups=member_groups
+        )
+
+    def to_windows(rows):
+        picked = rows[route_flat]
+        if group > 1:
+            moved = exchange(picked).reshape(group, dest, per_peer, model_width)
+            picked = moved.transpose(1, 0, 2, 3).reshape(rows_dev, model_width)
+        return picked
+
+    def from_windows(rows):
+        if group > 1:
+            moved = rows.reshape(dest, group, per_peer, model_width).transpose(1, 0, 2, 3)
+            rows = exchange(moved.reshape(rows_dev, model_width))
+        return jnp.zeros((rows_dev, model_width), rows.dtype).at[route_flat].set(rows)
+
+    all_bands = lax.all_gather(window_band[0], "space", axis=0)
+    bands = lax.dynamic_slice(
+        all_bands, ((me % group) * dest, (me // group) * per_dest), (dest, per_dest)
+    ).reshape(-1)
+    selector = (bands[:, None] == jnp.arange(LAT_BANDS, dtype=jnp.int32)[None, :]).astype(
         jnp.bfloat16
     )
     gathered = lax.all_gather(params.astype(jnp.bfloat16), ("dp", "space"), axis=0, tiled=True)
     pieces = unpack_params(gathered)
-    shifted = lax.all_to_all(
-        flat_in[routes], "space", split_axis=0, concat_axis=0, tiled=True
-    ).reshape(rows_dev, model_width)
+    shifted = to_windows(flat_in)
     window_out, window_saved = window_forward(pieces, shifted, selector)
-    returned = lax.all_to_all(
-        window_out.astype(jnp.bfloat16).reshape(routes.shape[0], routes.shape[1], model_width),
-        "space",
-        split_axis=0,
-        concat_axis=0,
-        tiled=True,
-    )
-    branch = (
-        jnp.zeros((rows_dev, model_width), jnp.bfloat16)
-        .at[route_flat]
-        .set(returned.reshape(-1, model_width))
-    )
+    branch = from_windows(window_out.astype(jnp.bfloat16))
     after_window = as_float(flat_in) + as_float(branch)
     output, column_saved = column_forward(pieces, after_window, level_rows)
-    again = unpack_params(
-        lax.all_gather(params.astype(jnp.bfloat16), ("dp", "space"), axis=0, tiled=True)
-    )
-    output_again, column_saved = column_forward(again, after_window, level_rows)
     grad_after, column_grads = column_backward(
-        again, column_saved, as_float(cotangent[0].reshape(rows_dev, model_width))
-    )
-    grad_branch = grad_after.astype(jnp.bfloat16)
-    grad_window = lax.all_to_all(
-        grad_branch[routes], "space", split_axis=0, concat_axis=0, tiled=True
-    ).reshape(rows_dev, model_width)
-    window_again, window_saved = window_forward(again, shifted, selector)
-    grad_shifted, window_grads = window_backward(again, window_saved, grad_window, selector)
-    sent_back = lax.all_to_all(
-        grad_shifted.astype(jnp.bfloat16).reshape(routes.shape[0], routes.shape[1], model_width),
-        "space",
-        split_axis=0,
-        concat_axis=0,
-        tiled=True,
-    )
-    input_grad = grad_after + jnp.zeros((rows_dev, model_width), jnp.float32).at[route_flat].set(
-        as_float(sent_back.reshape(-1, model_width))
-    )
+        pieces, column_saved, as_float(cotangent[0].reshape(rows_dev, model_width))
+    )
+    grad_window = to_windows(grad_after.astype(jnp.bfloat16))
+    grad_shifted, window_grads = window_backward(pieces, window_saved, grad_window, selector)
+    input_grad = grad_after + as_float(from_windows(grad_shifted.astype(jnp.bfloat16)))
     gradient = dict(column_grads)
     gradient.update(window_grads)
     flat_grad = jnp.concatenate(

time: 789 us -> 726 us (0.920)
  waiting for transfers between devices: 198 us -> 150 us
  starting transfers between devices: 19.1 us -> 0.08 us
  blocking collectives: 0 us -> 13.5 us
    all_to_all x4 -> x0, waiting for transfers between devices: 61.3 us -> none  [the longest x1 34.8 us: body(): lax.all_to_all(flat_in[routes], 'space', split_axis=0, concat_axis=0, til...]
    all_to_all x4 -> x0, starting transfers between devices: 19 us -> none  [the longest x1 6.46 us: body(): lax.all_to_all(flat_in[routes], 'space', split_axis=0, concat_axis=0, til...]
    all_gather x1, waiting for transfers between devices: 23.6 us -> 40.7 us  [body(): lax.all_gather(params.astype(jnp.bfloat16), ('dp', 'space'), axis=0, tile...]
    all_gather x0 -> x1, blocking collectives: none -> 13.5 us  [body(): all_bands = lax.all_gather(window_band[0], 'space', axis=0)]
    reshape x5 -> x0, local copies, waits for them, and re-layouts: 8.99 us -> none  [the longest x2 4.54 us: body(): window_out.astype(jnp.bfloat16)]
    unnamed x197 -> x165, local copies, waits for them, and re-layouts: 16.1 us -> 15.8 us
  transfers between devices with their start and end apart: 6 -> 2, of which waited for: 5 -> 2; matrix products, arithmetic and copies ran while one was open for 18% -> 7% of each run, Pallas kernels for 0% -> 0%
where the time goes in v1:
time: 726 us; the launch traced here: 712 us
  local copies, waits for them, and re-layouts  349 us (48%)
  waiting for transfers between devices  150 us (21%)
  matrix products  127 us (17%)
  other arithmetic  57.7 us (8%)
  between operations  15.2 us (2%)
  blocking collectives  13.5 us (2%)
    unnamed x3, waiting for transfers between devices  109 us
    concatenate x1, local copies, waits for them, and re-layouts, body(): jnp.concatenate([gradient[entry_name].reshape(-1) for entry_name, entry_s...  55.8 us
    all_gather x1, waiting for transfers between devices, body(): lax.all_gather(params.astype(jnp.bfloat16), ('dp', 'space'), axis=0, tile...  40.7 us
    scatter x4, local copies, waits for them, and re-layouts, from_windows(): jnp.zeros((rows_dev, model_width), rows.dtype).at[route_flat].set(rows)  31 us
    convert_element_type x2, local copies, waits for them, and re-layouts, column_backward(): grad_packed = jnp.stack([grad_query, grad_key, grad_value], axis=2).astyp...  30.4 us
    dot_general x7, matrix products, plain_product(): return jnp.dot(left, right, preferred_element_type=jnp.float32)  19.8 us
    dot_general x7, matrix products, left_product(): lax.dot_general(left, right, (((0,), (0,)), ((), ())), preferred_element_...  17.3 us
    all_gather x1, other arithmetic, body(): lax.all_gather(params.astype(jnp.bfloat16), ('dp', 'space'), axis=0, tile...  16.6 us
  transfers between devices with their start and end apart: 2, of which 2 were waited for; matrix products, arithmetic and copies ran while one was open for 7% of the time, Pallas kernels for 0%

profile of v1, /device:TPU:0, one launch (start us, length us, event | category | flops | bytes accessed | tf_op | source)
XLA Modules:
  0.0 712.5 jit_solution(8090718846678111993)
XLA Ops:
  9.8 13.5 %all-gather.1 = s32[8,1,32]{2,1,0:T(1,128)S(1)} all-gather(s32[1,1,32]{2,1,0:T(1,128)} %bitcast.153), channel_id=1, replica_groups=mesh['dp'=4,'space'=8] {'space'}, dimensions={0}, use_global_device_ids=true | all-gather | bytes 1152 | tf_op jit(solution)/shard_map/all_gather | solution.py:317
  27.5 7.5 %gather_fusion = bf16[2304,192]{1,0:T(8,128)(2,1)} fusion(bf16[2304,192]{1,0:T(8,128)(2,1)S(1)} %bitcast.146, s32[3072]{0:T(1024)S(1)} %pad_clamp_fusion), kind=kCustom, calls=%fused_computation | custom fusion | bytes 1778688 | tf_op jit(solution)/shard_map/gather | solution.py:305
  37.9 40.7 %all-gather.4.cloned.1.call-done = bf16[32,1,38016]{2,1,0:T(2,128)(2,1)} async-done(((bf16[1,1,38016]{2,1,0:T(2,128)(2,1)}), bf16[32,1,38016]{2,1,0:T(2,128)(2,1)}) %all-gather.4.cloned.1.call-update) | async-done | bytes 2433040 | tf_op jit(solution)/shard_map/all_gather | solution.py:324
  78.6 16.6 %reduce.3 = bf16[32,38016]{1,0:T(8,128)(2,1)} reduce(bf16[32,1,38016]{2,1,0:T(2,128)(2,1)} %all-gather.4.cloned.1.call-done, bf16[]{:T(256)} %constant.90), dimensions={1}, to_apply=%all-gather.reduce_sub_computation | reduce | bytes 4866050 | tf_op jit(solution)/shard_map/all_gather | solution.py:324
  129.4 12.8 %reshape.257 = bf16[32,72,3,6,32]{1,0,4,3,2:T(8,128)(2,1)} reshape(bf16[2304,576]{0,1:T(8,128)(2,1)} %convolution_convert_fusion.1) | data formatting | bytes 5308416 | tf_op jit(solution)/shard_map/reshape | solution.py:93
  151.4 8.8 %copy.129 = f32[32,6,72,72]{2,3,1,0:T(8,128)} copy(f32[32,6,72,72]{3,0,2,1:T(8,128)} %fusion.32) | data formatting | bytes 7962624 | tf_op jit(solution)/shard_map/dot_general | solution.py:62
  160.2 7.1 multiply_add_fusion
  172.3 9.4 %fusion.53 = bf16[32,72,6,32]{1,3,2,0:T(8,128)(2,1)} fusion(bf16[32,72,1,6,32]{1,0,4,3,2:T(8,128)(2,1)} %get-tuple-element.30, f32[32,6,72]{2,1,0:T(8,128)S(1)} %get-tuple-element.46, f32[32,6,72,72]{2,3,1,0:T(8,128)} %copy-done.4), kind=kOutput, calls=%fused_computation.100 | convolution fusion | flops 67143240 | bytes 5806080 | tf_op jit(solution)/shard_map/uhqk,ukhe->uqhe/dot_general | solution.py:108
  190.4 13.5 %scatter_custom_fusion = bf16[2304,192]{1,0:T(8,128)(2,1)S(1)} fusion(s32[2304]{0:T(1024)S(1)} %fusion.82, bf16[2304,192]{1,0:T(8,128)(2,1)} %copy.132, bf16[]{:T(256)} %constant.31.clone.1), kind=kCustom, calls=%fused_computation.115 | custom fusion | bytes 885248 | tf_op jit(solution)/shard_map/scatter | solution.py:315
  212.6 13.6 %reshape.260 = bf16[288,8,3,6,32]{4,3,2,1,0:T(8,128)(2,1)} reshape(bf16[2304,576]{1,0:T(8,128)(2,1)S(1)} %copy.134) | data formatting | bytes 5308416 | tf_op jit(solution)/shard_map/reshape | solution.py:172
  226.2 14.1 %slice_bitcast_fusion.1 = (bf16[288,8,6,32]{3,2,1,0:T(8,128)(2,1)}, bf16[288,8,6,32]{3,2,1,0:T(8,128)(2,1)}, bf16[288,8,6,32]{3,2,1,0:T(8,128)(2,1)}, bf16[288,8...) fusion(bf16[288,8,3,6,32]{4,3,2,1,0:T(8,128)(2,1)} %reshape.260), kind=kLoop, calls=%fused_computation.167 | loop fusion | bytes 7962624 | tf_op jit(solution)/shard_map/squeeze | solution.py:176
  267.0 6.4 convert_element_type.190
  281.4 6.5 convert_reduce_fusion
  311.9 7.2 %fusion.16 = f32[6,288,8,8]{3,2,1,0:T(8,128)} fusion(bf16[288,8,6,32]{3,2,1,0:T(8,128)(2,1)} %get-tuple-element.23, bf16[288,8,6,32]{3,2,1,0:T(8,128)(2,1)S(1)} %copy-done.1), kind=kOutput, calls=%fused_computation.39 | convolution fusion | flops 7077888 | bytes 2211840 | tf_op jit(solution)/shard_map/cqhe,ckhe->hqkc/dot_general | solution.py:250
  360.8 14.3 %copy.156 = bf16[288,8,3,6,32]{4,3,2,1,0:T(8,128)(2,1)} copy(bf16[288,8,3,6,32]{0,4,3,2,1:T(8,128)(2,1)S(1)} %maximum_convert_fusion.1) | data formatting | bytes 5308416 | tf_op jit(solution)/shard_map/convert_element_type | solution.py:273
  375.2 16.1 %convert_element_type.205 = bf16[2304,576]{1,0:T(8,128)(2,1)} reshape(bf16[288,8,3,6,32]{4,3,2,1,0:T(8,128)(2,1)} %copy.156) | data formatting | bytes 5308416 | tf_op jit(solution)/shard_map/convert_element_type | solution.py:273
  400.0 6.9 gather_fusion.1
  413.0 8.7 %convolution_bitcast_fusion = bf16[32,72,1,6,32]{1,4,3,0,2:T(8,128)(2,1)} fusion(bf16[32,72,6,32]{1,0,3,2:T(8,128)(2,1)S(1)} %reshape.265, f32[32,6,72]{2,1,0:T(8,128)S(1)} %copy-done.42, f32[32,6,72,72]{2,3,1,0:T(8,128)} %copy-done.4), kind=kOutput, calls=%fused_computation.71 | convolution fusion | flops 66700872 | bytes 5806080 | tf_op jit(solution)/shard_map/uhqk,uqhe->ukhe/dot_general | solution.py:130
  421.8 9.0 %multiply_reduce_fusion = (f32[32,6,72]{2,1,0:T(8,128)S(1)}, f32[32,6,72,72]{2,3,1,0:T(8,128)}) fusion(f32[32,6,72,72]{2,3,1,0:T(8,128)} %get-tuple-element.47, f32[32,6,72]{2,1,0:T(8,128)S(1)} %copy-done.42, bf16[32,72,1,6,32]{1,0,4,3,2:T(8,128)(2,1)S(1)} %copy-done.33, bf16[32,72,6,32]{1,0,3,2:T(8,128)(2,1)S(1)} %reshape.265), kind=kOutput, calls=%fused_computation.20 | convolution fusion | flops 66673152 | bytes 9842688 | tf_op jit(solution)/shard_map/uqhe,ukhe->uhqk/dot_general | solution.py:127
  455.8 9.4 %convert_element_type.210 = bf16[2304,576]{0,1:T(8,128)(2,1)} reshape(bf16[32,72,3,6,32]{1,0,4,3,2:T(8,128)(2,1)} %copy.163) | data formatting | bytes 5308416 | tf_op jit(solution)/shard_map/convert_element_type | solution.py:153
  480.8 6.5 reshape.273
  499.9 55.8 %concatenate.3 = f32[1214400]{0:T(1024)} concatenate(f32[192]{0:T(256)} %get-tuple-element.10, f32[192]{0:T(256)} %get-tuple-element.14, f32[110592]{0:T(1024)} %reshape.267, f32[36864]{0:T(1024)S(1)} %reshape.268, f32[192]{0:T(256)} %convert_reduce_fusion.2, f32[192]{0:T(256)} %get-tuple-element.8, f32[192]{0:T(256)} %get-tuple-element.13, f32[110592]{0:T(1024)} %reshape.269, ...), dimensions={0} | concatenate | bytes 9715200 | tf_op jit(solution)/shard_map/concatenate | solution.py:339
  571.7 14.4 %scatter_custom_fusion.1 = bf16[2304,192]{1,0:T(8,128)(2,1)} fusion(s32[2304]{0:T(1024)} %copy-done.65, bf16[2304,192]{1,0:T(8,128)(2,1)} %copy.164, bf16[]{:T(256)} %constant.31.clone.1), kind=kCustom, calls=%fused_computation.113 | custom fusion | bytes 885248 | tf_op jit(solution)/shard_map/scatter | solution.py:315
  594.4 109.4 %all-reduce.4.cloned.1.call-done = f32[1216512]{0:T(1024)} async-done(((f32[1216512]{0:T(1024)}), f32[1216512]{0:T(1024)}) %all-reduce.4.cloned.1.call-update) | async-done | bytes 4866064
  (287 shorter events, 269.3 us)
Async XLA Ops:
  7.2 18.9 %copy-start.27 = (bf16[1,288,8,192]{3,2,1,0:T(8,128)(2,1)S(1)}, bf16[1,288,8,192]{3,2,1,0:T(8,128)(2,1)}, u32[]{:S(2)}) copy-start(bf16[1,288,8,192]{3,2,1,0:T(8,128)(2,1)} %param.7) | copy-start | bytes 2654212
  7.2 71.4 %all-gather.4.cloned.1.call-start = ((), (), s32[]{:S(2)}) async-start(), calls=%async_computation | async-start | bytes 5018112 | tf_op jit(solution)/shard_map/all_gather | solution.py:324
  9.0 694.8 %all-reduce.4.cloned.1.call-start = ((), (), s32[]{:S(2)}) async-start(), calls=%async_computation.1 | async-start | bytes 9732096
  23.5 123.8 %copy-start.71 = (s32[32]{0:T(128)}, s32[32]{0:T(128)S(1)}, u32[]{:S(2)}) copy-start(s32[32]{0:T(128)S(1)} %eq.17) | copy-start | bytes 388
  26.0 179.4 %copy-start.10 = (bf16[2304,192]{0,1:T(8,128)(2,1)}, bf16[2304,192]{0,1:T(8,128)(2,1)S(1)}, u32[]{:S(2)}) copy-start(bf16[2304,192]{0,1:T(8,128)(2,1)S(1)} %copy.123) | copy-start | bytes 2654212
  27.4 163.0 %copy-start.65 = (s32[2304]{0:T(1024)}, s32[2304]{0:T(1024)S(1)}, u32[]{:S(2)}) copy-start(s32[2304]{0:T(1024)S(1)} %fusion.82) | copy-start | bytes 27652
  36.5 90.3 %copy-start.8 = (bf16[2304,192]{0,1:T(8,128)(2,1)}, bf16[2304,192]{0,1:T(8,128)(2,1)S(1)}, u32[]{:S(2)}) copy-start(bf16[2304,192]{0,1:T(8,128)(2,1)S(1)} %copy.124) | copy-start | bytes 2654212
  37.6 89.2 %copy-start.49 = (f32[2304]{0:T(1024)}, f32[2304]{0:T(1024)S(1)}, u32[]{:S(2)}) copy-start(f32[2304]{0:T(1024)S(1)} %broadcast_multiply_fusion.2) | copy-start | bytes 27652
  37.8 57.3 %copy-start.55 = (f32[2304]{0:T(1024)}, f32[2304]{0:T(1024)S(1)}, u32[]{:S(2)}) copy-start(f32[2304]{0:T(1024)S(1)} %fusion.43) | copy-start | bytes 27652
  37.9 88.9 %copy-start.59 = (f32[2304]{0:T(1024)}, f32[2304]{0:T(1024)S(1)}, u32[]{:S(2)}) copy-start(f32[2304]{0:T(1024)S(1)} %fusion.79) | copy-start | bytes 27652
  103.9 22.9 %copy-start.69 = (f32[192]{0:T(256)}, f32[192]{0:T(256)S(1)}, u32[]{:S(2)}) copy-start(f32[192]{0:T(256)S(1)} %get-tuple-element.39) | copy-start | bytes 2308
  103.9 22.9 %copy-start.74 = (f32[192]{0:T(256)}, f32[192]{0:T(256)S(1)}, u32[]{:S(2)}) copy-start(f32[192]{0:T(256)S(1)} %get-tuple-element.38) | copy-start | bytes 2308
  103.9 101.6 %copy-start.76 = (f32[192]{0:T(256)}, f32[192]{0:T(256)S(1)}, u32[]{:S(2)}) copy-start(f32[192]{0:T(256)S(1)} %get-tuple-element.35) | copy-start | bytes 2308
  111.6 77.0 %copy-start.36 = (bf16[192,192]{1,0:T(8,128)(2,1)}, bf16[192,192]{1,0:T(8,128)(2,1)S(1)}, u32[]{:S(2)}) copy-start(bf16[192,192]{1,0:T(8,128)(2,1)S(1)} %reshape.258) | copy-start | bytes 221188
  292.5 105.2 %copy-start.51 = (f32[2304]{0:T(1024)}, f32[2304]{0:T(1024)S(1)}, u32[]{:S(2)}) copy-start(f32[2304]{0:T(1024)S(1)} %negate_multiply_fusion.2) | copy-start | bytes 27652
  375.1 16.1 %copy-start.11 = (bf16[2304,192]{0,1:T(8,128)(2,1)S(1)}, bf16[2304,192]{0,1:T(8,128)(2,1)}, u32[]{:S(2)}) copy-start(bf16[2304,192]{0,1:T(8,128)(2,1)} %copy-done.10) | copy-start | bytes 2654212
  375.1 16.1 %copy-start.13 = (bf16[2304,192]{0,1:T(8,128)(2,1)S(1)}, bf16[2304,192]{0,1:T(8,128)(2,1)}, u32[]{:S(2)}) copy-start(bf16[2304,192]{0,1:T(8,128)(2,1)} %copy-done.12) | copy-start | bytes 2654212
  375.1 16.1 %copy-start.63 = (f32[2304]{0:T(1024)S(1)}, f32[2304]{0:T(1024)}, u32[]{:S(2)}) copy-start(f32[2304]{0:T(1024)} %copy-done.62) | copy-start | bytes 27652
  375.1 16.1 %copy-start.67 = (f32[2304]{0:T(1024)S(1)}, f32[2304]{0:T(1024)}, u32[]{:S(2)}) copy-start(f32[2304]{0:T(1024)} %copy-done.66) | copy-start | bytes 27652
  375.1 16.1 %copy-start.77 = (f32[192]{0:T(256)S(1)}, f32[192]{0:T(256)}, u32[]{:S(2)}) copy-start(f32[192]{0:T(256)} %copy-done.76) | copy-start | bytes 2308
  470.7 26.0 %copy-start.25 = (f32[2304,192]{0,1:T(8,128)}, f32[2304,192]{0,1:T(8,128)S(1)}, u32[]{:S(2)}) copy-start(f32[2304,192]{0,1:T(8,128)S(1)} %get-tuple-element.58) | copy-start | bytes 5308420
  569.1 19.3 %copy-start.15 = (f32[2304,192]{0,1:T(8,128)S(1)}, f32[2304,192]{0,1:T(8,128)}, u32[]{:S(2)}) copy-start(f32[2304,192]{0,1:T(8,128)} %copy-done.14) | copy-start | bytes 5308420
  571.6 16.7 %copy-start.7 = (f32[2304,192]{0,1:T(8,128)S(1)}, f32[2304,192]{0,1:T(8,128)}, u32[]{:S(2)}) copy-start(f32[2304,192]{0,1:T(8,128)} %copy-done.5) | copy-start | bytes 5308420
  571.7 16.7 %copy-start.52 = (f32[2304]{0:T(1024)S(1)}, f32[2304]{0:T(1024)}, u32[]{:S(2)}) copy-start(f32[2304]{0:T(1024)} %copy-done.51) | copy-start | bytes 27652
  (59 other events, 260.2 us)
Sparse Core Ops, SparseCore 0:
  11.5 66.9 all-gather.3
  560.0 143.7 all-reduce.3

commit v2 on v1

v2 whole, which is shorter than its diff:
```python
import functools
import math

import jax
import jax.numpy as jnp
from jax import lax
from jax.experimental import pallas as pl
from jax.experimental.pallas import tpu as pltpu
from jax.sharding import PartitionSpec as P

D = 192
HEADS = 6
HEAD_DIM = 32
FF = 768
LEVELS = 8
WIN = 72
LAT_BANDS = 20
LANES = 128
HALF = LANES // 2
KEYS = 80
SCALE = HEAD_DIM ** (-0.5)
LOG2E = math.log2(math.e)
F32 = jnp.float32
BF16 = jnp.bfloat16
VMEM_LIMIT = 58 << 20

norm_eps = 1e-05


def param_layout():
    return [
        ("norm1_gain", (D,)),
        ("norm1_shift", (D,)),
        ("qkv1", (D, 3 * D)),
        ("proj1", (D, D)),
        ("proj1_bias", (D,)),
        ("norm2_gain", (D,)),
        ("norm2_shift", (D,)),
        ("qkv2", (D, 3 * D)),
        ("proj2", (D, D)),
        ("proj2_bias", (D,)),
        ("norm3_gain", (D,)),
        ("norm3_shift", (D,)),
        ("mlp_in", (D, FF)),
        ("mlp_in_bias", (FF,)),
        ("mlp_out", (FF, D)),
        ("mlp_out_bias", (D,)),
        ("earth_bias", (LAT_BANDS, HEADS, WIN, WIN)),
    ]


def param_offsets():
    offsets = {}
    filled = 0
    for entry_name, entry_shape in param_layout():
        offsets[entry_name] = filled
        filled += math.prod(entry_shape)
    return offsets


OFFSET = param_offsets()
BIAS_ROW, BIAS_LANE = divmod(OFFSET["earth_bias"], LANES)
BIAS_ROWS = LAT_BANDS * HEADS * WIN
WIDE = LANES // math.gcd(WIN, LANES)
DENSE = WIN // math.gcd(WIN, LANES)
PERIODS = -(-(BIAS_ROWS // WIDE + 1) // 8) * 8
COL_LO = (OFFSET["norm2_gain"] // LANES) // 8 * 8
COL_HI = -(-BIAS_ROW // 8) * 8 + 8
BIAS_LO = BIAS_ROW // 8 * 8


def mm(left, right):
    return lax.dot_general(left, right, (((1,), (0,)), ((), ())), preferred_element_type=F32)


def mt(left, right):
    return lax.dot_general(left, right, (((1,), (1,)), ((), ())), preferred_element_type=F32)


def lane_ids(rows):
    return lax.broadcasted_iota(jnp.int32, (rows, LANES), 1)


def rows_at(start, count, stride):
    return pl.ds(start, count) if stride == 1 else pl.ds(start, count, stride=stride)


def read_matrix(dense, first_row, name, matrix):
    rows, width = dict(param_layout())[name]
    halves = width // HALF
    step = 1 + halves % 2
    count, stride = rows // step, halves * step // 2
    low = lane_ids(count) < HALF
    for part in range(step):
        for chunk in range(-(-halves // 2)):
            unit = OFFSET[name] // HALF + part * halves + 2 * chunk
            row = unit // 2 - first_row
            value = dense[rows_at(row, count, stride), :]
            if unit % 2:
                after = dense[rows_at(row + 1, count, stride), :]
                value = pltpu.roll(jnp.where(low, after, value), HALF, 1)
            matrix[chunk, rows_at(part, count, step), :] = value


def write_matrix(dense, first_row, name, matrix):
    rows, width = dict(param_layout())[name]
    halves = width // HALF
    step = 1 + halves % 2
    count, stride = rows // step, halves * step // 2
    lane = lane_ids(count)
    for part in range(step):
        piece = 0
        while piece < halves:
            unit = OFFSET[name] // HALF + part * halves + piece
            where_to = rows_at(unit // 2 - first_row, count, stride)
            chunk = piece // 2
            value = matrix[chunk, rows_at(part, count, step), :]
            if unit % 2 == piece % 2 == 0 and piece + 1 < halves:
                dense[where_to, :] = value
                piece += 2
                continue
            if unit % 2 != piece % 2:
                value = pltpu.roll(value, HALF, 1)
            mine = lane < HALF if unit % 2 == 0 else lane >= HALF
            dense[where_to, :] = jnp.where(mine, value, dense[where_to, :])
            piece += 1


def joined(matrix, width):
    chunks = [matrix[k] for k in range(-(-width // LANES))]
    return jnp.concatenate(chunks, axis=1)[:, :width]


def split_into(matrix, value):
    width = value.shape[1]
    for k in range(-(-width // LANES)):
        end = min(width, (k + 1) * LANES)
        matrix[k, :, : end - k * LANES] = value[:, k * LANES : end]


def read_vector(dense, first_row, name):
    size = dict(param_layout())[name][0]
    unit = OFFSET[name] // HALF
    row = unit // 2 - first_row
    turned = dense[row : row + 8, :].T
    pieces = []
    for k in range(size // HALF):
        spot = unit % 2 + k
        pieces.append(turned[spot % 2 * HALF : (spot % 2 + 1) * HALF, spot // 2 : spot // 2 + 1])
    return jnp.concatenate(pieces, axis=0)


def write_vector(dense, first_row, name, sums):
    size = dict(param_layout())[name][0]
    line = jnp.sum(sums.T, axis=0, keepdims=True)
    lane = lane_ids(1)
    for k in range(size // HALF):
        unit = OFFSET[name] // HALF + k
        row = unit // 2 - first_row
        if size % LANES and k == size // HALF - 1:
            tail = line[:, k * HALF :]
            piece = jnp.concatenate([tail, tail], axis=1)
        else:
            piece = line[:, k // 2 * LANES : (k // 2 + 1) * LANES]
            if unit % 2 != k % 2:
                piece = pltpu.roll(piece, HALF, 1)
        mine = lane < HALF if unit % 2 == 0 else lane >= HALF
        dense[row : row + 1, :] = jnp.where(mine, piece, dense[row : row + 1, :])


def read_bias(dense, wide):
    lane = lane_ids(PERIODS)
    for j in range(WIDE):
        row, first = divmod(BIAS_LANE + j * WIN, LANES)
        value = dense[pl.ds(BIAS_ROW + row, PERIODS, stride=DENSE), :]
        if first + WIN > LANES:
            after = dense[pl.ds(BIAS_ROW + row + 1, PERIODS, stride=DENSE), :]
            value = jnp.where(lane < first, after, value)
        if first:
            value = pltpu.roll(value, LANES - first, 1)
        wide[pl.ds(j, PERIODS, stride=WIDE), :] = value


def write_bias(wide, dense, first_row):
    lane = lane_ids(PERIODS)
    for i in range(DENSE):
        begin = i * LANES - BIAS_LANE
        line = begin // WIN
        value = None
        while line * WIN < begin + LANES:
            shift = line * WIN - begin
            piece = wide[pl.ds(WIDE + line, PERIODS, stride=WIDE), :]
            if shift % LANES:
                piece = pltpu.roll(piece, shift % LANES, 1)
            value = piece if value is None else jnp.where(lane >= shift, piece, value)
            line += 1
        dense[pl.ds(BIAS_ROW - first_row + i, PERIODS, stride=DENSE), :] = value


def norm_parts(rows_in):
    mean = jnp.mean(rows_in, axis=0, keepdims=True)
    centered = rows_in - mean
    var = jnp.mean(centered * centered, axis=0, keepdims=True)
    scale = lax.rsqrt(var + norm_eps)
    return centered * scale, scale


def norm_back(grad, unit, scale, gain):
    scaled = grad * gain
    first = jnp.mean(scaled, axis=0, keepdims=True)
    second = jnp.mean(scaled * unit, axis=0, keepdims=True)
    return scale * (scaled - first - unit * second)


def lane_fold(value):
    total = value[:, :LANES]
    for k in range(1, value.shape[1] // LANES):
        total = total + value[:, k * LANES : (k + 1) * LANES]
    return total


def head_rows(h):
    return slice(h * HEAD_DIM, (h + 1) * HEAD_DIM)


def head_lanes(h):
    return slice(h * LANES, (h + 1) * LANES)


def diagonal(full):
    return jnp.concatenate([full[head_rows(h), head_lanes(h)] for h in range(HEADS)], axis=0)


def scatter_heads(block, rows_in):
    for h in range(HEADS):
        block[head_rows(h), head_lanes(h)] = rows_in[head_rows(h), :]


def chooser(first, rows, slots):
    ids = lax.broadcasted_iota(jnp.int32, (rows, slots.shape[1]), 0) + first
    return jnp.where(ids == slots, 1.0, 0.0).astype(BF16)


def to_slots(rows_t, slots):
    tokens = rows_t.shape[1]
    pick = jnp.concatenate([chooser(k, 256, slots) for k in range(0, tokens, 256)], axis=0)
    return mm(rows_t, pick).astype(BF16)


def from_slots(slot_rows, slots, first, rows):
    return mt(slot_rows, chooser(first, rows, slots))


def call(kernel, grid, ins, outs, scratch, name, scalars=0):
    in_specs = [s for _, s in ins]
    spec = pltpu.PrefetchScalarGridSpec(
        num_scalar_prefetch=scalars,
        grid=grid,
        in_specs=in_specs[scalars:],
        out_specs=[s for _, _, s in outs],
        scratch_shapes=scratch,
    )
    return pl.pallas_call(
        kernel,
        grid_spec=spec,
        out_shape=[jax.ShapeDtypeStruct(shape, kind) for shape, kind, _ in outs],
        compiler_params=pltpu.CompilerParams(
            dimension_semantics=("arbitrary",) * len(grid), vmem_limit_bytes=VMEM_LIMIT
        ),
        name=name,
    )(*[a for a, _ in ins])


def whole_block(shape):
    return pl.BlockSpec(shape, lambda *_: (0,) * len(shape))


SLOT_BLOCK = 512
TOKEN_BLOCK = 256


def shift_kernel(x_ref, slots_ref, out_ref, x_t):
    @pl.when(pl.program_id(0) == 0)
    def _():
        x_t[...] = x_ref[...].astype(F32).T.astype(BF16)

    out_ref[...] = to_slots(x_t[...], slots_ref[...])


def shift_call(tokens, slots):
    count, n = tokens.shape[0], slots.shape[1]
    return call(
        shift_kernel,
        (n // SLOT_BLOCK,),
        [
            (tokens, whole_block(tokens.shape)),
            (slots, pl.BlockSpec((1, SLOT_BLOCK), lambda i: (0, i))),
        ],
        [((D, n), BF16, pl.BlockSpec((D, SLOT_BLOCK), lambda i: (0, i)))],
        [pltpu.VMEM((D, count), BF16)],
        "shift",
    )[0]


def load_dense(me_ref, parts, blocks, dense, sem, order):
    copies = []
    first = 0
    for part in parts:
        copies.append(pltpu.make_async_copy(part, blocks.at[pl.ds(first, part.shape[0])], sem))
        first += part.shape[0]
    for copy in copies:
        copy.start()
    for copy in copies:
        copy.wait()
    shards, rows = blocks.shape[0], blocks.shape[1]
    for shard in range(shards):
        spot = position(me_ref[0] ^ shard, order)
        dense[shard * rows : (shard + 1) * rows, :] = blocks[spot].astype(F32)
    if dense.shape[0] > shards * rows:
        dense[shards * rows :, :] = jnp.zeros((dense.shape[0] - shards * rows, LANES), F32)


def position(relative, order):
    spot = 0
    for place, bit in enumerate(reversed(order)):
        spot = spot + ((relative >> bit) & 1) * (1 << place)
    return spot


def window_forward_kernel(me_ref, band_ref, *refs, parts, order, steps, fused):
    ins = refs[:parts]
    refs = refs[parts:]
    if fused:
        shifted_ref, slots_ref, x_ref = refs[:3]
        refs = refs[3:]
    else:
        shifted_ref, refs = refs[0], refs[1:]
    (
        out_ref,
        qkv_ref,
        mixed_ref,
        prob_ref,
        weights_ref,
        column_ref,
        vec,
        blocks,
        dense,
        wide,
        bias,
        mat,
        qkv_t,
        proj_t,
        spread,
        y_all,
        sem,
    ) = refs
    step = pl.program_id(0)

    @pl.when(step == 0)
    def _():
        load_dense(me_ref, ins, blocks, dense, sem, order)
        column_ref[...] = dense[COL_LO:COL_HI, :]
        read_matrix(dense, 0, "qkv1", mat)
        weights_ref[:, : 3 * D] = joined(mat, 3 * D).astype(BF16)
        qkv_t[...] = joined(mat, 3 * D).T.astype(BF16)
        read_matrix(dense, 0, "proj1", mat)
        weights_ref[:, 3 * D :] = joined(mat, D).astype(BF16)
        proj_t[...] = joined(mat, D).T.astype(BF16)
        vec[:, 0:1] = read_vector(dense, 0, "norm1_gain")
        vec[:, 1:2] = read_vector(dense, 0, "norm1_shift")
        vec[:, 2:3] = read_vector(dense, 0, "proj1_bias")
        read_bias(dense, wide)
        wide[BIAS_ROWS:, :] = jnp.zeros((wide.shape[0] - BIAS_ROWS, LANES), F32)

        def turn(k, _):
            block = wide[pl.ds(pl.multiple_of(k * WIN, 8), LANES), :].T
            bias[k, :WIN, :] = block[:WIN].astype(BF16)
            return 0

        lax.fori_loop(0, LAT_BANDS * HEADS, turn, 0)
        bias[:, WIN:, :] = jnp.full((LAT_BANDS * HEADS, KEYS - WIN, LANES), -jnp.inf, BF16)
        spread[...] = jnp.zeros_like(spread)

    @pl.when(step < steps)
    def _():
        per_step = SLOT_BLOCK // LANES
        unit, _ = norm_parts(shifted_ref[...].astype(F32))
        normed = (unit * vec[:, 0:1] + vec[:, 1:2]).astype(BF16)
        qkv = mm(qkv_t[...], normed).astype(BF16)
        qkv_ref[...] = qkv
        mixed = []
        for w in range(per_step):
            lanes = slice(w * LANES, (w + 1) * LANES)
            band = band_ref[step * per_step + w]
            scatter_heads(spread.at[w], qkv[:D, lanes])
            scores = mm(qkv[D : 2 * D, lanes].T[:KEYS], spread[w])
            probs = []
            for h in range(HEADS):
                score = scores[:, head_lanes(h)] * SCALE + bias[band * HEADS + h].astype(F32)
                grown = jnp.exp(score - jnp.max(score, axis=0, keepdims=True))
                probs.append(
                    (grown * (1.0 / jnp.sum(grown, axis=0, keepdims=True))).astype(BF16)
                )
            prob = jnp.concatenate(probs, axis=1)
            prob_ref[w] = prob
            tall = jnp.concatenate([prob, jnp.zeros((LANES - KEYS, HEADS * LANES), BF16)], axis=0)
            mixed.append(diagonal(mm(qkv[2 * D :, lanes], tall)))
        mixed = jnp.concatenate(mixed, axis=1).astype(BF16)
        mixed_ref[...] = mixed
        result = (mm(proj_t[...], mixed) + vec[:, 2:3]).astype(BF16)
        if fused:
            y_all[:, pl.ds(pl.multiple_of(step * SLOT_BLOCK, SLOT_BLOCK), SLOT_BLOCK)] = result
        else:
            out_ref[...] = result

    if fused:

        @pl.when(step >= steps)
        def _():
            branch = from_slots(
                y_all[...], slots_ref[...], (step - steps) * TOKEN_BLOCK, TOKEN_BLOCK
            )
            out_ref[...] = x_ref[...].astype(F32).T + branch


def window_forward_call(me, bands, parts, order, shifted, tokens, slots, fused):
    n = shifted.shape[1]
    steps = n // SLOT_BLOCK
    per_step = SLOT_BLOCK // LANES
    shards, rows = sum(p.shape[0] for p in parts), parts[0].shape[1]
    flat_rows = max(shards * rows, BIAS_ROW + DENSE * PERIODS + 8)
    slot_block = lambda r: pl.BlockSpec((r, SLOT_BLOCK), lambda i, *_: (0, jnp.minimum(i, steps - 1)))
    ins = [(me, None), (bands, None)]
    ins += [(p, pl.BlockSpec(memory_space=pl.ANY)) for p in parts]
    ins += [(shifted, slot_block(D))]
    if fused:
        count = tokens.shape[0]
        late = lambda i: jnp.maximum(i - steps, 0)
        ins += [
            (slots, whole_block(slots.shape)),
            (tokens, pl.BlockSpec((TOKEN_BLOCK, D), lambda i, *_: (late(i), 0))),
        ]
        first = ((D, count), F32, pl.BlockSpec((D, TOKEN_BLOCK), lambda i, *_: (0, late(i))))
        grid = steps + count // TOKEN_BLOCK
    else:
        first = ((D, n), BF16, slot_block(D))
        grid = steps
    outs = [
        first,
        ((3 * D, n), BF16, slot_block(3 * D)),
        ((D, n), BF16, slot_block(D)),
        (
            (n // LANES, KEYS, HEADS * LANES),
            BF16,
            pl.BlockSpec(
                (per_step, KEYS, HEADS * LANES), lambda i, *_: (jnp.minimum(i, steps - 1), 0, 0)
            ),
        ),
        ((D, 4 * D), BF16, whole_block((D, 4 * D))),
        ((COL_HI - COL_LO, LANES), F32, whole_block((COL_HI - COL_LO, LANES))),
        ((D, LANES), F32, whole_block((D, LANES))),
    ]
    scratch = [
        pltpu.VMEM((shards, rows, LANES), BF16),
        pltpu.VMEM((flat_rows, LANES), F32),
        pltpu.VMEM((WIDE * PERIODS + LANES, LANES), F32),
        pltpu.VMEM((LAT_BANDS * HEADS, KEYS, LANES), BF16),
        pltpu.VMEM((5, D, LANES), F32),
        pltpu.VMEM((3 * D, D), BF16),
        pltpu.VMEM((D, D), BF16),
        pltpu.VMEM((per_step, D, HEADS * LANES), BF16),
        pltpu.VMEM((D, n), BF16),
        pltpu.SemaphoreType.DMA,
    ]
    kernel = functools.partial(
        window_forward_kernel, parts=len(parts), order=order, steps=steps, fused=fused
    )
    return call(kernel, (grid,), ins, outs, scratch, "window_forward", scalars=2)


COLUMN_BLOCK = 768
COLUMN_VECTORS = (
    "norm2_gain",
    "norm2_shift",
    "proj2_bias",
    "norm3_gain",
    "norm3_shift",
    "mlp_out_bias",
)
COLUMN_MATRICES = ("qkv2", "proj2", "mlp_in", "mlp_out")


def column_kernel(
    dense,
    x_ref,
    cot_ref,
    count_ref,
    out_ref,
    after_ref,
    branch_ref,
    grad_ref,
    mat,
    tall,
    w_qkv,
    w_proj,
    w_in,
    w_out,
    t_qkv,
    t_proj,
    t_in,
    t_out,
    vec,
    fvec,
    n2_s,
    dqkv_s,
    mixed_s,
    attn_s,
    n3_s,
    dpre_s,
    act_s,
    cot_s,
    sums,
    fsums,
    spread,
):
    step = pl.program_id(0)

    @pl.when(step == 0)
    def _():
        for name, plain, turned in (
            ("qkv2", w_qkv, t_qkv),
            ("proj2", w_proj, t_proj),
            ("mlp_in", w_in, t_in),
            ("mlp_out", w_out, t_out),
        ):
            rows, width = plain.shape
            source = tall if rows == FF else mat
            read_matrix(dense, COL_LO, name, source)
            plain[...] = joined(source, width).astype(BF16)
            turned[...] = joined(source, width).T.astype(BF16)
        for k, name in enumerate(COLUMN_VECTORS):
            vec[:, k : k + 1] = read_vector(dense, COL_LO, name)
        fvec[:, 0:1] = read_vector(dense, COL_LO, "mlp_in_bias")
        sums[...] = jnp.zeros_like(sums)
        fsums[...] = jnp.zeros_like(fsums)
        spread[...] = jnp.zeros_like(spread)

    groups = COLUMN_BLOCK // LANES
    cols = pl.ds(pl.multiple_of(step * COLUMN_BLOCK, COLUMN_BLOCK), COLUMN_BLOCK)
    x = x_ref[...]
    gain2, shift2, bias2, gain3, shift3, bias_out = [vec[:, k : k + 1] for k in range(6)]
    unit2, scale2 = norm_parts(x)
    n2 = (unit2 * gain2 + shift2).astype(BF16)
    n2_s[:, cols] = n2
    qkv = mm(t_qkv[...], n2).astype(BF16)
    key_id = lax.broadcasted_iota(jnp.int32, (LANES, LANES), 0)
    query_id = lax.broadcasted_iota(jnp.int32, (LANES, LANES), 1)
    same = key_id // LEVELS == query_id // LEVELS
    level = key_id % LEVELS
    probs, tall_probs, mixed = {}, {}, []
    for g in range(groups):
        lanes = slice(g * LANES, (g + 1) * LANES)
        valid = jnp.logical_and(same, level < count_ref[:, lanes])
        scatter_heads(spread.at[0, g], qkv[:D, lanes])
        scores = mm(qkv[D : 2 * D, lanes].T, spread[0, g])
        rounded = []
        for h in range(HEADS):
            score = jnp.where(valid, scores[:, head_lanes(h)] * SCALE, -jnp.inf)
            grown = jnp.exp(score - jnp.max(score, axis=0, keepdims=True))
            prob = grown * (1.0 / jnp.sum(grown, axis=0, keepdims=True))
            probs[g, h] = prob
            rounded.append(prob.astype(BF16))
        tall_probs[g] = jnp.concatenate(rounded, axis=1)
        mixed.append(diagonal(mm(qkv[2 * D :, lanes], tall_probs[g])))
    mixed = jnp.concatenate(mixed, axis=1).astype(BF16)
    mixed_s[:, cols] = mixed
    middle = x + (mm(t_proj[...], mixed) + bias2)
    unit3, scale3 = norm_parts(middle)
    n3 = (unit3 * gain3 + shift3).astype(BF16)
    n3_s[:, cols] = n3
    pre = mm(t_in[...], n3) + fvec[:, 0:1]
    root = math.sqrt(2.0 / math.pi)
    square = pre * pre
    share = 0.5 + 0.5 * jnp.tanh(pre * (root + (root * 0.044715) * square))
    act = pre * share
    slope = share + act * (1.0 - share) * (2.0 * root + (6.0 * root * 0.044715) * square)
    act = act.astype(BF16)
    act_s[:, cols] = act
    output = middle + (mm(t_out[...], act) + bias_out)
    out_ref[...] = output.T.astype(BF16)

    cot = cot_ref[...].astype(F32).T
    cot_bf = cot.astype(BF16)
    cot_s[:, cols] = cot_bf
    dpre = (mm(w_out[...], cot_bf) * slope).astype(BF16)
    dpre_s[:, cols] = dpre
    dn3 = mm(w_in[...], dpre)
    dmiddle = cot + norm_back(dn3, unit3, scale3, gain3)
    dattn = dmiddle.astype(BF16)
    attn_s[:, cols] = dattn
    dmixed = mm(w_proj[...], dattn).astype(BF16)
    dq, dk, dv = [], [], []
    for g in range(groups):
        lanes = slice(g * LANES, (g + 1) * LANES)
        scatter_heads(spread.at[1, g], dmixed[:, lanes])
        dprobs = mm(qkv[2 * D :, lanes].T, spread[1, g])
        dscores = []
        for h in range(HEADS):
            prob, dprob = probs[g, h], dprobs[:, head_lanes(h)]
            dscores.append(
                (prob * (dprob - jnp.sum(prob * dprob, axis=0, keepdims=True))).astype(BF16)
            )
        dscores = jnp.concatenate(dscores, axis=1)
        dq.append(diagonal(mm(qkv[D : 2 * D, lanes], dscores)) * SCALE)
        dk.append(mt(spread[0, g], dscores) * SCALE)
        dv.append(mt(spread[1, g], tall_probs[g]))
    dqkv = jnp.concatenate([jnp.concatenate(d, axis=1) for d in (dq, dk, dv)], axis=0).astype(BF16)
    dqkv_s[:, cols] = dqkv
    dn2 = mm(w_qkv[...], dqkv)
    dafter = dmiddle + norm_back(dn2, unit2, scale2, gain2)
    after_ref[...] = dafter
    branch_ref[...] = dafter.astype(BF16)
    for k, value in enumerate(
        (dn2 * unit2, dn2, dattn.astype(F32), dn3 * unit3, dn3, cot_bf.astype(F32))
    ):
        sums[k] += lane_fold(value)
    fsums[...] += lane_fold(dpre.astype(F32))

    @pl.when(step == pl.num_programs(0) - 1)
    def _():
        grad_ref[...] = jnp.zeros_like(grad_ref)
        split_into(mat, mt(n2_s[...], dqkv_s[...]))
        write_matrix(grad_ref, COL_LO, "qkv2", mat)
        split_into(mat, mt(mixed_s[...], attn_s[...]))
        write_matrix(grad_ref, COL_LO, "proj2", mat)
        split_into(mat, mt(n3_s[...], dpre_s[...]))
        write_matrix(grad_ref, COL_LO, "mlp_in", mat)
        split_into(tall, mt(act_s[...], cot_s[...]))
        write_matrix(grad_ref, COL_LO, "mlp_out", tall)
        for k, name in enumerate(COLUMN_VECTORS):
            write_vector(grad_ref, COL_LO, name, sums[k])
        write_vector(grad_ref, COL_LO, "mlp_in_bias", fsums[...])


def column_call(dense, after_t, cotangent, counts):
    n = after_t.shape[1]
    feature = lambda r: pl.BlockSpec((r, COLUMN_BLOCK), lambda i: (0, i))
    token = pl.BlockSpec((COLUMN_BLOCK, D), lambda i: (i, 0))
    keep = lambda r: pltpu.VMEM((r, n), BF16)
    return call(
        column_kernel,
        (n // COLUMN_BLOCK,),
        [
            (dense, whole_block(dense.shape)),
            (after_t, feature(D)),
            (cotangent, token),
            (counts, feature(1)),
        ],
        [
            ((n, D), BF16, token),
            ((D, n), F32, feature(D)),
            ((D, n), BF16, feature(D)),
            (dense.shape, F32, whole_block(dense.shape)),
        ],
        [
            pltpu.VMEM((FF // LANES, D, LANES), F32),
            pltpu.VMEM((2, FF, LANES), F32),
            pltpu.VMEM((D, 3 * D), BF16),
            pltpu.VMEM((D, D), BF16),
            pltpu.VMEM((D, FF), BF16),
            pltpu.VMEM((FF, D), BF16),
            pltpu.VMEM((3 * D, D), BF16),
            pltpu.VMEM((D, D), BF16),
            pltpu.VMEM((FF, D), BF16),
            pltpu.VMEM((D, FF), BF16),
            pltpu.VMEM((D, LANES), F32),
            pltpu.VMEM((FF, LANES), F32),
            keep(D),
            keep(3 * D),
            keep(D),
            keep(D),
            keep(D),
            keep(FF),
            keep(FF),
            keep(D),
            pltpu.VMEM((6, D, LANES), F32),
            pltpu.VMEM((FF, LANES), F32),
            pltpu.VMEM((2, COLUMN_BLOCK // LANES, D, HEADS * LANES), BF16),
        ],
        "column",
    )


def window_backward_kernel(me_ref, band_ref, *refs, order, fused):
    if fused:
        slots_ref, refs = refs[0], refs[1:]
    (
        grad_ref,
        weights_ref,
        vec,
        column_ref,
        shifted_ref,
        qkv_ref,
        mixed_ref,
        prob_ref,
        out_ref,
        keep_ref,
        send_ref,
        total,
        kept,
        wide,
        dense,
        mat,
        blocks,
        spread,
        normed_s,
        dqkv_s,
        mixed_s,
        grad_s,
        sums,
        sem,
    ) = refs
    step = pl.program_id(0)
    per_step = SLOT_BLOCK // LANES

    @pl.when(step == 0)
    def _():
        total[...] = jnp.zeros_like(total)
        sums[...] = jnp.zeros_like(sums)
        spread[...] = jnp.zeros_like(spread)

    cols = pl.ds(pl.multiple_of(step * SLOT_BLOCK, SLOT_BLOCK), SLOT_BLOCK)
    if fused:
        grad = to_slots(grad_ref[...], slots_ref[...])
    else:
        grad = grad_ref[...]
    grad_s[:, cols] = grad
    mixed_s[:, cols] = mixed_ref[...]
    dmixed = mm(weights_ref[:, 3 * D :], grad).astype(BF16)
    qkv = qkv_ref[...]
    dq, dk, dv = [], [], []
    for w in range(per_step):
        lanes = slice(w * LANES, (w + 1) * LANES)
        scatter_heads(spread.at[0, w], qkv[:D, lanes])
        scatter_heads(spread.at[1, w], dmixed[:, lanes])
        dprobs = mm(qkv[2 * D :, lanes].T[:KEYS], spread[1, w])
        dscores = []
        for h in range(HEADS):
            prob = prob_ref[w, :, head_lanes(h)].astype(F32)
            dprob = dprobs[:, head_lanes(h)]
            dscore = (prob * (dprob - jnp.sum(prob * dprob, axis=0, keepdims=True))).astype(BF16)
            dscores.append(dscore)
        for h in range(HEADS):
            kept[w, h] = dscores[h].astype(F32)
        blank = jnp.zeros((LANES - KEYS, HEADS * LANES), BF16)
        dscores = jnp.concatenate([jnp.concatenate(dscores, axis=1), blank], axis=0)
        probs = jnp.concatenate([prob_ref[w], blank], axis=0)
        dq.append(diagonal(mm(qkv[D : 2 * D, lanes], dscores)) * SCALE)
        dk.append(mt(spread[0, w], dscores) * SCALE)
        dv.append(mt(spread[1, w], probs))
    dqkv = jnp.concatenate([jnp.concatenate(d, axis=1) for d in (dq, dk, dv)], axis=0).astype(BF16)
    dqkv_s[:, cols] = dqkv

    def add(w, _):
        total[band_ref[step * per_step + w]] += kept[w]
        return 0

    lax.fori_loop(0, per_step, add, 0)
    unit, scale = norm_parts(shifted_ref[...].astype(F32))
    normed_s[:, cols] = (unit * vec[:, 0:1] + vec[:, 1:2]).astype(BF16)
    dnormed = mm(weights_ref[:, : 3 * D], dqkv)
    out_ref[...] = norm_back(dnormed, unit, scale, vec[:, 0:1]).astype(BF16)
    for k, value in enumerate((dnormed * unit, dnormed, grad.astype(F32))):
        sums[k] += lane_fold(value)

    @pl.when(step == pl.num_programs(0) - 1)
    def _():
        wide[:WIDE, :] = jnp.zeros((WIDE, LANES), F32)
        wide[WIDE + BIAS_ROWS :, :] = jnp.zeros((wide.shape[0] - WIDE - BIAS_ROWS, LANES), F32)

        def turn(k, _):
            for h in range(HEADS):
                spot = pl.multiple_of(WIDE + (k * HEADS + h) * WIN, 8)
                wide[pl.ds(spot, WIN), :KEYS] = total[k, h].T[:WIN]
            return 0

        lax.fori_loop(0, LAT_BANDS, turn, 0)
        dense[:COL_LO, :] = jnp.zeros((COL_LO, LANES), F32)
        write_bias(wide, dense, 0)
        covered = BIAS_ROW + DENSE * PERIODS
        dense[covered:, :] = jnp.zeros((dense.shape[0] - covered, LANES), F32)
        both = column_ref[COL_HI - COL_LO - 16 :, :]
        rows = lax.broadcasted_iota(jnp.int32, both.shape, 0) + (COL_HI - 16)
        lane = lane_ids(16)
        start = rows * LANES + lane < OFFSET["earth_bias"]
        dense[COL_LO : COL_HI - 16, :] = column_ref[: COL_HI - COL_LO - 16, :]
        dense[COL_HI - 16 : COL_HI, :] = jnp.where(start, both, dense[COL_HI - 16 : COL_HI, :])
        split_into(mat, mt(normed_s[...], dqkv_s[...]))
        write_matrix(dense, 0, "qkv1", mat)
        split_into(mat, mt(mixed_s[...], grad_s[...]))
        write_matrix(dense, 0, "proj1", mat)
        for k, name in enumerate(("norm1_gain", "norm1_shift", "proj1_bias")):
            write_vector(dense, 0, name, sums[k])
        shards, rows = blocks.shape[0], blocks.shape[1]
        for shard in range(shards):
            spot = position(me_ref[0] ^ shard, order)
            blocks[spot] = dense[shard * rows : (shard + 1) * rows, :].astype(BF16)
        first = pltpu.make_async_copy(blocks.at[pl.ds(0, shards // 2)], keep_ref, sem.at[0])
        second = pltpu.make_async_copy(
            blocks.at[pl.ds(shards // 2, shards // 2)], send_ref, sem.at[1]
        )
        first.start()
        second.start()
        first.wait()
        second.wait()


def window_backward_call(
    me, bands, order, shards, rows, slots, grad, weights, vec, column_grad, shifted, qkv, mixed, prob, fused
):
    n = shifted.shape[1]
    per_step = SLOT_BLOCK // LANES
    slot_block = lambda r: pl.BlockSpec((r, SLOT_BLOCK), lambda i, *_: (0, i))
    ins = [(me, None), (bands, None)]
    if fused:
        ins += [(slots, slot_block(1)), (grad, whole_block(grad.shape))]
    else:
        ins += [(grad, slot_block(D))]
    ins += [
        (weights, whole_block(weights.shape)),
        (vec, whole_block(vec.shape)),
        (column_grad, whole_block(column_grad.shape)),
        (shifted, slot_block(D)),
        (qkv, slot_block(3 * D)),
        (mixed, slot_block(D)),
        (
            prob,
            pl.BlockSpec((per_step, KEYS, HEADS * LANES), lambda i, *_: (i, 0, 0)),
        ),
    ]
    flat_rows = max(shards * rows, BIAS_ROW + DENSE * PERIODS + 8)
    outs = [
        ((D, n), BF16, slot_block(D)),
        ((shards // 2, rows, LANES), BF16, pl.BlockSpec(memory_space=pl.ANY)),
        ((shards // 2, rows, LANES), BF16, pl.BlockSpec(memory_space=pl.ANY)),
    ]
    scratch = [
        pltpu.VMEM((LAT_BANDS, HEADS, KEYS, LANES), F32),
        pltpu.VMEM((per_step, HEADS, KEYS, LANES), F32),
        pltpu.VMEM((WIDE * (PERIODS + 2), LANES), F32),
        pltpu.VMEM((flat_rows, LANES), F32),
        pltpu.VMEM((5, D, LANES), F32),
        pltpu.VMEM((shards, rows, LANES), BF16),
        pltpu.VMEM((2, per_step, D, HEADS * LANES), BF16),
        pltpu.VMEM((D, n), BF16),
        pltpu.VMEM((3 * D, n), BF16),
        pltpu.VMEM((D, n), BF16),
        pltpu.VMEM((D, n), BF16),
        pltpu.VMEM((3, D, LANES), F32),
        pltpu.SemaphoreType.DMA((2,)),
    ]
    kernel = functools.partial(window_backward_kernel, order=order, fused=fused)
    return call(kernel, (n // SLOT_BLOCK,), ins, outs, scratch, "window_backward", scalars=2)


def finish_kernel(shift_ref, slots_ref, after_ref, out_ref):
    first = pl.program_id(0) * TOKEN_BLOCK
    back = from_slots(shift_ref[...], slots_ref[...], first, TOKEN_BLOCK)
    out_ref[...] = (after_ref[...] + back).T


def finish_call(grad_shifted, slots, after_t):
    n = after_t.shape[1]
    return call(
        finish_kernel,
        (n // TOKEN_BLOCK,),
        [
            (grad_shifted, whole_block(grad_shifted.shape)),
            (slots, whole_block(slots.shape)),
            (after_t, pl.BlockSpec((D, TOKEN_BLOCK), lambda i: (0, i))),
        ],
        [((n, D), F32, pl.BlockSpec((TOKEN_BLOCK, D), lambda i: (i, 0)))],
        [],
        "finish",
    )[0]


def body(block_input, cotangent, params, send_rows, window_band, level_count):
    model_width = block_input.shape[-1]
    rows_dev = block_input.shape[1] * block_input.shape[2]
    n_space, per_peer = send_rows.shape[1], send_rows.shape[3]
    devices = lax.axis_size(("dp", "space"))
    group = WIN // math.gcd(per_peer, WIN)
    if n_space % group:
        group = n_space
    fused = group == 1
    dest = n_space // group
    per_dest = group * per_peer // WIN
    member_groups = [[first + k for k in range(group)] for first in range(0, n_space, group)]
    place = lax.axis_index("space")
    index = lax.axis_index(("dp", "space"))
    me = index.astype(jnp.int32).reshape(1)
    bits = devices.bit_length() - 1
    order = [0] + list(range(bits - 1, 0, -1))

    def swap(value, bit):
        pairs = [(k, k ^ (1 << bit)) for k in range(devices)]
        return lax.ppermute(value, ("dp", "space"), pairs)

    def exchange(value):
        return lax.all_to_all(
            value, "space", split_axis=0, concat_axis=0, tiled=True, axis_index_groups=member_groups
        )

    def to_windows(rows):
        moved = exchange(rows[route_flat]).reshape(group, dest, per_peer, model_width)
        windows = moved.transpose(1, 0, 2, 3).reshape(-1, WIN, model_width)
        windows = jnp.pad(windows, ((0, 0), (0, LANES - WIN), (0, 0)))
        return windows.reshape(-1, model_width).T

    def from_windows(rows_t):
        rows = rows_t.T.reshape(-1, LANES, model_width)[:, :WIN]
        moved = rows.reshape(dest, group, per_peer, model_width).transpose(1, 0, 2, 3)
        rows = exchange(moved.reshape(rows_dev, model_width))
        return jnp.zeros((rows_dev, model_width), rows.dtype).at[route_flat].set(rows)

    shard_rows = params.shape[0] // LANES
    held = [params.astype(BF16).reshape(1, shard_rows, LANES)]
    for bit in reversed(order):
        held = held + [swap(part, bit) for part in held]
        if sum(part.shape[0] for part in held) <= devices // 4:
            held = [jnp.concatenate(held, axis=0)]

    flat_in = block_input[0].reshape(rows_dev, model_width)
    routes = send_rows[0, :, 0, :]
    route_flat = routes.reshape(-1)
    slots = jnp.pad(
        routes.reshape(-1, WIN), ((0, 0), (0, LANES - WIN)), constant_values=-1
    ).reshape(1, -1)
    if fused:
        bands = lax.all_to_all(
            window_band[0].reshape(n_space, per_dest), "space", split_axis=0, concat_axis=0, tiled=True
        ).reshape(-1)
        shifted = shift_call(flat_in, slots)
    else:
        all_bands = lax.all_gather(window_band[0], "space", axis=0)
        bands = lax.dynamic_slice(
            all_bands, ((place % group) * dest, (place // group) * per_dest), (dest, per_dest)
        ).reshape(-1)
        shifted = to_windows(flat_in)
    first, qkv, mixed, prob, weights, column_rows, vec = window_forward_call(
        me, bands, held, order, shifted, flat_in, slots, fused
    )
    if fused:
        after_t = first
    else:
        after_t = (flat_in.astype(F32) + from_windows(first).astype(F32)).T
    counts = jnp.repeat(level_count[0], LEVELS).reshape(1, -1)
    output, grad_after, grad_branch, column_grad = column_call(
        column_rows, after_t, cotangent[0].reshape(rows_dev, model_width), counts
    )
    if not fused:
        grad_branch = to_windows(grad_branch.T)
    grad_shifted, keep, send = window_backward_call(
        me, bands, order, devices, shard_rows, slots, grad_branch, weights, vec, column_grad,
        shifted, qkv, mixed, prob, fused
    )
    if fused:
        input_grad = finish_call(grad_shifted, slots, grad_after)
    else:
        input_grad = grad_after.T + from_windows(grad_shifted).astype(F32)
    total = keep.astype(F32) + swap(send, order[0]).astype(F32)
    for bit in order[1:]:
        half = total.shape[0] // 2
        total = total[:half] + swap(total[half:].astype(BF16), bit).astype(F32)
    return (
        output.reshape(block_input.shape),
        input_grad.reshape(block_input.shape),
        total.reshape(-1),
    )


def solution(mesh):
    return jax.shard_map(
        body,
        mesh=mesh,
        in_specs=(
            P("dp", "space", None, None),
            P("dp", "space", None, None),
            P(("dp", "space")),
            P("dp", None, "space", None),
            P("dp", "space"),
            P("dp", "space"),
        ),
        out_specs=(P("dp", "space", None, None), P("dp", "space", None, None), P(("dp", "space"))),
        check_vma=False,
    )
```

time: 726 us -> 229 us (0.32); the launches traced: 712 us -> 228 us
  local copies, waits for them, and re-layouts: 349 us -> 8.31 us
  Pallas kernels: 0 us -> 136 us
  matrix products: 127 us -> 0 us
  waiting for transfers between devices: 150 us -> 58 us
  other arithmetic: 57.7 us -> 3.58 us
  starting transfers between devices: 0.08 us -> 21.6 us
  between operations: 15.2 us -> 0.82 us
  blocking collectives: 13.5 us -> 0 us
    pallas_call x0 -> x5, Pallas kernels: none -> 136 us  [call(): pl.pallas_call(kernel, grid_spec=spec, out_shape=[jax.ShapeDtypeStruct(sh...]
    dot_general x32 -> x0, matrix products: 127 us -> none  [the longest x7 19.8 us: plain_product(): return jnp.dot(left, right, preferred_element_type=jnp.float32)]
    unnamed x3 -> x0, waiting for transfers between devices: 109 us -> none
    convert_element_type x17 -> x0, local copies, waits for them, and re-layouts: 89.1 us -> none  [the longest x2 30.4 us: column_backward(): grad_packed = jnp.stack([grad_query, grad_key, grad_value], axis=2).astyp...]
    reshape x16 -> x1, local copies, waits for them, and re-layouts: 58.7 us -> 0.62 us  [body(): bands = lax.all_to_all(window_band[0].reshape(n_space, per_dest), 'space'...]
    ppermute x0 -> x11, waiting for transfers between devices: none -> 58 us  [swap(): return lax.ppermute(value, ('dp', 'space'), pairs)]
    concatenate x1, local copies, waits for them, and re-layouts: 55.8 us -> 0.16 us  [body(): held = [jnp.concatenate(held, axis=0)]]
    all_gather x1 -> x0, waiting for transfers between devices: 40.7 us -> none  [body(): lax.all_gather(params.astype(jnp.bfloat16), ('dp', 'space'), axis=0, tile...]
  transfers between devices with their start and end apart: 2 -> 12, of which waited for: 2 -> 8; matrix products, arithmetic and copies ran while one was open for 7% -> 3% of each run, Pallas kernels for 0% -> 8%
where the time goes in v2:
time: 229 us; the launch traced here: 228 us
  Pallas kernels  136 us (59%)
  waiting for transfers between devices  58 us (25%)
  starting transfers between devices  21.6 us (9%)
  local copies, waits for them, and re-layouts  8.31 us (4%)
  other arithmetic  3.58 us (2%)
    pallas_call x5, Pallas kernels, call(): pl.pallas_call(kernel, grid_spec=spec, out_shape=[jax.ShapeDtypeStruct(sh...  136 us
    ppermute x11, waiting for transfers between devices, swap(): return lax.ppermute(value, ('dp', 'space'), pairs)  58 us
    ppermute x11, starting transfers between devices, swap(): return lax.ppermute(value, ('dp', 'space'), pairs)  15.8 us
    all_to_all x1, starting transfers between devices, body(): lax.all_to_all(window_band[0].reshape(n_space, per_dest), 'space', split_...  5.81 us
  transfers between devices with their start and end apart: 12, of which 8 were waited for; matrix products, arithmetic and copies ran while one was open for 3% of the time, Pallas kernels for 8%

profile of v2, /device:TPU:0, one launch (start us, length us, event | category | flops | bytes accessed | tf_op | source)
XLA Modules:
  0.0 227.9 jit_solution(2568137400253370483)
XLA Ops:
  1.6 3.1 %collective-permute-start = (bf16[1,297,128]{2,1,0:T(8,128)(2,1)S(1)}, bf16[1,297,128]{2,1,0:T(8,128)(2,1)S(1)}, u32[]{:S(2)}, u32[]{:S(2)}) collective-permute-start(bf16[1,297,128]{2,1,0:T(8,128)(2,1)S(1)} %convert_bitcast_fusion), channel_id=1, source_target_pairs={{0,2},{1,3},{2,0},{3,1},{4,6},{5,7},{6,4},{7,5},{8,10},{9,11},{10,... | collective-permute-start | bytes 228104 | tf_op jit(solution)/shard_map/ppermute | solution.py:908
  4.6 2.4 %collective-permute-done = bf16[1,297,128]{2,1,0:T(8,128)(2,1)S(1)} collective-permute-done((bf16[1,297,128]{2,1,0:T(8,128)(2,1)S(1)}, bf16[1,297,128]{2,1,0:T(8,128)(2,1)S(1)}, u32[]{:S(2)}, u32[]{:S(2)}) %collective-permute-start) | collective-permute-done | bytes 76064 | tf_op jit(solution)/shard_map/ppermute | solution.py:908
  7.1 3.1 %collective-permute-start.1 = (bf16[2,297,128]{2,1,0:T(8,128)(2,1)S(1)}, bf16[2,297,128]{2,1,0:T(8,128)(2,1)S(1)}, u32[]{:S(2)}, u32[]{:S(2)}) collective-permute-start(bf16[2,297,128]{2,1,0:T(8,128)(2,1)S(1)} %pad_maximum_fusion.2), channel_id=1, source_target_pairs={{0,4},{1,5},{2,6},{3,7},{4,0},{5,1},{6,2},{7,3},{8,12},{9,13},{10,... | collective-permute-start | bytes 456200 | tf_op jit(solution)/shard_map/ppermute | solution.py:908
  10.2 6.2 %collective-permute-done.1 = bf16[2,297,128]{2,1,0:T(8,128)(2,1)S(1)} collective-permute-done((bf16[2,297,128]{2,1,0:T(8,128)(2,1)S(1)}, bf16[2,297,128]{2,1,0:T(8,128)(2,1)S(1)}, u32[]{:S(2)}, u32[]{:S(2)}) %collective-permute-start.1) | collective-permute-done | bytes 152096 | tf_op jit(solution)/shard_map/ppermute | solution.py:908
  16.4 1.6 collective-permute-start.2
  18.0 6.6 %collective-permute-done.2 = bf16[4,297,128]{2,1,0:T(8,128)(2,1)S(1)} collective-permute-done((bf16[4,297,128]{2,1,0:T(8,128)(2,1)S(1)}, bf16[4,297,128]{2,1,0:T(8,128)(2,1)S(1)}, u32[]{:S(2)}, u32[]{:S(2)}) %collective-permute-start.2) | collective-permute-done | bytes 304160 | tf_op jit(solution)/shard_map/ppermute | solution.py:908
  24.9 1.7 collective-permute-start.3
  26.6 12.0 %collective-permute-done.3 = bf16[8,297,128]{2,0,1:T(8,128)(2,1)S(1)} collective-permute-done((bf16[8,297,128]{2,0,1:T(8,128)(2,1)S(1)}, bf16[8,297,128]{2,0,1:T(8,128)(2,1)S(1)}, u32[]{:S(2)}, u32[]{:S(2)}) %collective-permute-start.3) | collective-permute-done | bytes 608288 | tf_op jit(solution)/shard_map/ppermute | solution.py:908
  40.4 5.8 %all-to-all-start = ((s32[8,1,4]{2,1,0:T(1,128)}), s32[8,1,4]{2,1,0:T(1,128)S(1)}, u32[]{:S(2)}, u32[]{:S(2)}) async-start(s32[8,1,4]{2,1,0:T(1,128)} %bitcast.1), calls=%async_computation | async-start | bytes 8192 | tf_op jit(solution)/shard_map/all_to_all | solution.py:941
  47.8 7.8 %shift.1.refs_4_.refs_5_ = bf16[192,4096]{1,0:T(8,128)(2,1)} custom-call(bf16[2304,192]{1,0:T(8,128)(2,1)} %bitcast.11, s32[1,4096]{1,0:T(1,128)} %bitcast.15), custom_call_target="tpu_custom_call" | custom-call | tf_op jit(solution)/shard_map/shift/pallas_call | solution.py:263
  56.9 0.9 copy.12.refs_1_
  57.8 1.0 copy.13.refs_2_
  59.7 43.2 %window_forward.1 = (f32[192,2304]{1,0:T(8,128)}, bf16[576,4096]{1,0:T(8,128)(2,1)}, bf16[192,4096]{1,0:T(8,128)(2,1)}, bf16[32,80,768]{2,1,0:T(8,128)(2,1)}, bf...) custom-call(s32[1]{0:T(128)} %bitcast.me_ref, s32[32]{0:T(128)} %reshape.32.band_ref, ...), custom_call_target="tpu_custom_call" | custom-call | tf_op jit(solution)/shard_map/window_forward/pallas_call | solution.py:263
  102.9 34.0 %column.1 = (bf16[2304,192]{1,0:T(8,128)(2,1)}, f32[192,2304]{1,0:T(8,128)}, bf16[192,2304]{1,0:T(8,128)(2,1)}, f32[3488,128]{1,0:T(8,128)}) custom-call(f32[3488,128]{1,0:T(8,128)} %get-tuple-element.17.dense, f32[192,2304]{1,0:T(8,128)} %get-tuple-element.18.x_ref, bf16[2304,192]{1,0:T(8,128)(2,1)} %bitcast.14, s32[1,2304]{1,0:T(1,128)} %reshape_reshape.3.count_ref), custom_call_target="tpu_custom_call" | custom-call | tf_op jit(solution)/shard_map/column/pallas_call | solution.py:263
  136.9 39.5 %window_backward.1 = (bf16[192,4096]{1,0:T(8,128)(2,1)}, bf16[16,297,128]{2,1,0:T(8,128)(2,1)}, bf16[16,297,128]{2,1,0:T(8,128)(2,1)}) custom-call(s32[1]{0:T(128)} %bitcast.me_ref, s32[32]{0:T(128)} %reshape.32.band_ref, s32[1,4096]{1,0:T(1,128)} %bitcast.17, bf16[192,2304]{1,0:T(8,128)(2,1)} %get-tuple-element.20.refs_1_, ...), custom_call_target="tpu_custom_call" | custom-call | tf_op jit(solution)/shard_map/window_backward/pallas_call | solution.py:263
  176.5 1.7 copy.15
  178.7 2.5 %collective-permute-done.6 = bf16[16,297,128]{2,0,1:T(8,128)(2,1)S(1)} collective-permute-done((bf16[16,297,128]{2,0,1:T(8,128)(2,1)S(1)}, bf16[16,297,128]{2,0,1:T(8,128)(2,1)S(1)}, u32[]{:S(2)}, u32[]{:S(2)}) %collective-permute-start.6) | collective-permute-done | bytes 1216544 | tf_op jit(solution)/shard_map/ppermute | solution.py:908
  181.8 1.6 collective-permute-start.7
  183.4 14.5 %collective-permute-done.7 = bf16[8,297,128]{2,0,1:T(8,128)(2,1)S(1)} collective-permute-done((bf16[8,297,128]{2,0,1:T(8,128)(2,1)S(1)}, bf16[8,297,128]{2,0,1:T(8,128)(2,1)S(1)}, u32[]{:S(2)}, u32[]{:S(2)}) %collective-permute-start.7) | collective-permute-done | bytes 608288 | tf_op jit(solution)/shard_map/ppermute | solution.py:908
  198.0 1.6 collective-permute-start.8
  199.6 7.3 %collective-permute-done.8 = bf16[4,297,128]{2,1,0:T(8,128)(2,1)S(1)} collective-permute-done((bf16[4,297,128]{2,1,0:T(8,128)(2,1)S(1)}, bf16[4,297,128]{2,1,0:T(8,128)(2,1)S(1)}, u32[]{:S(2)}, u32[]{:S(2)}) %collective-permute-start.8) | collective-permute-done | bytes 304160 | tf_op jit(solution)/shard_map/ppermute | solution.py:908
  207.0 2.4 %collective-permute-start.9 = (bf16[2,297,128]{2,1,0:T(8,128)(2,1)S(1)}, bf16[2,297,128]{2,1,0:T(8,128)(2,1)S(1)}, u32[]{:S(2)}, u32[]{:S(2)}) collective-permute-start(bf16[2,297,128]{2,1,0:T(8,128)(2,1)S(1)} %slice.56), channel_id=1, source_target_pairs={{0,4},{1,5},{2,6},{3,7},{4,0},{5,1},{6,2},{7,3},{8,12},{9,13},{10,... | collective-permute-start | bytes 456200 | tf_op jit(solution)/shard_map/ppermute | solution.py:908
  209.4 6.5 %collective-permute-done.9 = bf16[2,297,128]{2,1,0:T(8,128)(2,1)S(1)} collective-permute-done((bf16[2,297,128]{2,1,0:T(8,128)(2,1)S(1)}, bf16[2,297,128]{2,1,0:T(8,128)(2,1)S(1)}, u32[]{:S(2)}, u32[]{:S(2)}) %collective-permute-start.9) | collective-permute-done | bytes 152096 | tf_op jit(solution)/shard_map/ppermute | solution.py:908
  216.2 11.0 %finish.1 = f32[2304,192]{1,0:T(8,128)} custom-call(bf16[192,4096]{1,0:T(8,128)(2,1)} %get-tuple-element.27.shift_ref, s32[1,4096]{1,0:T(1,128)} %bitcast.18, f32[192,2304]{1,0:T(8,128)} %get-tuple-element.28.after_ref), custom_call_target="tpu_custom_call" | custom-call | tf_op jit(solution)/shard_map/finish/pallas_call | solution.py:263
  (45 shorter events, 9.1 us)
Async XLA Ops:
  1.6 5.5 %collective-permute-start = (bf16[1,297,128]{2,1,0:T(8,128)(2,1)S(1)}, bf16[1,297,128]{2,1,0:T(8,128)(2,1)S(1)}, u32[]{:S(2)}, u32[]{:S(2)}) collective-permute-start(bf16[1,297,128]{2,1,0:T(8,128)(2,1)S(1)} %convert_bitcast_fusion), channel_id=1, source_target_pairs={{0,2},{1,3},{2,0},{3,1},{4,6},{5,7},{6,4},{7,5},{8,10},{9,11},{10,... | collective-permute-start | bytes 228104 | tf_op jit(solution)/shard_map/ppermute | solution.py:908
  7.0 32.0 %copy-start.4 = (s32[1,32]{1,0:T(1,128)S(1)}, s32[1,32]{1,0:T(1,128)}, u32[]{:S(2)}) copy-start(s32[1,32]{1,0:T(1,128)} %param.10) | copy-start | bytes 388
  7.1 39.2 %copy-start.3 = (s32[1,288]{1,0:T(1,128)S(1)}, s32[1,288]{1,0:T(1,128)}, u32[]{:S(2)}) copy-start(s32[1,288]{1,0:T(1,128)} %param.11) | copy-start | bytes 3460
  7.1 39.2 %copy-start.2 = (s32[1,8,1,288]{3,2,1,0:T(1,128)S(1)}, s32[1,8,1,288]{3,2,1,0:T(1,128)}, u32[]{:S(2)}) copy-start(s32[1,8,1,288]{3,2,1,0:T(1,128)} %param.9) | copy-start | bytes 27652
  7.1 9.3 %collective-permute-start.1 = (bf16[2,297,128]{2,1,0:T(8,128)(2,1)S(1)}, bf16[2,297,128]{2,1,0:T(8,128)(2,1)S(1)}, u32[]{:S(2)}, u32[]{:S(2)}) collective-permute-start(bf16[2,297,128]{2,1,0:T(8,128)(2,1)S(1)} %pad_maximum_fusion.2), channel_id=1, source_target_pairs={{0,4},{1,5},{2,6},{3,7},{4,0},{5,1},{6,2},{7,3},{8,12},{9,13},{10,... | collective-permute-start | bytes 456200 | tf_op jit(solution)/shard_map/ppermute | solution.py:908
  16.4 8.2 %collective-permute-start.2 = (bf16[4,297,128]{2,1,0:T(8,128)(2,1)S(1)}, bf16[4,297,128]{2,1,0:T(8,128)(2,1)S(1)}, u32[]{:S(2)}, u32[]{:S(2)}) collective-permute-start(bf16[4,297,128]{2,1,0:T(8,128)(2,1)S(1)} %pad_maximum_fusion.1), channel_id=1, source_target_pairs={{0,8},{1,9},{2,10},{3,11},{4,12},{5,13},{6,14},{7,15},{8,0},{9,1},... | collective-permute-start | bytes 912392 | tf_op jit(solution)/shard_map/ppermute | solution.py:908
  24.7 30.9 %copy-start = (bf16[8,297,128]{2,1,0:T(8,128)(2,1)}, bf16[8,297,128]{2,1,0:T(8,128)(2,1)S(1)}, u32[]{:S(2)}) copy-start(bf16[8,297,128]{2,1,0:T(8,128)(2,1)S(1)} %pad_maximum_fusion.refs_0_) | copy-start | bytes 1824772
  24.9 13.7 %collective-permute-start.3 = (bf16[8,297,128]{2,0,1:T(8,128)(2,1)S(1)}, bf16[8,297,128]{2,0,1:T(8,128)(2,1)S(1)}, u32[]{:S(2)}, u32[]{:S(2)}) collective-permute-start(bf16[8,297,128]{2,0,1:T(8,128)(2,1)S(1)} %copy.10), channel_id=1, source_target_pairs={{0,16},{1,17},{2,18},{3,19},{4,20},{5,21},{6,22},{7,23},{8,24},{9,... | collective-permute-start | bytes 1824776 | tf_op jit(solution)/shard_map/ppermute | solution.py:908
  26.6 31.2 %collective-permute-start.4 = (bf16[8,297,128]{2,0,1:T(8,128)(2,1)S(1)}, bf16[8,297,128]{2,0,1:T(8,128)(2,1)S(1)}, u32[]{:S(2)}, u32[]{:S(2)}) collective-permute-start(bf16[8,297,128]{2,0,1:T(8,128)(2,1)S(1)} %copy.10), channel_id=1, source_target_pairs={{0,1},{1,0},{2,3},{3,2},{4,5},{5,4},{6,7},{7,6},{8,9},{9,8},{10,11... | collective-permute-start | bytes 1824776 | tf_op jit(solution)/shard_map/ppermute | solution.py:908
  38.5 20.2 %collective-permute-start.5 = (bf16[8,297,128]{2,0,1:T(8,128)(2,1)S(1)}, bf16[8,297,128]{2,0,1:T(8,128)(2,1)S(1)}, u32[]{:S(2)}, u32[]{:S(2)}) collective-permute-start(bf16[8,297,128]{2,0,1:T(8,128)(2,1)S(1)} %collective-permute-done.3), channel_id=1, source_target_pairs={{0,1},{1,0},{2,3},{3,2},{4,5},{5,4},{6,7},{7,6},{8,9},{9,8},{10,11... | collective-permute-start | bytes 1824776 | tf_op jit(solution)/shard_map/ppermute | solution.py:908
  40.4 15.2 %all-to-all-start = ((s32[8,1,4]{2,1,0:T(1,128)}), s32[8,1,4]{2,1,0:T(1,128)S(1)}, u32[]{:S(2)}, u32[]{:S(2)}) async-start(s32[8,1,4]{2,1,0:T(1,128)} %bitcast.1), calls=%async_computation | async-start | bytes 8192 | tf_op jit(solution)/shard_map/all_to_all | solution.py:941
  176.4 4.8 %copy-start.1 = (bf16[16,297,128]{2,1,0:T(8,128)(2,1)S(1)}, bf16[16,297,128]{2,1,0:T(8,128)(2,1)}, u32[]{:S(2)}) copy-start(bf16[16,297,128]{2,1,0:T(8,128)(2,1)} %get-tuple-element.29) | copy-start | bytes 3649540
  178.2 3.1 %collective-permute-start.6 = (bf16[16,297,128]{2,0,1:T(8,128)(2,1)S(1)}, bf16[16,297,128]{2,0,1:T(8,128)(2,1)S(1)}, u32[]{:S(2)}, u32[]{:S(2)}) collective-permute-start(bf16[16,297,128]{2,0,1:T(8,128)(2,1)S(1)} %copy.15), channel_id=1, source_target_pairs={{0,1},{1,0},{2,3},{3,2},{4,5},{5,4},{6,7},{7,6},{8,9},{9,8},{10,11... | collective-permute-start | bytes 3649544 | tf_op jit(solution)/shard_map/ppermute | solution.py:908
  181.8 16.1 %collective-permute-start.7 = (bf16[8,297,128]{2,0,1:T(8,128)(2,1)S(1)}, bf16[8,297,128]{2,0,1:T(8,128)(2,1)S(1)}, u32[]{:S(2)}, u32[]{:S(2)}) collective-permute-start(bf16[8,297,128]{2,0,1:T(8,128)(2,1)S(1)} %copy.17), channel_id=1, source_target_pairs={{0,16},{1,17},{2,18},{3,19},{4,20},{5,21},{6,22},{7,23},{8,24},{9,... | collective-permute-start | bytes 1824776 | tf_op jit(solution)/shard_map/ppermute | solution.py:908
  198.0 8.9 %collective-permute-start.8 = (bf16[4,297,128]{2,1,0:T(8,128)(2,1)S(1)}, bf16[4,297,128]{2,1,0:T(8,128)(2,1)S(1)}, u32[]{:S(2)}, u32[]{:S(2)}) collective-permute-start(bf16[4,297,128]{2,1,0:T(8,128)(2,1)S(1)} %slice.55), channel_id=1, source_target_pairs={{0,8},{1,9},{2,10},{3,11},{4,12},{5,13},{6,14},{7,15},{8,0},{9,1},... | collective-permute-start | bytes 912392 | tf_op jit(solution)/shard_map/ppermute | solution.py:908
  207.0 8.9 %collective-permute-start.9 = (bf16[2,297,128]{2,1,0:T(8,128)(2,1)S(1)}, bf16[2,297,128]{2,1,0:T(8,128)(2,1)S(1)}, u32[]{:S(2)}, u32[]{:S(2)}) collective-permute-start(bf16[2,297,128]{2,1,0:T(8,128)(2,1)S(1)} %slice.56), channel_id=1, source_target_pairs={{0,4},{1,5},{2,6},{3,7},{4,0},{5,1},{6,2},{7,3},{8,12},{9,13},{10,... | collective-permute-start | bytes 456200 | tf_op jit(solution)/shard_map/ppermute | solution.py:908
  215.9 11.3 %collective-permute-start.10 = (bf16[1,297,128]{2,1,0:T(8,128)(2,1)S(1)}, bf16[1,297,128]{2,1,0:T(8,128)(2,1)S(1)}, u32[]{:S(2)}, u32[]{:S(2)}) collective-permute-start(bf16[1,297,128]{2,1,0:T(8,128)(2,1)S(1)} %slice.57), channel_id=1, source_target_pairs={{0,2},{1,3},{2,0},{3,1},{4,6},{5,7},{6,4},{7,5},{8,10},{9,11},{10,... | collective-permute-start | bytes 228104 | tf_op jit(solution)/shard_map/ppermute | solution.py:908

commit v3 on v2

--- a/solution.py
+++ b/solution.py
@@ -236,22 +236,25 @@
         block[head_rows(h), head_lanes(h)] = rows_in[head_rows(h), :]
 
 
-def chooser(first, rows, slots):
-    ids = lax.broadcasted_iota(jnp.int32, (rows, slots.shape[1]), 0) + first
-    return jnp.where(ids == slots, 1.0, 0.0).astype(BF16)
+def chooser(first, slots):
+    ids = lax.broadcasted_iota(jnp.int32, (PICK, slots.shape[1]), 0).astype(F32).astype(BF16)
+    near = jnp.clip(slots - first, -1, PICK).astype(F32).astype(BF16)
+    return jnp.where(ids == near, jnp.ones((), BF16), jnp.zeros((), BF16))
 
 
 def to_slots(rows_t, slots):
     tokens = rows_t.shape[1]
-    pick = jnp.concatenate([chooser(k, 256, slots) for k in range(0, tokens, 256)], axis=0)
+    pick = jnp.concatenate([chooser(k, slots) for k in range(0, tokens, PICK)], axis=0)
     return mm(rows_t, pick).astype(BF16)
 
 
 def from_slots(slot_rows, slots, first, rows):
-    return mt(slot_rows, chooser(first, rows, slots))
-
-
-def call(kernel, grid, ins, outs, scratch, name, scalars=0):
+    return jnp.concatenate(
+        [mt(slot_rows, chooser(first + k, slots)) for k in range(0, rows, PICK)], axis=1
+    )
+
+
+def call(kernel, grid, ins, outs, scratch, name, macs, scalars=0):
     in_specs = [s for _, s in ins]
     spec = pltpu.PrefetchScalarGridSpec(
         num_scalar_prefetch=scalars,
@@ -267,16 +270,28 @@
         compiler_params=pltpu.CompilerParams(
             dimension_semantics=("arbitrary",) * len(grid), vmem_limit_bytes=VMEM_LIMIT
         ),
+        cost_estimate=pl.CostEstimate(
+            flops=2 * macs,
+            transcendentals=0,
+            bytes_accessed=sum(a.size * a.dtype.itemsize for a, _ in ins)
+            + sum(math.prod(shape) * jnp.dtype(kind).itemsize for shape, kind, _ in outs),
+        ),
         name=name,
     )(*[a for a, _ in ins])
 
 
+def padded_rows(rows):
+    return -(-(rows + 1) // 8) * 8
+
+
 def whole_block(shape):
     return pl.BlockSpec(shape, lambda *_: (0,) * len(shape))
 
 
-SLOT_BLOCK = 512
-TOKEN_BLOCK = 256
+SLOT_BLOCK = 1024
+TURNS = 12
+PICK = 256
+TOKEN_BLOCK = 768
 
 
 def shift_kernel(x_ref, slots_ref, out_ref, x_t):
@@ -299,23 +314,28 @@
         [((D, n), BF16, pl.BlockSpec((D, SLOT_BLOCK), lambda i: (0, i)))],
         [pltpu.VMEM((D, count), BF16)],
         "shift",
+        D * count * n,
     )[0]
 
 
-def load_dense(me_ref, parts, blocks, dense, sem, order):
+def load_dense(me_ref, parts, plan, blocks, dense, sem, order, rows):
     copies = []
-    first = 0
-    for part in parts:
-        copies.append(pltpu.make_async_copy(part, blocks.at[pl.ds(first, part.shape[0])], sem))
-        first += part.shape[0]
+    for part, first, spot, count, row in plan:
+        copies.append(
+            pltpu.make_async_copy(
+                parts[part].at[pl.ds(first, count)],
+                blocks.at[pl.ds(spot, count), pl.ds(row, parts[part].shape[1])],
+                sem,
+            )
+        )
     for copy in copies:
         copy.start()
     for copy in copies:
         copy.wait()
-    shards, rows = blocks.shape[0], blocks.shape[1]
+    shards = blocks.shape[0]
     for shard in range(shards):
         spot = position(me_ref[0] ^ shard, order)
-        dense[shard * rows : (shard + 1) * rows, :] = blocks[spot].astype(F32)
+        dense[shard * rows : (shard + 1) * rows, :] = blocks[spot, :rows, :].astype(F32)
     if dense.shape[0] > shards * rows:
         dense[shards * rows :, :] = jnp.zeros((dense.shape[0] - shards * rows, LANES), F32)
 
@@ -327,7 +347,15 @@
     return spot
 
 
-def window_forward_kernel(me_ref, band_ref, *refs, parts, order, steps, fused):
+def band_of(table, window, me_ref, space, steps):
+    if not space:
+        return table[0, window]
+    each = steps * (SLOT_BLOCK // LANES) // space
+    return table[window // each, me_ref[0] % space * each + window % each]
+
+
+def window_forward_kernel(me_ref, band_ref, *refs, parts, plan, order, rows, steps, space):
+    fused = space > 0
     ins = refs[:parts]
     refs = refs[parts:]
     if fused:
@@ -343,6 +371,7 @@
         weights_ref,
         column_ref,
         vec,
+        table_ref,
         blocks,
         dense,
         wide,
@@ -352,13 +381,24 @@
         proj_t,
         spread,
         y_all,
+        band_s,
         sem,
     ) = refs
     step = pl.program_id(0)
 
     @pl.when(step == 0)
     def _():
-        load_dense(me_ref, ins, blocks, dense, sem, order)
+        load_dense(me_ref, ins, plan, blocks, dense, sem, order, rows)
+        if fused:
+            lines = []
+            for source in range(space):
+                shard = me_ref[0] // space * space + source
+                tile = blocks[position(me_ref[0] ^ shard, order), rows // 8 * 8 : rows // 8 * 8 + 8, :]
+                lines.append(tile.astype(F32)[rows % 8 : rows % 8 + 1])
+            table_ref[...] = jnp.concatenate(lines, axis=0).astype(jnp.int32)
+            copy = pltpu.make_async_copy(table_ref, band_s, sem)
+            copy.start()
+            copy.wait()
         column_ref[...] = dense[COL_LO:COL_HI, :]
         read_matrix(dense, 0, "qkv1", mat)
         weights_ref[:, : 3 * D] = joined(mat, 3 * D).astype(BF16)
@@ -373,11 +413,12 @@
         wide[BIAS_ROWS:, :] = jnp.zeros((wide.shape[0] - BIAS_ROWS, LANES), F32)
 
         def turn(k, _):
-            block = wide[pl.ds(pl.multiple_of(k * WIN, 8), LANES), :].T
-            bias[k, :WIN, :] = block[:WIN].astype(BF16)
+            for j in range(TURNS):
+                spot = pl.multiple_of((k * TURNS + j) * WIN, 8)
+                bias[k * TURNS + j, :WIN, :] = wide[pl.ds(spot, LANES), :].T[:WIN].astype(BF16)
             return 0
 
-        lax.fori_loop(0, LAT_BANDS * HEADS, turn, 0)
+        lax.fori_loop(0, LAT_BANDS * HEADS // TURNS, turn, 0)
         bias[:, WIN:, :] = jnp.full((LAT_BANDS * HEADS, KEYS - WIN, LANES), -jnp.inf, BF16)
         spread[...] = jnp.zeros_like(spread)
 
@@ -391,7 +432,7 @@
         mixed = []
         for w in range(per_step):
             lanes = slice(w * LANES, (w + 1) * LANES)
-            band = band_ref[step * per_step + w]
+            band = band_of(band_s if fused else band_ref, step * per_step + w, me_ref, space, steps)
             scatter_heads(spread.at[w], qkv[:D, lanes])
             scores = mm(qkv[D : 2 * D, lanes].T[:KEYS], spread[w])
             probs = []
@@ -423,11 +464,12 @@
             out_ref[...] = x_ref[...].astype(F32).T + branch
 
 
-def window_forward_call(me, bands, parts, order, shifted, tokens, slots, fused):
+def window_forward_call(me, bands, parts, plan, order, shards, rows, shifted, tokens, slots, space):
+    fused = space > 0
     n = shifted.shape[1]
     steps = n // SLOT_BLOCK
     per_step = SLOT_BLOCK // LANES
-    shards, rows = sum(p.shape[0] for p in parts), parts[0].shape[1]
+    padded = padded_rows(rows)
     flat_rows = max(shards * rows, BIAS_ROW + DENSE * PERIODS + 8)
     slot_block = lambda r: pl.BlockSpec((r, SLOT_BLOCK), lambda i, *_: (0, jnp.minimum(i, steps - 1)))
     ins = [(me, None), (bands, None)]
@@ -459,9 +501,10 @@
         ((D, 4 * D), BF16, whole_block((D, 4 * D))),
         ((COL_HI - COL_LO, LANES), F32, whole_block((COL_HI - COL_LO, LANES))),
         ((D, LANES), F32, whole_block((D, LANES))),
+        ((max(space, 1), LANES), jnp.int32, whole_block((max(space, 1), LANES))),
     ]
     scratch = [
-        pltpu.VMEM((shards, rows, LANES), BF16),
+        pltpu.VMEM((shards, padded, LANES), BF16),
         pltpu.VMEM((flat_rows, LANES), F32),
         pltpu.VMEM((WIDE * PERIODS + LANES, LANES), F32),
         pltpu.VMEM((LAT_BANDS * HEADS, KEYS, LANES), BF16),
@@ -470,12 +513,19 @@
         pltpu.VMEM((D, D), BF16),
         pltpu.VMEM((per_step, D, HEADS * LANES), BF16),
         pltpu.VMEM((D, n), BF16),
+        pltpu.SMEM((max(space, 1), LANES), jnp.int32),
         pltpu.SemaphoreType.DMA,
     ]
     kernel = functools.partial(
-        window_forward_kernel, parts=len(parts), order=order, steps=steps, fused=fused
+        window_forward_kernel,
+        parts=len(parts),
+        plan=plan,
+        order=order,
+        rows=rows,
+        steps=steps,
+        space=space,
     )
-    return call(kernel, (grid,), ins, outs, scratch, "window_forward", scalars=2)
+    return call(kernel, (grid,), ins, outs, scratch, "window_forward", 12 * D * D * n, scalars=2)
 
 
 COLUMN_BLOCK = 768
@@ -688,10 +738,12 @@
             pltpu.VMEM((2, COLUMN_BLOCK // LANES, D, HEADS * LANES), BF16),
         ],
         "column",
+        40 * D * D * n,
     )
 
 
-def window_backward_kernel(me_ref, band_ref, *refs, order, fused):
+def window_backward_kernel(me_ref, band_ref, *refs, order, shard_rows, space):
+    fused = space > 0
     if fused:
         slots_ref, refs = refs[0], refs[1:]
     (
@@ -762,7 +814,8 @@
     dqkv_s[:, cols] = dqkv
 
     def add(w, _):
-        total[band_ref[step * per_step + w]] += kept[w]
+        band = band_of(band_ref, step * per_step + w, me_ref, space, pl.num_programs(0))
+        total[band] += kept[w]
         return 0
 
     lax.fori_loop(0, per_step, add, 0)
@@ -801,10 +854,10 @@
         write_matrix(dense, 0, "proj1", mat)
         for k, name in enumerate(("norm1_gain", "norm1_shift", "proj1_bias")):
             write_vector(dense, 0, name, sums[k])
-        shards, rows = blocks.shape[0], blocks.shape[1]
+        shards, rows = blocks.shape[0], shard_rows
         for shard in range(shards):
             spot = position(me_ref[0] ^ shard, order)
-            blocks[spot] = dense[shard * rows : (shard + 1) * rows, :].astype(BF16)
+            blocks[spot, :rows, :] = dense[shard * rows : (shard + 1) * rows, :].astype(BF16)
         first = pltpu.make_async_copy(blocks.at[pl.ds(0, shards // 2)], keep_ref, sem.at[0])
         second = pltpu.make_async_copy(
             blocks.at[pl.ds(shards // 2, shards // 2)], send_ref, sem.at[1]
@@ -816,8 +869,10 @@
 
 
 def window_backward_call(
-    me, bands, order, shards, rows, slots, grad, weights, vec, column_grad, shifted, qkv, mixed, prob, fused
+    me, bands, order, shards, rows, slots, grad, weights, vec, column_grad, shifted, qkv, mixed, prob, space
 ):
+    fused = space > 0
+    padded = padded_rows(rows)
     n = shifted.shape[1]
     per_step = SLOT_BLOCK // LANES
     slot_block = lambda r: pl.BlockSpec((r, SLOT_BLOCK), lambda i, *_: (0, i))
@@ -841,8 +896,8 @@
     flat_rows = max(shards * rows, BIAS_ROW + DENSE * PERIODS + 8)
     outs = [
         ((D, n), BF16, slot_block(D)),
-        ((shards // 2, rows, LANES), BF16, pl.BlockSpec(memory_space=pl.ANY)),
-        ((shards // 2, rows, LANES), BF16, pl.BlockSpec(memory_space=pl.ANY)),
+        ((shards // 2, padded, LANES), BF16, pl.BlockSpec(memory_space=pl.ANY)),
+        ((shards // 2, padded, LANES), BF16, pl.BlockSpec(memory_space=pl.ANY)),
     ]
     scratch = [
         pltpu.VMEM((LAT_BANDS, HEADS, KEYS, LANES), F32),
@@ -850,7 +905,7 @@
         pltpu.VMEM((WIDE * (PERIODS + 2), LANES), F32),
         pltpu.VMEM((flat_rows, LANES), F32),
         pltpu.VMEM((5, D, LANES), F32),
-        pltpu.VMEM((shards, rows, LANES), BF16),
+        pltpu.VMEM((shards, padded, LANES), BF16),
         pltpu.VMEM((2, per_step, D, HEADS * LANES), BF16),
         pltpu.VMEM((D, n), BF16),
         pltpu.VMEM((3 * D, n), BF16),
@@ -859,8 +914,10 @@
         pltpu.VMEM((3, D, LANES), F32),
         pltpu.SemaphoreType.DMA((2,)),
     ]
-    kernel = functools.partial(window_backward_kernel, order=order, fused=fused)
-    return call(kernel, (n // SLOT_BLOCK,), ins, outs, scratch, "window_backward", scalars=2)
+    kernel = functools.partial(
+        window_backward_kernel, order=order, shard_rows=rows, space=space
+    )
+    return call(kernel, (n // SLOT_BLOCK,), ins, outs, scratch, "window_backward", 24 * D * D * n, scalars=2)
 
 
 def finish_kernel(shift_ref, slots_ref, after_ref, out_ref):
@@ -882,6 +939,7 @@
         [((n, D), F32, pl.BlockSpec((TOKEN_BLOCK, D), lambda i: (i, 0)))],
         [],
         "finish",
+        D * n * slots.shape[1],
     )[0]
 
 
@@ -924,13 +982,6 @@
         rows = exchange(moved.reshape(rows_dev, model_width))
         return jnp.zeros((rows_dev, model_width), rows.dtype).at[route_flat].set(rows)
 
-    shard_rows = params.shape[0] // LANES
-    held = [params.astype(BF16).reshape(1, shard_rows, LANES)]
-    for bit in reversed(order):
-        held = held + [swap(part, bit) for part in held]
-        if sum(part.shape[0] for part in held) <= devices // 4:
-            held = [jnp.concatenate(held, axis=0)]
-
     flat_in = block_input[0].reshape(rows_dev, model_width)
     routes = send_rows[0, :, 0, :]
     route_flat = routes.reshape(-1)
@@ -938,19 +989,55 @@
         routes.reshape(-1, WIN), ((0, 0), (0, LANES - WIN)), constant_values=-1
     ).reshape(1, -1)
     if fused:
-        bands = lax.all_to_all(
-            window_band[0].reshape(n_space, per_dest), "space", split_axis=0, concat_axis=0, tiled=True
-        ).reshape(-1)
-        shifted = shift_call(flat_in, slots)
+        bands = jnp.zeros((1, LANES), jnp.int32)
     else:
         all_bands = lax.all_gather(window_band[0], "space", axis=0)
         bands = lax.dynamic_slice(
             all_bands, ((place % group) * dest, (place // group) * per_dest), (dest, per_dest)
-        ).reshape(-1)
+        ).reshape(1, -1)
         shifted = to_windows(flat_in)
-    first, qkv, mixed, prob, weights, column_rows, vec = window_forward_call(
-        me, bands, held, order, shifted, flat_in, slots, fused
+
+    shard_rows = params.shape[0] // LANES
+    padded = padded_rows(shard_rows)
+    band_row = jnp.pad(window_band[0].astype(BF16), (0, LANES - window_band.shape[1]))
+    held = jnp.concatenate(
+        [
+            params.astype(BF16).reshape(shard_rows, LANES),
+            band_row.reshape(1, LANES),
+            jnp.zeros((padded - shard_rows - 1, LANES), BF16),
+        ],
+        axis=0,
+    ).reshape(1, padded, LANES)
+    for bit in reversed(order[3:]):
+        held = jnp.concatenate([held, swap(held, bit)], axis=0)
+    top, next_top = order[1], order[2]
+    cut = padded // 16 * 8
+    upper, lower = held[:, :cut], held[:, cut:]
+    upper = jnp.concatenate([upper, swap(upper, next_top)], axis=0)
+    lower = jnp.concatenate([lower, swap(lower, top)], axis=0)
+    if fused:
+        upper, lower, slots = lax.optimization_barrier((upper, lower, slots))
+        shifted = shift_call(flat_in, slots)
+    parts = [upper, swap(upper, top), lower, swap(lower, next_top)]
+    if fused:
+        parts, shifted = lax.optimization_barrier((parts, shifted))
+    parts = parts + [swap(part, order[0]) for part in parts]
+    few = devices // 8
+    plan = []
+    for core in range(2):
+        base = core * 4 * few
+        plan += [(4 * core, 0, base, 2 * few, 0), (4 * core + 1, 0, base + 2 * few, 2 * few, 0)]
+        for part, spot in ((2, 0), (3, few)):
+            plan += [
+                (4 * core + part, 0, base + spot, few, cut),
+                (4 * core + part, few, base + spot + 2 * few, few, cut),
+            ]
+    space = n_space if fused else 0
+    first, qkv, mixed, prob, weights, column_rows, vec, table = window_forward_call(
+        me, bands, parts, plan, order, devices, shard_rows, shifted, flat_in, slots, space
     )
+    if fused:
+        bands = table
     if fused:
         after_t = first
     else:
@@ -963,16 +1050,30 @@
         grad_branch = to_windows(grad_branch.T)
     grad_shifted, keep, send = window_backward_call(
         me, bands, order, devices, shard_rows, slots, grad_branch, weights, vec, column_grad,
-        shifted, qkv, mixed, prob, fused
+        shifted, qkv, mixed, prob, space
     )
+    total = keep.astype(F32) + swap(send, order[0]).astype(F32)
+    total, grad_shifted = lax.optimization_barrier((total, grad_shifted))
     if fused:
         input_grad = finish_call(grad_shifted, slots, grad_after)
     else:
         input_grad = grad_after.T + from_windows(grad_shifted).astype(F32)
-    total = keep.astype(F32) + swap(send, order[0]).astype(F32)
-    for bit in order[1:]:
+
+    def fold(kept, sent, bit):
+        return kept + swap(sent.astype(BF16), bit).astype(F32)
+
+    upper = total[:, :cut]
+    lower = total[:, cut:].reshape(2, 2, few, padded - cut, LANES)
+    upper = fold(upper[: 2 * few], upper[2 * few :], top)
+    lower = fold(lower[:, 0], lower[:, 1], next_top)
+    upper, lower, input_grad = lax.optimization_barrier((upper, lower, input_grad))
+    upper = fold(upper[:few], upper[few:], next_top)
+    lower = fold(lower[0], lower[1], top)
+    total = jnp.concatenate([upper, lower], axis=1)
+    for bit in order[3:]:
         half = total.shape[0] // 2
-        total = total[:half] + swap(total[half:].astype(BF16), bit).astype(F32)
+        total = fold(total[:half], total[half:], bit)
+    total = total[0, :shard_rows]
     return (
         output.reshape(block_input.shape),
         input_grad.reshape(block_input.shape),

time: 229 us -> 177 us (0.77)
  waiting for transfers between devices: 58 us -> 32.3 us
  Pallas kernels: 136 us -> 119 us
  local copies, waits for them, and re-layouts: 8.31 us -> 2.57 us
  starting transfers between devices: 21.6 us -> 17.1 us
    ppermute x11 -> x17, waiting for transfers between devices: 58 us -> 32.3 us  [swap(): return lax.ppermute(value, ('dp', 'space'), pairs)]
    pallas_call x5, Pallas kernels: 136 us -> 119 us  [call(): pl.pallas_call(kernel, grid_spec=spec, out_shape=[jax.ShapeDtypeStruct(sh...]
    all_to_all x1 -> x0, starting transfers between devices: 5.81 us -> none  [body(): lax.all_to_all(window_band[0].reshape(n_space, per_dest), 'space', split_...]
    ppermute x3 -> x0, local copies, waits for them, and re-layouts: 2.8 us -> none  [swap(): return lax.ppermute(value, ('dp', 'space'), pairs)]
    ppermute x11 -> x17, starting transfers between devices: 15.8 us -> 17.1 us  [swap(): return lax.ppermute(value, ('dp', 'space'), pairs)]
  transfers between devices with their start and end apart: 12 -> 17, of which waited for: 8 -> 12; matrix products, arithmetic and copies ran while one was open for 3% -> 1% of each run, Pallas kernels for 8% -> 9%
where the time goes in v3:
time: 177 us; the launch traced here: 176 us
  Pallas kernels  119 us (67%)
  waiting for transfers between devices  32.3 us (18%)
  starting transfers between devices  17.1 us (10%)
  other arithmetic  4.31 us (2%)
  local copies, waits for them, and re-layouts  2.57 us (1%)
    pallas_call x5, Pallas kernels, call(): pl.pallas_call(kernel, grid_spec=spec, out_shape=[jax.ShapeDtypeStruct(sh...  119 us
    ppermute x17, waiting for transfers between devices, swap(): return lax.ppermute(value, ('dp', 'space'), pairs)  32.3 us
    ppermute x17, starting transfers between devices, swap(): return lax.ppermute(value, ('dp', 'space'), pairs)  17.1 us
  transfers between devices with their start and end apart: 17, of which 12 were waited for; matrix products, arithmetic and copies ran while one was open for 1% of the time, Pallas kernels for 9%

profile of v3, /device:TPU:0, one launch (start us, length us, event | category | flops | bytes accessed | tf_op | source)
XLA Modules:
  0.0 176.4 jit_solution(6248827097425173984)
XLA Ops:
  1.3 0.9 convert_bitcast_fusion
  2.4 3.1 %collective-permute-start = (bf16[1,304,128]{2,1,0:T(8,128)(2,1)S(1)}, bf16[1,304,128]{2,1,0:T(8,128)(2,1)S(1)}, u32[]{:S(2)}, u32[]{:S(2)}) collective-permute-start(bf16[1,304,128]{2,1,0:T(8,128)(2,1)S(1)} %maximum_bitcast_fusion), channel_id=1, source_target_pairs={{0,2},{1,3},{2,0},{3,1},{4,6},{5,7},{6,4},{7,5},{8,10},{9,11},{10,... | collective-permute-start | bytes 233480 | tf_op jit(solution)/shard_map/ppermute | solution.py:966
  5.5 2.4 %collective-permute-done = bf16[1,304,128]{2,1,0:T(8,128)(2,1)S(1)} collective-permute-done((bf16[1,304,128]{2,1,0:T(8,128)(2,1)S(1)}, bf16[1,304,128]{2,1,0:T(8,128)(2,1)S(1)}, u32[]{:S(2)}, u32[]{:S(2)}) %collective-permute-start) | collective-permute-done | bytes 77856 | tf_op jit(solution)/shard_map/ppermute | solution.py:966
  7.9 3.1 %collective-permute-start.1 = (bf16[2,304,128]{2,1,0:T(8,128)(2,1)S(1)}, bf16[2,304,128]{2,1,0:T(8,128)(2,1)S(1)}, u32[]{:S(2)}, u32[]{:S(2)}) collective-permute-start(bf16[2,304,128]{2,1,0:T(8,128)(2,1)S(1)} %pad_maximum_fusion.4), channel_id=1, source_target_pairs={{0,4},{1,5},{2,6},{3,7},{4,0},{5,1},{6,2},{7,3},{8,12},{9,13},{10,... | collective-permute-start | bytes 466952 | tf_op jit(solution)/shard_map/ppermute | solution.py:966
  11.0 6.2 %collective-permute-done.1 = bf16[2,304,128]{2,1,0:T(8,128)(2,1)S(1)} collective-permute-done((bf16[2,304,128]{2,1,0:T(8,128)(2,1)S(1)}, bf16[2,304,128]{2,1,0:T(8,128)(2,1)S(1)}, u32[]{:S(2)}, u32[]{:S(2)}) %collective-permute-start.1) | collective-permute-done | bytes 155680 | tf_op jit(solution)/shard_map/ppermute | solution.py:966
  17.3 1.6 collective-permute-start.3
  18.9 1.5 collective-permute-start.2
  21.2 1.4 collective-permute-done.3
  22.6 1.5 collective-permute-done.2
  24.7 1.5 collective-permute-start.5
  26.3 6.9 %shift.1.refs_8_.refs_5_ = bf16[192,4096]{1,0:T(8,128)(2,1)} custom-call(bf16[2304,192]{1,0:T(8,128)(2,1)} %bitcast.33, s32[1,4096]{1,0:T(1,128)} %bitcast.29), custom_call_target="tpu_custom_call" | custom-call | flops 3623878656 | bytes 2473984 | tf_op jit(solution)/shard_map/shift/pallas_call | solution.py:266
  34.4 0.7 reshape_reshape.3.count_ref
  36.9 30.8 %window_forward.1 = (f32[192,2304]{1,0:T(8,128)}, bf16[576,4096]{1,0:T(8,128)(2,1)}, bf16[192,4096]{1,0:T(8,128)(2,1)}, bf16[32,80,768]{2,1,0:T(8,128)(2,1)}, bf...) custom-call(s32[1]{0:T(128)} %bitcast.me_ref, ...), custom_call_target="tpu_custom_call" | custom-call | flops 3623878656 | bytes 19141124 | tf_op jit(solution)/shard_map/window_forward/pallas_call | solution.py:266
  67.8 34.1 %column.1 = (bf16[2304,192]{1,0:T(8,128)(2,1)}, f32[192,2304]{1,0:T(8,128)}, bf16[192,2304]{1,0:T(8,128)(2,1)}, f32[3488,128]{1,0:T(8,128)}) custom-call(f32[3488,128]{1,0:T(8,128)} %get-tuple-element.39.dense, f32[192,2304]{1,0:T(8,128)} %get-tuple-element.40.x_ref, bf16[2304,192]{1,0:T(8,128)(2,1)} %bitcast.35, s32[1,2304]{1,0:T(1,128)} %reshape_reshape.3.count_ref), custom_call_target="tpu_custom_call" | custom-call | flops 6794772480 | bytes 9774080 | tf_op jit(solution)/shard_map/column/pallas_call | solution.py:266
  101.8 37.9 %window_backward.1 = (bf16[192,4096]{1,0:T(8,128)(2,1)}, bf16[16,304,128]{2,1,0:T(8,128)(2,1)}, bf16[16,304,128]{2,1,0:T(8,128)(2,1)}) custom-call(s32[1]{0:T(128)} %bitcast.me_ref, s32[8,128]{1,0:T(8,128)} %get-tuple-element.42.band_ref, s32[1,4096]{1,0:T(1,128)} %bitcast.31, bf16[192,2304]{1,0:T(8,128)(2,1)} %get-tuple-element.43.refs_1_, ...), custom_call_target="tpu_custom_call" | custom-call | flops 7247757312 | bytes 18944004 | tf_op jit(solution)/shard_map/window_backward/pallas_call | solution.py:266
  140.0 3.0 %collective-permute-done.10 = bf16[16,304,128]{2,1,0:T(8,128)(2,1)S(1)} collective-permute-done((bf16[16,304,128]{2,1,0:T(8,128)(2,1)}, bf16[16,304,128]{2,1,0:T(8,128)(2,1)S(1)}, u32[]{:S(2)}, u32[]{:S(2)}) %collective-permute-start.10) | collective-permute-done | bytes 1245216 | tf_op jit(solution)/shard_map/ppermute | solution.py:966
  143.0 1.6 convert_add_fusion
  144.7 1.6 collective-permute-start.11
  146.9 9.6 %finish.1 = f32[2304,192]{1,0:T(8,128)} custom-call(bf16[192,4096]{1,0:T(8,128)(2,1)} %get-tuple-element.54.shift_ref, s32[1,4096]{1,0:T(1,128)} %bitcast.32, f32[192,2304]{1,0:T(8,128)} %get-tuple-element.55.after_ref), custom_call_target="tpu_custom_call" | custom-call | flops 3623878656 | bytes 5128192 | tf_op jit(solution)/shard_map/finish/pallas_call | solution.py:266
  157.2 1.6 collective-permute-start.13
  158.8 3.4 %collective-permute-done.14 = bf16[4,152,128]{2,1,0:T(8,128)(2,1)S(1)} collective-permute-done((bf16[4,152,128]{2,1,0:T(8,128)(2,1)S(1)}, bf16[4,152,128]{2,1,0:T(8,128)(2,1)S(1)}, u32[]{:S(2)}, u32[]{:S(2)}) %collective-permute-start.14) | collective-permute-done | bytes 155680 | tf_op jit(solution)/shard_map/ppermute | solution.py:966
  162.7 8.6 %collective-permute-done.15 = bf16[2,304,128]{2,1,0:T(8,128)(2,1)S(1)} collective-permute-done((bf16[2,304,128]{2,1,0:T(8,128)(2,1)S(1)}, bf16[2,304,128]{2,1,0:T(8,128)(2,1)S(1)}, u32[]{:S(2)}, u32[]{:S(2)}) %collective-permute-start.15) | collective-permute-done | bytes 155680 | tf_op jit(solution)/shard_map/ppermute | solution.py:966
  171.4 4.4 %collective-permute-done.16 = bf16[1,304,128]{2,1,0:T(8,128)(2,1)S(1)} collective-permute-done((bf16[1,304,128]{2,1,0:T(8,128)(2,1)S(1)}, bf16[1,304,128]{2,1,0:T(8,128)(2,1)S(1)}, u32[]{:S(2)}, u32[]{:S(2)}) %collective-permute-start.16) | collective-permute-done | bytes 77856 | tf_op jit(solution)/shard_map/ppermute | solution.py:966
  175.8 0.7 fusion.6
  (68 shorter events, 7.4 us)
Async XLA Ops:
  0.6 19.8 %copy-start.2 = (s32[1,8,1,288]{3,2,1,0:T(1,128)S(1)}, s32[1,8,1,288]{3,2,1,0:T(1,128)}, u32[]{:S(2)}) copy-start(s32[1,8,1,288]{3,2,1,0:T(1,128)} %param.9) | copy-start | bytes 27652
  2.4 5.5 %collective-permute-start = (bf16[1,304,128]{2,1,0:T(8,128)(2,1)S(1)}, bf16[1,304,128]{2,1,0:T(8,128)(2,1)S(1)}, u32[]{:S(2)}, u32[]{:S(2)}) collective-permute-start(bf16[1,304,128]{2,1,0:T(8,128)(2,1)S(1)} %maximum_bitcast_fusion), channel_id=1, source_target_pairs={{0,2},{1,3},{2,0},{3,1},{4,6},{5,7},{6,4},{7,5},{8,10},{9,11},{10,... | collective-permute-start | bytes 233480 | tf_op jit(solution)/shard_map/ppermute | solution.py:966
  7.9 9.3 %collective-permute-start.1 = (bf16[2,304,128]{2,1,0:T(8,128)(2,1)S(1)}, bf16[2,304,128]{2,1,0:T(8,128)(2,1)S(1)}, u32[]{:S(2)}, u32[]{:S(2)}) collective-permute-start(bf16[2,304,128]{2,1,0:T(8,128)(2,1)S(1)} %pad_maximum_fusion.4), channel_id=1, source_target_pairs={{0,4},{1,5},{2,6},{3,7},{4,0},{5,1},{6,2},{7,3},{8,12},{9,13},{10,... | collective-permute-start | bytes 466952 | tf_op jit(solution)/shard_map/ppermute | solution.py:966
  17.3 5.3 %collective-permute-start.3 = (bf16[4,152,128]{2,1,0:T(8,128)(2,1)S(1)}, bf16[4,152,128]{2,1,0:T(8,128)(2,1)S(1)}, u32[]{:S(2)}, u32[]{:S(2)}) collective-permute-start(bf16[4,152,128]{2,1,0:T(8,128)(2,1)S(1)} %get-tuple-element.59), channel_id=1, source_target_pairs={{0,16},{1,17},{2,18},{3,19},{4,20},{5,21},{6,22},{7,23},{8,24},{9,... | collective-permute-start | bytes 466952 | tf_op jit(solution)/shard_map/ppermute | solution.py:966
  18.9 5.2 %collective-permute-start.2 = (bf16[4,152,128]{2,1,0:T(8,128)(2,1)S(1)}, bf16[4,152,128]{2,1,0:T(8,128)(2,1)S(1)}, u32[]{:S(2)}, u32[]{:S(2)}) collective-permute-start(bf16[4,152,128]{2,1,0:T(8,128)(2,1)S(1)} %get-tuple-element.60), channel_id=1, source_target_pairs={{0,8},{1,9},{2,10},{3,11},{4,12},{5,13},{6,14},{7,15},{8,0},{9,1},... | collective-permute-start | bytes 466952 | tf_op jit(solution)/shard_map/ppermute | solution.py:966
  22.6 11.2 %copy-start = (bf16[8,152,128]{2,1,0:T(8,128)(2,1)}, bf16[8,152,128]{2,1,0:T(8,128)(2,1)S(1)}, u32[]{:S(2)}) copy-start(bf16[8,152,128]{2,1,0:T(8,128)(2,1)S(1)} %pad_maximum_fusion.3.refs_2_) | copy-start | bytes 933892
  24.2 9.0 %copy-start.1 = (bf16[8,152,128]{2,1,0:T(8,128)(2,1)}, bf16[8,152,128]{2,1,0:T(8,128)(2,1)S(1)}, u32[]{:S(2)}) copy-start(bf16[8,152,128]{2,1,0:T(8,128)(2,1)S(1)} %pad_maximum_fusion.2.refs_0_) | copy-start | bytes 933892
  24.2 9.0 %collective-permute-start.4 = (bf16[8,152,128]{2,1,0:T(8,128)(2,1)S(1)}, bf16[8,152,128]{2,1,0:T(8,128)(2,1)S(1)}, u32[]{:S(2)}, u32[]{:S(2)}) collective-permute-start(bf16[8,152,128]{2,1,0:T(8,128)(2,1)S(1)} %pad_maximum_fusion.2.refs_0_), channel_id=1, source_target_pairs={{0,16},{1,17},{2,18},{3,19},{4,20},{5,21},{6,22},{7,23},{8,24},{9,... | collective-permute-start | bytes 933896 | tf_op jit(solution)/shard_map/ppermute | solution.py:966
  24.7 8.4 %collective-permute-start.5 = (bf16[8,152,128]{2,1,0:T(8,128)(2,1)S(1)}, bf16[8,152,128]{2,1,0:T(8,128)(2,1)S(1)}, u32[]{:S(2)}, u32[]{:S(2)}) collective-permute-start(bf16[8,152,128]{2,1,0:T(8,128)(2,1)S(1)} %pad_maximum_fusion.3.refs_2_), channel_id=1, source_target_pairs={{0,8},{1,9},{2,10},{3,11},{4,12},{5,13},{6,14},{7,15},{8,0},{9,1},... | collective-permute-start | bytes 933896 | tf_op jit(solution)/shard_map/ppermute | solution.py:966
  26.3 8.0 %copy-start.3 = (s32[1,288]{1,0:T(1,128)S(1)}, s32[1,288]{1,0:T(1,128)}, u32[]{:S(2)}) copy-start(s32[1,288]{1,0:T(1,128)} %param.11) | copy-start | bytes 3460
  33.2 3.6 %copy-start.4 = (bf16[8,152,128]{2,1,0:T(8,128)(2,1)}, bf16[8,152,128]{2,1,0:T(8,128)(2,1)S(1)}, u32[]{:S(2)}) copy-start(bf16[8,152,128]{2,1,0:T(8,128)(2,1)S(1)} %collective-permute-done.4.refs_1_) | copy-start | bytes 933892
  33.2 3.6 %copy-start.5 = (bf16[8,152,128]{2,1,0:T(8,128)(2,1)}, bf16[8,152,128]{2,1,0:T(8,128)(2,1)S(1)}, u32[]{:S(2)}) copy-start(bf16[8,152,128]{2,1,0:T(8,128)(2,1)S(1)} %collective-permute-done.5.refs_3_) | copy-start | bytes 933892
  33.2 1.9 %collective-permute-start.6 = (bf16[8,152,128]{2,1,0:T(8,128)(2,1)S(1)}, bf16[8,152,128]{2,1,0:T(8,128)(2,1)S(1)}, u32[]{:S(2)}, u32[]{:S(2)}) collective-permute-start(bf16[8,152,128]{2,1,0:T(8,128)(2,1)S(1)} %pad_maximum_fusion.2.refs_0_), channel_id=1, source_target_pairs={{0,1},{1,0},{2,3},{3,2},{4,5},{5,4},{6,7},{7,6},{8,9},{9,8},{10,11... | collective-permute-start | bytes 933896 | tf_op jit(solution)/shard_map/ppermute | solution.py:966
  33.3 2.0 %collective-permute-start.7 = (bf16[8,152,128]{2,1,0:T(8,128)(2,1)S(1)}, bf16[8,152,128]{2,1,0:T(8,128)(2,1)S(1)}, u32[]{:S(2)}, u32[]{:S(2)}) collective-permute-start(bf16[8,152,128]{2,1,0:T(8,128)(2,1)S(1)} %collective-permute-done.4.refs_1_), channel_id=1, source_target_pairs={{0,1},{1,0},{2,3},{3,2},{4,5},{5,4},{6,7},{7,6},{8,9},{9,8},{10,11... | collective-permute-start | bytes 933896 | tf_op jit(solution)/shard_map/ppermute | solution.py:966
  33.8 2.0 %collective-permute-start.8 = (bf16[8,152,128]{2,1,0:T(8,128)(2,1)S(1)}, bf16[8,152,128]{2,1,0:T(8,128)(2,1)S(1)}, u32[]{:S(2)}, u32[]{:S(2)}) collective-permute-start(bf16[8,152,128]{2,1,0:T(8,128)(2,1)S(1)} %pad_maximum_fusion.3.refs_2_), channel_id=1, source_target_pairs={{0,1},{1,0},{2,3},{3,2},{4,5},{5,4},{6,7},{7,6},{8,9},{9,8},{10,11... | collective-permute-start | bytes 933896 | tf_op jit(solution)/shard_map/ppermute | solution.py:966
  33.9 2.3 %collective-permute-start.9 = (bf16[8,152,128]{2,1,0:T(8,128)(2,1)S(1)}, bf16[8,152,128]{2,1,0:T(8,128)(2,1)S(1)}, u32[]{:S(2)}, u32[]{:S(2)}) collective-permute-start(bf16[8,152,128]{2,1,0:T(8,128)(2,1)S(1)} %collective-permute-done.5.refs_3_), channel_id=1, source_target_pairs={{0,1},{1,0},{2,3},{3,2},{4,5},{5,4},{6,7},{7,6},{8,9},{9,8},{10,11... | collective-permute-start | bytes 933896 | tf_op jit(solution)/shard_map/ppermute | solution.py:966
  35.1 1.6 copy-start.6
  139.8 3.2 %collective-permute-start.10 = (bf16[16,304,128]{2,1,0:T(8,128)(2,1)}, bf16[16,304,128]{2,1,0:T(8,128)(2,1)S(1)}, u32[]{:S(2)}, u32[]{:S(2)}) collective-permute-start(bf16[16,304,128]{2,1,0:T(8,128)(2,1)} %get-tuple-element.51), channel_id=1, source_target_pairs={{0,1},{1,0},{2,3},{3,2},{4,5},{5,4},{6,7},{7,6},{8,9},{9,8},{10,11... | collective-permute-start | bytes 3735560 | tf_op jit(solution)/shard_map/ppermute | solution.py:966
  144.7 11.8 %collective-permute-start.11 = (bf16[8,152,128]{2,1,0:T(8,128)(2,1)S(1)}, bf16[8,152,128]{2,1,0:T(8,128)(2,1)S(1)}, u32[]{:S(2)}, u32[]{:S(2)}) collective-permute-start(bf16[8,152,128]{2,1,0:T(8,128)(2,1)S(1)} %slice.107), channel_id=1, source_target_pairs={{0,16},{1,17},{2,18},{3,19},{4,20},{5,21},{6,22},{7,23},{8,24},{9,... | collective-permute-start | bytes 933896 | tf_op jit(solution)/shard_map/ppermute | solution.py:966
  146.3 10.2 %collective-permute-start.12 = (bf16[2,4,152,128]{3,2,1,0:T(8,128)(2,1)S(1)}, bf16[2,4,152,128]{3,2,1,0:T(8,128)(2,1)S(1)}, u32[]{:S(2)}, u32[]{:S(2)}) collective-permute-start(bf16[2,4,152,128]{3,2,1,0:T(8,128)(2,1)S(1)} %fusion.3), channel_id=1, source_target_pairs={{0,8},{1,9},{2,10},{3,11},{4,12},{5,13},{6,14},{7,15},{8,0},{9,1},... | collective-permute-start | bytes 933896 | tf_op jit(solution)/shard_map/ppermute | solution.py:966
  156.7 5.6 %collective-permute-start.14 = (bf16[4,152,128]{2,1,0:T(8,128)(2,1)S(1)}, bf16[4,152,128]{2,1,0:T(8,128)(2,1)S(1)}, u32[]{:S(2)}, u32[]{:S(2)}) collective-permute-start(bf16[4,152,128]{2,1,0:T(8,128)(2,1)S(1)} %fusion.5), channel_id=1, source_target_pairs={{0,16},{1,17},{2,18},{3,19},{4,20},{5,21},{6,22},{7,23},{8,24},{9,... | collective-permute-start | bytes 466952 | tf_op jit(solution)/shard_map/ppermute | solution.py:966
  157.2 5.3 %collective-permute-start.13 = (bf16[4,152,128]{2,1,0:T(8,128)(2,1)S(1)}, bf16[4,152,128]{2,1,0:T(8,128)(2,1)S(1)}, u32[]{:S(2)}, u32[]{:S(2)}) collective-permute-start(bf16[4,152,128]{2,1,0:T(8,128)(2,1)S(1)} %slice.108), channel_id=1, source_target_pairs={{0,8},{1,9},{2,10},{3,11},{4,12},{5,13},{6,14},{7,15},{8,0},{9,1},... | collective-permute-start | bytes 466952 | tf_op jit(solution)/shard_map/ppermute | solution.py:966
  162.6 8.7 %collective-permute-start.15 = (bf16[2,304,128]{2,1,0:T(8,128)(2,1)S(1)}, bf16[2,304,128]{2,1,0:T(8,128)(2,1)S(1)}, u32[]{:S(2)}, u32[]{:S(2)}) collective-permute-start(bf16[2,304,128]{2,1,0:T(8,128)(2,1)S(1)} %fusion.4), channel_id=1, source_target_pairs={{0,4},{1,5},{2,6},{3,7},{4,0},{5,1},{6,2},{7,3},{8,12},{9,13},{10,... | collective-permute-start | bytes 466952 | tf_op jit(solution)/shard_map/ppermute | solution.py:966
  171.3 4.5 %collective-permute-start.16 = (bf16[1,304,128]{2,1,0:T(8,128)(2,1)S(1)}, bf16[1,304,128]{2,1,0:T(8,128)(2,1)S(1)}, u32[]{:S(2)}, u32[]{:S(2)}) collective-permute-start(bf16[1,304,128]{2,1,0:T(8,128)(2,1)S(1)} %slice.109), channel_id=1, source_target_pairs={{0,2},{1,3},{2,0},{3,1},{4,6},{5,7},{6,4},{7,5},{8,10},{9,11},{10,... | collective-permute-start | bytes 233480 | tf_op jit(solution)/shard_map/ppermute | solution.py:966
  (3 other events, 3.1 us)

commit v4 on v3

--- a/solution.py
+++ b/solution.py
@@ -227,8 +227,47 @@
     return slice(h * LANES, (h + 1) * LANES)
 
 
-def diagonal(full):
-    return jnp.concatenate([full[head_rows(h), head_lanes(h)] for h in range(HEADS)], axis=0)
+def interleave(parts):
+    parts = list(parts)
+    live, started = [], 0
+    while live or started < len(parts):
+        if started < len(parts):
+            live.append(parts[started])
+            started += 1
+        live = [part for part in live if next(part, live) is None]
+
+
+def own_column(full, bits):
+    heads = []
+    for h in range(HEADS):
+        tiles = [full[k * LEVELS : (k + 1) * LEVELS, head_lanes(h)] for k in range(LANES // LEVELS)]
+        for bit in bits:
+            tiles = [jnp.where(bit, b, a) for a, b in zip(tiles[::2], tiles[1::2])]
+        heads.append(tiles[0])
+    return jnp.concatenate(heads, axis=1)
+
+
+def all_columns(own, same):
+    pair = jnp.concatenate([own, own], axis=0).astype(BF16)
+    tall = jnp.concatenate([pair] * (LANES // (2 * LEVELS)), axis=0)
+    return jnp.concatenate([tall[:, head_lanes(h)] * same for h in range(HEADS)], axis=1)
+
+
+def blend(rows_in, weights):
+    pieces = []
+    for h in range(0, HEADS, 2):
+        pair = slice(h * HEAD_DIM, (h + 2) * HEAD_DIM)
+        both = mm(rows_in[pair], weights[:, h * LANES : (h + 2) * LANES])
+        pieces += [both[:HEAD_DIM, :LANES], both[HEAD_DIM:, LANES:]]
+    return jnp.concatenate(pieces, axis=0)
+
+
+def gather_pairs(block, weights):
+    pieces = []
+    for h in range(0, HEADS, 2):
+        lanes = slice(h * LANES, (h + 2) * LANES)
+        pieces.append(mt(block[h * HEAD_DIM : (h + 2) * HEAD_DIM, lanes], weights[:, lanes]))
+    return jnp.concatenate(pieces, axis=0)
 
 
 def scatter_heads(block, rows_in):
@@ -429,23 +468,30 @@
         normed = (unit * vec[:, 0:1] + vec[:, 1:2]).astype(BF16)
         qkv = mm(qkv_t[...], normed).astype(BF16)
         qkv_ref[...] = qkv
-        mixed = []
-        for w in range(per_step):
-            lanes = slice(w * LANES, (w + 1) * LANES)
-            band = band_of(band_s if fused else band_ref, step * per_step + w, me_ref, space, steps)
-            scatter_heads(spread.at[w], qkv[:D, lanes])
-            scores = mm(qkv[D : 2 * D, lanes].T[:KEYS], spread[w])
-            probs = []
-            for h in range(HEADS):
-                score = scores[:, head_lanes(h)] * SCALE + bias[band * HEADS + h].astype(F32)
-                grown = jnp.exp(score - jnp.max(score, axis=0, keepdims=True))
-                probs.append(
-                    (grown * (1.0 / jnp.sum(grown, axis=0, keepdims=True))).astype(BF16)
-                )
-            prob = jnp.concatenate(probs, axis=1)
-            prob_ref[w] = prob
-            tall = jnp.concatenate([prob, jnp.zeros((LANES - KEYS, HEADS * LANES), BF16)], axis=0)
-            mixed.append(diagonal(mm(qkv[2 * D :, lanes], tall)))
+        blank = jnp.zeros((LANES - KEYS, HEADS * LANES), BF16)
+        scores, probs, mixed = {}, {}, []
+        for turn in range(per_step + 2):
+            if turn < per_step:
+                lanes = slice(turn * LANES, (turn + 1) * LANES)
+                scatter_heads(spread.at[turn], qkv[:D, lanes])
+                scores[turn] = mm(qkv[D : 2 * D, lanes].T[:KEYS], spread[turn])
+            if 1 <= turn <= per_step:
+                w = turn - 1
+                table = band_s if fused else band_ref
+                band = band_of(table, step * per_step + w, me_ref, space, steps)
+                heads = []
+                for h in range(HEADS):
+                    score = scores[w][:, head_lanes(h)] * SCALE + bias[band * HEADS + h].astype(F32)
+                    grown = jnp.exp(score - jnp.max(score, axis=0, keepdims=True))
+                    heads.append(
+                        (grown * (1.0 / jnp.sum(grown, axis=0, keepdims=True))).astype(BF16)
+                    )
+                probs[w] = jnp.concatenate(heads, axis=1)
+                prob_ref[w] = probs[w]
+            if turn >= 2:
+                w = turn - 2
+                tall = jnp.concatenate([probs[w], blank], axis=0)
+                mixed.append(blend(qkv[2 * D :, w * LANES : (w + 1) * LANES], tall))
         mixed = jnp.concatenate(mixed, axis=1).astype(BF16)
         mixed_ref[...] = mixed
         result = (mm(proj_t[...], mixed) + vec[:, 2:3]).astype(BF16)
@@ -529,6 +575,7 @@
 
 
 COLUMN_BLOCK = 768
+COLUMN_PART = 768
 COLUMN_VECTORS = (
     "norm2_gain",
     "norm2_shift",
@@ -595,86 +642,113 @@
         fsums[...] = jnp.zeros_like(fsums)
         spread[...] = jnp.zeros_like(spread)
 
-    groups = COLUMN_BLOCK // LANES
-    cols = pl.ds(pl.multiple_of(step * COLUMN_BLOCK, COLUMN_BLOCK), COLUMN_BLOCK)
-    x = x_ref[...]
     gain2, shift2, bias2, gain3, shift3, bias_out = [vec[:, k : k + 1] for k in range(6)]
-    unit2, scale2 = norm_parts(x)
-    n2 = (unit2 * gain2 + shift2).astype(BF16)
-    n2_s[:, cols] = n2
-    qkv = mm(t_qkv[...], n2).astype(BF16)
     key_id = lax.broadcasted_iota(jnp.int32, (LANES, LANES), 0)
     query_id = lax.broadcasted_iota(jnp.int32, (LANES, LANES), 1)
-    same = key_id // LEVELS == query_id // LEVELS
-    level = key_id % LEVELS
-    probs, tall_probs, mixed = {}, {}, []
-    for g in range(groups):
-        lanes = slice(g * LANES, (g + 1) * LANES)
-        valid = jnp.logical_and(same, level < count_ref[:, lanes])
-        scatter_heads(spread.at[0, g], qkv[:D, lanes])
-        scores = mm(qkv[D : 2 * D, lanes].T, spread[0, g])
-        rounded = []
-        for h in range(HEADS):
-            score = jnp.where(valid, scores[:, head_lanes(h)] * SCALE, -jnp.inf)
+    same = jnp.where(key_id // LEVELS == query_id // LEVELS, 1.0, 0.0).astype(BF16)
+    column = lax.broadcasted_iota(jnp.int32, (LEVELS, LANES), 1) // LEVELS
+    bits = [(column >> k) & 1 == 1 for k in range(4)]
+    level = lax.broadcasted_iota(jnp.int32, (LEVELS, LANES), 0)
+    groups = COLUMN_PART // LANES
+
+    def part_steps(part):
+        here = slice(part * COLUMN_PART, (part + 1) * COLUMN_PART)
+        start = step * COLUMN_BLOCK + part * COLUMN_PART
+        cols = pl.ds(pl.multiple_of(start, COLUMN_PART), COLUMN_PART)
+        x = x_ref[:, here]
+        unit2, scale2 = norm_parts(x)
+        n2 = (unit2 * gain2 + shift2).astype(BF16)
+        n2_s[:, cols] = n2
+        yield
+        qkv = mm(t_qkv[...], n2).astype(BF16)
+        yield
+        scores = []
+        for g in range(groups):
+            lanes = slice(g * LANES, (g + 1) * LANES)
+            scatter_heads(spread.at[0, part * groups + g], qkv[:D, lanes])
+            scores.append(own_column(mm(qkv[D : 2 * D, lanes].T, spread[0, part * groups + g]), bits))
+        yield
+        probs, tall_probs = [], []
+        for g in range(groups):
+            begin = part * COLUMN_PART + g * LANES
+            valid = level < count_ref[:, begin : begin + LANES]
+            score = jnp.where(jnp.concatenate([valid] * HEADS, axis=1), scores[g] * SCALE, -jnp.inf)
             grown = jnp.exp(score - jnp.max(score, axis=0, keepdims=True))
             prob = grown * (1.0 / jnp.sum(grown, axis=0, keepdims=True))
-            probs[g, h] = prob
-            rounded.append(prob.astype(BF16))
-        tall_probs[g] = jnp.concatenate(rounded, axis=1)
-        mixed.append(diagonal(mm(qkv[2 * D :, lanes], tall_probs[g])))
-    mixed = jnp.concatenate(mixed, axis=1).astype(BF16)
-    mixed_s[:, cols] = mixed
-    middle = x + (mm(t_proj[...], mixed) + bias2)
-    unit3, scale3 = norm_parts(middle)
-    n3 = (unit3 * gain3 + shift3).astype(BF16)
-    n3_s[:, cols] = n3
-    pre = mm(t_in[...], n3) + fvec[:, 0:1]
-    root = math.sqrt(2.0 / math.pi)
-    square = pre * pre
-    share = 0.5 + 0.5 * jnp.tanh(pre * (root + (root * 0.044715) * square))
-    act = pre * share
-    slope = share + act * (1.0 - share) * (2.0 * root + (6.0 * root * 0.044715) * square)
-    act = act.astype(BF16)
-    act_s[:, cols] = act
-    output = middle + (mm(t_out[...], act) + bias_out)
-    out_ref[...] = output.T.astype(BF16)
-
-    cot = cot_ref[...].astype(F32).T
-    cot_bf = cot.astype(BF16)
-    cot_s[:, cols] = cot_bf
-    dpre = (mm(w_out[...], cot_bf) * slope).astype(BF16)
-    dpre_s[:, cols] = dpre
-    dn3 = mm(w_in[...], dpre)
-    dmiddle = cot + norm_back(dn3, unit3, scale3, gain3)
-    dattn = dmiddle.astype(BF16)
-    attn_s[:, cols] = dattn
-    dmixed = mm(w_proj[...], dattn).astype(BF16)
-    dq, dk, dv = [], [], []
-    for g in range(groups):
-        lanes = slice(g * LANES, (g + 1) * LANES)
-        scatter_heads(spread.at[1, g], dmixed[:, lanes])
-        dprobs = mm(qkv[2 * D :, lanes].T, spread[1, g])
+            probs.append(prob)
+            tall_probs.append(all_columns(prob, same))
+        yield
+        mixed = [
+            blend(qkv[2 * D :, g * LANES : (g + 1) * LANES], tall_probs[g]) for g in range(groups)
+        ]
+        mixed = jnp.concatenate(mixed, axis=1).astype(BF16)
+        mixed_s[:, cols] = mixed
+        projected = mm(t_proj[...], mixed)
+        yield
+        middle = x + (projected + bias2)
+        unit3, scale3 = norm_parts(middle)
+        n3 = (unit3 * gain3 + shift3).astype(BF16)
+        n3_s[:, cols] = n3
+        yield
+        pre = mm(t_in[...], n3)
+        cot = cot_ref[here, :].astype(F32).T
+        cot_bf = cot.astype(BF16)
+        cot_s[:, cols] = cot_bf
+        dact = mm(w_out[...], cot_bf)
+        yield
+        pre = pre + fvec[:, 0:1]
+        root = math.sqrt(2.0 / math.pi)
+        square = pre * pre
+        share = 0.5 + 0.5 * jnp.tanh(pre * (root + (root * 0.044715) * square))
+        act = pre * share
+        slope = share + act * (1.0 - share) * (2.0 * root + (6.0 * root * 0.044715) * square)
+        act = act.astype(BF16)
+        act_s[:, cols] = act
+        dpre = (dact * slope).astype(BF16)
+        dpre_s[:, cols] = dpre
+        yield
+        output = middle + (mm(t_out[...], act) + bias_out)
+        out_ref[here, :] = output.T.astype(BF16)
+        dn3 = mm(w_in[...], dpre)
+        yield
+        dmiddle = cot + norm_back(dn3, unit3, scale3, gain3)
+        dattn = dmiddle.astype(BF16)
+        attn_s[:, cols] = dattn
+        sums[2] += lane_fold(dattn.astype(F32))
+        sums[3] += lane_fold(dn3 * unit3)
+        sums[4] += lane_fold(dn3)
+        sums[5] += lane_fold(cot_bf.astype(F32))
+        fsums[...] += lane_fold(dpre.astype(F32))
+        yield
+        dmixed = mm(w_proj[...], dattn).astype(BF16)
+        dprobs = []
+        for g in range(groups):
+            lanes = slice(g * LANES, (g + 1) * LANES)
+            scatter_heads(spread.at[1, part * groups + g], dmixed[:, lanes])
+            dprobs.append(own_column(mm(qkv[2 * D :, lanes].T, spread[1, part * groups + g]), bits))
+        yield
         dscores = []
-        for h in range(HEADS):
-            prob, dprob = probs[g, h], dprobs[:, head_lanes(h)]
-            dscores.append(
-                (prob * (dprob - jnp.sum(prob * dprob, axis=0, keepdims=True))).astype(BF16)
-            )
-        dscores = jnp.concatenate(dscores, axis=1)
-        dq.append(diagonal(mm(qkv[D : 2 * D, lanes], dscores)) * SCALE)
-        dk.append(mt(spread[0, g], dscores) * SCALE)
-        dv.append(mt(spread[1, g], tall_probs[g]))
-    dqkv = jnp.concatenate([jnp.concatenate(d, axis=1) for d in (dq, dk, dv)], axis=0).astype(BF16)
-    dqkv_s[:, cols] = dqkv
-    dn2 = mm(w_qkv[...], dqkv)
-    dafter = dmiddle + norm_back(dn2, unit2, scale2, gain2)
-    after_ref[...] = dafter
-    branch_ref[...] = dafter.astype(BF16)
-    for k, value in enumerate(
-        (dn2 * unit2, dn2, dattn.astype(F32), dn3 * unit3, dn3, cot_bf.astype(F32))
-    ):
-        sums[k] += lane_fold(value)
-    fsums[...] += lane_fold(dpre.astype(F32))
+        for prob, dprob in zip(probs, dprobs):
+            dscore = prob * (dprob - jnp.sum(prob * dprob, axis=0, keepdims=True))
+            dscores.append(all_columns(dscore, same))
+        yield
+        dq, dk, dv = [], [], []
+        for g in range(groups):
+            dq.append(blend(qkv[D : 2 * D, g * LANES : (g + 1) * LANES], dscores[g]) * SCALE)
+            dk.append(gather_pairs(spread.at[0, part * groups + g], dscores[g]) * SCALE)
+            dv.append(gather_pairs(spread.at[1, part * groups + g], tall_probs[g]))
+        dqkv = [jnp.concatenate(d, axis=1) for d in (dq, dk, dv)]
+        dqkv = jnp.concatenate(dqkv, axis=0).astype(BF16)
+        dqkv_s[:, cols] = dqkv
+        dn2 = mm(w_qkv[...], dqkv)
+        yield
+        dafter = dmiddle + norm_back(dn2, unit2, scale2, gain2)
+        after_ref[:, here] = dafter
+        branch_ref[:, here] = dafter.astype(BF16)
+        sums[0] += lane_fold(dn2 * unit2)
+        sums[1] += lane_fold(dn2)
+
+    interleave([part_steps(part) for part in range(COLUMN_BLOCK // COLUMN_PART)])
 
     @pl.when(step == pl.num_programs(0) - 1)
     def _():
@@ -790,32 +864,39 @@
     mixed_s[:, cols] = mixed_ref[...]
     dmixed = mm(weights_ref[:, 3 * D :], grad).astype(BF16)
     qkv = qkv_ref[...]
-    dq, dk, dv = [], [], []
-    for w in range(per_step):
-        lanes = slice(w * LANES, (w + 1) * LANES)
-        scatter_heads(spread.at[0, w], qkv[:D, lanes])
-        scatter_heads(spread.at[1, w], dmixed[:, lanes])
-        dprobs = mm(qkv[2 * D :, lanes].T[:KEYS], spread[1, w])
-        dscores = []
-        for h in range(HEADS):
-            prob = prob_ref[w, :, head_lanes(h)].astype(F32)
-            dprob = dprobs[:, head_lanes(h)]
-            dscore = (prob * (dprob - jnp.sum(prob * dprob, axis=0, keepdims=True))).astype(BF16)
-            dscores.append(dscore)
-        for h in range(HEADS):
-            kept[w, h] = dscores[h].astype(F32)
-        blank = jnp.zeros((LANES - KEYS, HEADS * LANES), BF16)
-        dscores = jnp.concatenate([jnp.concatenate(dscores, axis=1), blank], axis=0)
-        probs = jnp.concatenate([prob_ref[w], blank], axis=0)
-        dq.append(diagonal(mm(qkv[D : 2 * D, lanes], dscores)) * SCALE)
-        dk.append(mt(spread[0, w], dscores) * SCALE)
-        dv.append(mt(spread[1, w], probs))
+    blank = jnp.zeros((LANES - KEYS, HEADS * LANES), BF16)
+    dq, dk, dv, dprobs, dscores = [], [], [], {}, {}
+    for turn in range(per_step + 2):
+        if turn < per_step:
+            lanes = slice(turn * LANES, (turn + 1) * LANES)
+            scatter_heads(spread.at[0, turn], qkv[:D, lanes])
+            scatter_heads(spread.at[1, turn], dmixed[:, lanes])
+            dprobs[turn] = mm(qkv[2 * D :, lanes].T[:KEYS], spread[1, turn])
+        if 1 <= turn <= per_step:
+            w = turn - 1
+            heads = []
+            for h in range(HEADS):
+                prob = prob_ref[w, :, head_lanes(h)].astype(F32)
+                dprob = dprobs[w][:, head_lanes(h)]
+                heads.append(
+                    (prob * (dprob - jnp.sum(prob * dprob, axis=0, keepdims=True))).astype(BF16)
+                )
+            dscores[w] = jnp.concatenate(heads, axis=1)
+            kept[w] = dscores[w]
+        if turn >= 2:
+            w = turn - 2
+            tall = jnp.concatenate([dscores[w], blank], axis=0)
+            dq.append(blend(qkv[D : 2 * D, w * LANES : (w + 1) * LANES], tall) * SCALE)
+            dk.append(gather_pairs(spread.at[0, w], tall) * SCALE)
+            tall = jnp.concatenate([prob_ref[w], blank], axis=0)
+            dv.append(gather_pairs(spread.at[1, w], tall))
     dqkv = jnp.concatenate([jnp.concatenate(d, axis=1) for d in (dq, dk, dv)], axis=0).astype(BF16)
     dqkv_s[:, cols] = dqkv
 
     def add(w, _):
         band = band_of(band_ref, step * per_step + w, me_ref, space, pl.num_programs(0))
-        total[band] += kept[w]
+        for h in range(HEADS):
+            total[band, h] += kept[w, :, head_lanes(h)].astype(F32)
         return 0
 
     lax.fori_loop(0, per_step, add, 0)
@@ -901,7 +982,7 @@
     ]
     scratch = [
         pltpu.VMEM((LAT_BANDS, HEADS, KEYS, LANES), F32),
-        pltpu.VMEM((per_step, HEADS, KEYS, LANES), F32),
+        pltpu.VMEM((per_step, KEYS, HEADS * LANES), BF16),
         pltpu.VMEM((WIDE * (PERIODS + 2), LANES), F32),
         pltpu.VMEM((flat_rows, LANES), F32),
         pltpu.VMEM((5, D, LANES), F32),
@@ -961,9 +1042,9 @@
     bits = devices.bit_length() - 1
     order = [0] + list(range(bits - 1, 0, -1))
 
-    def swap(value, bit):
-        pairs = [(k, k ^ (1 << bit)) for k in range(devices)]
-        return lax.ppermute(value, ("dp", "space"), pairs)
+    def swap(value, *across):
+        flip = sum(1 << bit for bit in across)
+        return lax.ppermute(value, ("dp", "space"), [(k, k ^ flip) for k in range(devices)])
 
     def exchange(value):
         return lax.all_to_all(
@@ -1008,7 +1089,10 @@
         ],
         axis=0,
     ).reshape(1, padded, LANES)
-    for bit in reversed(order[3:]):
+    near, far = order[-1], order[-2]
+    direct = [swap(held, near), swap(held, far), swap(held, near, far)]
+    held = jnp.concatenate([held] + direct, axis=0)
+    for bit in reversed(order[3:-2]):
         held = jnp.concatenate([held, swap(held, bit)], axis=0)
     top, next_top = order[1], order[2]
     cut = padded // 16 * 8
@@ -1059,8 +1143,8 @@
     else:
         input_grad = grad_after.T + from_windows(grad_shifted).astype(F32)
 
-    def fold(kept, sent, bit):
-        return kept + swap(sent.astype(BF16), bit).astype(F32)
+    def fold(kept, sent, *across):
+        return kept + swap(sent.astype(BF16), *across).astype(F32)
 
     upper = total[:, :cut]
     lower = total[:, cut:].reshape(2, 2, few, padded - cut, LANES)
@@ -1070,10 +1154,13 @@
     upper = fold(upper[:few], upper[few:], next_top)
     lower = fold(lower[0], lower[1], top)
     total = jnp.concatenate([upper, lower], axis=1)
-    for bit in order[3:]:
+    for bit in order[3:-2]:
         half = total.shape[0] // 2
         total = fold(total[:half], total[half:], bit)
-    total = total[0, :shard_rows]
+    own = total[0]
+    for k, across in ((1, (near,)), (2, (far,)), (3, (near, far))):
+        own = fold(own, total[k], *across)
+    total = own[:shard_rows]
     return (
         output.reshape(block_input.shape),
         input_grad.reshape(block_input.shape),

time: 177 us -> 148 us (0.84)
  Pallas kernels: 119 us -> 97.3 us
  waiting for transfers between devices: 32.3 us -> 22.6 us
  starting transfers between devices: 17.1 us -> 20.1 us
    pallas_call x5, Pallas kernels: 119 us -> 97.3 us  [call(): pl.pallas_call(kernel, grid_spec=spec, out_shape=[jax.ShapeDtypeStruct(sh...]
    ppermute x17 -> x19, waiting for transfers between devices: 32.3 us -> 22.6 us  [swap(): lax.ppermute(value, ('dp', 'space'), [(k, k ^ flip) for k in range(device...]
    ppermute x17 -> x19, starting transfers between devices: 17.1 us -> 20.1 us  [swap(): lax.ppermute(value, ('dp', 'space'), [(k, k ^ flip) for k in range(device...]
  transfers between devices with their start and end apart: 17 -> 19, of which waited for: 12 -> 13; matrix products, arithmetic and copies ran while one was open for 1% -> 1% of each run, Pallas kernels for 9% -> 11%
where the time goes in v4:
time: 148 us
  Pallas kernels  97.3 us (66%)
  waiting for transfers between devices  22.6 us (15%)
  starting transfers between devices  20.1 us (14%)
  other arithmetic  4.32 us (3%)
  local copies, waits for them, and re-layouts  2.57 us (2%)
    pallas_call x5, Pallas kernels, call(): pl.pallas_call(kernel, grid_spec=spec, out_shape=[jax.ShapeDtypeStruct(sh...  97.3 us
    ppermute x19, waiting for transfers between devices, swap(): lax.ppermute(value, ('dp', 'space'), [(k, k ^ flip) for k in range(device...  22.6 us
    ppermute x19, starting transfers between devices, swap(): lax.ppermute(value, ('dp', 'space'), [(k, k ^ flip) for k in range(device...  20.1 us
  transfers between devices with their start and end apart: 19, of which 13 were waited for; matrix products, arithmetic and copies ran while one was open for 1% of the time, Pallas kernels for 11%

profile of v4, /device:TPU:0, one launch (start us, length us, event | category | flops | bytes accessed | tf_op | source)
XLA Modules:
  0.0 147.7 jit_solution(3626843795887374437)
XLA Ops:
  1.3 0.9 convert_bitcast_fusion
  2.4 5.1 %collective-permute-start.2 = (bf16[1,304,128]{2,1,0:T(8,128)(2,1)S(1)}, bf16[1,304,128]{2,1,0:T(8,128)(2,1)S(1)}, u32[]{:S(2)}, u32[]{:S(2)}) collective-permute-start(bf16[1,304,128]{2,1,0:T(8,128)(2,1)S(1)} %maximum_bitcast_fusion), channel_id=1, source_target_pairs={{0,6},{1,7},{2,4},{3,5},{4,2},{5,3},{6,0},{7,1},{8,14},{9,15},{10,... | collective-permute-start | bytes 233480 | tf_op jit(solution)/shard_map/ppermute | solution.py:1047
  8.2 2.2 %collective-permute-done.2 = bf16[1,304,128]{2,1,0:T(8,128)(2,1)S(1)} collective-permute-done((bf16[1,304,128]{2,1,0:T(8,128)(2,1)S(1)}, bf16[1,304,128]{2,1,0:T(8,128)(2,1)S(1)}, u32[]{:S(2)}, u32[]{:S(2)}) %collective-permute-start.2) | collective-permute-done | bytes 77856 | tf_op jit(solution)/shard_map/ppermute | solution.py:1047
  10.4 3.7 %collective-permute-done.1 = bf16[1,304,128]{2,1,0:T(8,128)(2,1)S(1)} collective-permute-done((bf16[1,304,128]{2,1,0:T(8,128)(2,1)S(1)}, bf16[1,304,128]{2,1,0:T(8,128)(2,1)S(1)}, u32[]{:S(2)}, u32[]{:S(2)}) %collective-permute-start.1) | collective-permute-done | bytes 77856 | tf_op jit(solution)/shard_map/ppermute | solution.py:1047
  14.2 1.6 %collective-permute-start.4 = (bf16[4,152,128]{2,1,0:T(8,128)(2,1)S(1)}, bf16[4,152,128]{2,1,0:T(8,128)(2,1)S(1)}, u32[]{:S(2)}, u32[]{:S(2)}) collective-permute-start(bf16[4,152,128]{2,1,0:T(8,128)(2,1)S(1)} %get-tuple-element.62), channel_id=1, source_target_pairs={{0,16},{1,17},{2,18},{3,19},{4,20},{5,21},{6,22},{7,23},{8,24},{9,... | collective-permute-start | bytes 466952 | tf_op jit(solution)/shard_map/ppermute | solution.py:1047
  15.7 1.5 %collective-permute-start.3 = (bf16[4,152,128]{2,1,0:T(8,128)(2,1)S(1)}, bf16[4,152,128]{2,1,0:T(8,128)(2,1)S(1)}, u32[]{:S(2)}, u32[]{:S(2)}) collective-permute-start(bf16[4,152,128]{2,1,0:T(8,128)(2,1)S(1)} %get-tuple-element.63), channel_id=1, source_target_pairs={{0,8},{1,9},{2,10},{3,11},{4,12},{5,13},{6,14},{7,15},{8,0},{9,1},... | collective-permute-start | bytes 466952 | tf_op jit(solution)/shard_map/ppermute | solution.py:1047
  18.0 1.6 %collective-permute-done.4 = bf16[4,152,128]{2,1,0:T(8,128)(2,1)S(1)} collective-permute-done((bf16[4,152,128]{2,1,0:T(8,128)(2,1)S(1)}, bf16[4,152,128]{2,1,0:T(8,128)(2,1)S(1)}, u32[]{:S(2)}, u32[]{:S(2)}) %collective-permute-start.4) | collective-permute-done | bytes 155680 | tf_op jit(solution)/shard_map/ppermute | solution.py:1047
  19.6 1.4 collective-permute-done.3
  21.6 1.5 %collective-permute-start.6 = (bf16[8,152,128]{2,1,0:T(8,128)(2,1)S(1)}, bf16[8,152,128]{2,1,0:T(8,128)(2,1)S(1)}, u32[]{:S(2)}, u32[]{:S(2)}) collective-permute-start(bf16[8,152,128]{2,1,0:T(8,128)(2,1)S(1)} %pad_maximum_fusion.3.refs_2_), channel_id=1, source_target_pairs={{0,8},{1,9},{2,10},{3,11},{4,12},{5,13},{6,14},{7,15},{8,0},{9,1},... | collective-permute-start | bytes 933896 | tf_op jit(solution)/shard_map/ppermute | solution.py:1047
  23.1 6.9 %shift.1.refs_8_.refs_5_ = bf16[192,4096]{1,0:T(8,128)(2,1)} custom-call(bf16[2304,192]{1,0:T(8,128)(2,1)} %bitcast.41, s32[1,4096]{1,0:T(1,128)} %bitcast.37), custom_call_target="tpu_custom_call" | custom-call | flops 3623878656 | bytes 2473984 | tf_op jit(solution)/shard_map/shift/pallas_call | solution.py:305
  33.7 25.5 %window_forward.1 = (f32[192,2304]{1,0:T(8,128)}, bf16[576,4096]{1,0:T(8,128)(2,1)}, bf16[192,4096]{1,0:T(8,128)(2,1)}, bf16[32,80,768]{2,1,0:T(8,128)(2,1)}, bf...) custom-call(s32[1]{0:T(128)} %bitcast.me_ref, ...), custom_call_target="tpu_custom_call" | custom-call | flops 3623878656 | bytes 19141124 | tf_op jit(solution)/shard_map/window_forward/pallas_call | solution.py:305
  59.2 25.7 %column.1 = (bf16[2304,192]{1,0:T(8,128)(2,1)}, f32[192,2304]{1,0:T(8,128)}, bf16[192,2304]{1,0:T(8,128)(2,1)}, f32[3488,128]{1,0:T(8,128)}) custom-call(f32[3488,128]{1,0:T(8,128)} %get-tuple-element.39.dense, f32[192,2304]{1,0:T(8,128)} %get-tuple-element.40.x_ref, bf16[2304,192]{1,0:T(8,128)(2,1)} %bitcast.43, s32[1,2304]{1,0:T(1,128)} %reshape_reshape.3.count_ref), custom_call_target="tpu_custom_call" | custom-call | flops 6794772480 | bytes 9774080 | tf_op jit(solution)/shard_map/column/pallas_call | solution.py:305
  84.9 29.6 %window_backward.1 = (bf16[192,4096]{1,0:T(8,128)(2,1)}, bf16[16,304,128]{2,1,0:T(8,128)(2,1)}, bf16[16,304,128]{2,1,0:T(8,128)(2,1)}) custom-call(s32[1]{0:T(128)} %bitcast.me_ref, s32[8,128]{1,0:T(8,128)} %get-tuple-element.42.band_ref, s32[1,4096]{1,0:T(1,128)} %bitcast.39, bf16[192,2304]{1,0:T(8,128)(2,1)} %get-tuple-element.43.refs_1_, ...), custom_call_target="tpu_custom_call" | custom-call | flops 7247757312 | bytes 18944004 | tf_op jit(solution)/shard_map/window_backward/pallas_call | solution.py:305
  114.8 3.0 %collective-permute-done.11 = bf16[16,304,128]{2,1,0:T(8,128)(2,1)S(1)} collective-permute-done((bf16[16,304,128]{2,1,0:T(8,128)(2,1)}, bf16[16,304,128]{2,1,0:T(8,128)(2,1)S(1)}, u32[]{:S(2)}, u32[]{:S(2)}) %collective-permute-start.11) | collective-permute-done | bytes 1245216 | tf_op jit(solution)/shard_map/ppermute | solution.py:1047
  117.8 1.6 %convert_add_fusion = f32[16,304,128]{2,1,0:T(8,128)S(1)} fusion(bf16[16,304,128]{2,1,0:T(8,128)(2,1)S(1)} %collective-permute-done.11, bf16[16,304,128]{2,1,0:T(8,128)(2,1)} %get-tuple-element.50), kind=kLoop, calls=%fused_computation | loop fusion | flops 1867776 | bytes 4980736 | tf_op jit(solution)/shard_map/add | solution.py:1139
  119.5 1.6 %collective-permute-start.12 = (bf16[8,152,128]{2,1,0:T(8,128)(2,1)S(1)}, bf16[8,152,128]{2,1,0:T(8,128)(2,1)S(1)}, u32[]{:S(2)}, u32[]{:S(2)}) collective-permute-start(bf16[8,152,128]{2,1,0:T(8,128)(2,1)S(1)} %slice.119), channel_id=1, source_target_pairs={{0,16},{1,17},{2,18},{3,19},{4,20},{5,21},{6,22},{7,23},{8,24},{9,... | collective-permute-start | bytes 933896 | tf_op jit(solution)/shard_map/ppermute | solution.py:1047
  121.7 9.6 %finish.1 = f32[2304,192]{1,0:T(8,128)} custom-call(bf16[192,4096]{1,0:T(8,128)(2,1)} %get-tuple-element.54.shift_ref, s32[1,4096]{1,0:T(1,128)} %bitcast.40, f32[192,2304]{1,0:T(8,128)} %get-tuple-element.55.after_ref), custom_call_target="tpu_custom_call" | custom-call | flops 3623878656 | bytes 5128192 | tf_op jit(solution)/shard_map/finish/pallas_call | solution.py:305
  132.1 1.5 %collective-permute-start.14 = (bf16[4,152,128]{2,1,0:T(8,128)(2,1)S(1)}, bf16[4,152,128]{2,1,0:T(8,128)(2,1)S(1)}, u32[]{:S(2)}, u32[]{:S(2)}) collective-permute-start(bf16[4,152,128]{2,1,0:T(8,128)(2,1)S(1)} %slice.120), channel_id=1, source_target_pairs={{0,8},{1,9},{2,10},{3,11},{4,12},{5,13},{6,14},{7,15},{8,0},{9,1},... | collective-permute-start | bytes 466952 | tf_op jit(solution)/shard_map/ppermute | solution.py:1047
  133.6 3.4 %collective-permute-done.15 = bf16[4,152,128]{2,1,0:T(8,128)(2,1)S(1)} collective-permute-done((bf16[4,152,128]{2,1,0:T(8,128)(2,1)S(1)}, bf16[4,152,128]{2,1,0:T(8,128)(2,1)S(1)}, u32[]{:S(2)}, u32[]{:S(2)}) %collective-permute-start.15) | collective-permute-done | bytes 155680 | tf_op jit(solution)/shard_map/ppermute | solution.py:1047
  137.5 1.0 collective-permute-start.16
  138.5 1.8 %collective-permute-start.18 = (bf16[304,128]{1,0:T(8,128)(2,1)S(1)}, bf16[304,128]{1,0:T(8,128)(2,1)S(1)}, u32[]{:S(2)}, u32[]{:S(2)}) collective-permute-start(bf16[304,128]{1,0:T(8,128)(2,1)S(1)} %get-tuple-element.60), channel_id=1, source_target_pairs={{0,6},{1,7},{2,4},{3,5},{4,2},{5,3},{6,0},{7,1},{8,14},{9,15},{10,... | collective-permute-start | bytes 233480 | tf_op jit(solution)/shard_map/ppermute | solution.py:1047
  141.1 2.2 %collective-permute-done.16 = bf16[304,128]{1,0:T(8,128)(2,1)S(1)} collective-permute-done((bf16[304,128]{1,0:T(8,128)(2,1)S(1)}, bf16[304,128]{1,0:T(8,128)(2,1)S(1)}, u32[]{:S(2)}, u32[]{:S(2)}) %collective-permute-start.16) | collective-permute-done | bytes 77856 | tf_op jit(solution)/shard_map/ppermute | solution.py:1047
  143.3 1.4 collective-permute-done.18
  144.7 2.3 %collective-permute-done.17 = bf16[304,128]{1,0:T(8,128)(2,1)S(1)} collective-permute-done((bf16[304,128]{1,0:T(8,128)(2,1)S(1)}, bf16[304,128]{1,0:T(8,128)(2,1)S(1)}, u32[]{:S(2)}, u32[]{:S(2)}) %collective-permute-start.17) | collective-permute-done | bytes 77856 | tf_op jit(solution)/shard_map/ppermute | solution.py:1047
  (70 shorter events, 10.2 us)
Async XLA Ops:
  0.6 16.6 %copy-start.2 = (s32[1,8,1,288]{3,2,1,0:T(1,128)S(1)}, s32[1,8,1,288]{3,2,1,0:T(1,128)}, u32[]{:S(2)}) copy-start(s32[1,8,1,288]{3,2,1,0:T(1,128)} %param.9) | copy-start | bytes 27652
  2.4 8.0 %collective-permute-start.2 = (bf16[1,304,128]{2,1,0:T(8,128)(2,1)S(1)}, bf16[1,304,128]{2,1,0:T(8,128)(2,1)S(1)}, u32[]{:S(2)}, u32[]{:S(2)}) collective-permute-start(bf16[1,304,128]{2,1,0:T(8,128)(2,1)S(1)} %maximum_bitcast_fusion), channel_id=1, source_target_pairs={{0,6},{1,7},{2,4},{3,5},{4,2},{5,3},{6,0},{7,1},{8,14},{9,15},{10,... | collective-permute-start | bytes 233480 | tf_op jit(solution)/shard_map/ppermute | solution.py:1047
  7.6 6.5 %collective-permute-start.1 = (bf16[1,304,128]{2,1,0:T(8,128)(2,1)S(1)}, bf16[1,304,128]{2,1,0:T(8,128)(2,1)S(1)}, u32[]{:S(2)}, u32[]{:S(2)}) collective-permute-start(bf16[1,304,128]{2,1,0:T(8,128)(2,1)S(1)} %maximum_bitcast_fusion), channel_id=1, source_target_pairs={{0,4},{1,5},{2,6},{3,7},{4,0},{5,1},{6,2},{7,3},{8,12},{9,13},{10,... | collective-permute-start | bytes 233480 | tf_op jit(solution)/shard_map/ppermute | solution.py:1047
  7.6 6.5 %collective-permute-start = (bf16[1,304,128]{2,1,0:T(8,128)(2,1)S(1)}, bf16[1,304,128]{2,1,0:T(8,128)(2,1)S(1)}, u32[]{:S(2)}, u32[]{:S(2)}) collective-permute-start(bf16[1,304,128]{2,1,0:T(8,128)(2,1)S(1)} %maximum_bitcast_fusion), channel_id=1, source_target_pairs={{0,2},{1,3},{2,0},{3,1},{4,6},{5,7},{6,4},{7,5},{8,10},{9,11},{10,... | collective-permute-start | bytes 233480 | tf_op jit(solution)/shard_map/ppermute | solution.py:1047
  14.2 5.4 %collective-permute-start.4 = (bf16[4,152,128]{2,1,0:T(8,128)(2,1)S(1)}, bf16[4,152,128]{2,1,0:T(8,128)(2,1)S(1)}, u32[]{:S(2)}, u32[]{:S(2)}) collective-permute-start(bf16[4,152,128]{2,1,0:T(8,128)(2,1)S(1)} %get-tuple-element.62), channel_id=1, source_target_pairs={{0,16},{1,17},{2,18},{3,19},{4,20},{5,21},{6,22},{7,23},{8,24},{9,... | collective-permute-start | bytes 466952 | tf_op jit(solution)/shard_map/ppermute | solution.py:1047
  15.7 5.2 %collective-permute-start.3 = (bf16[4,152,128]{2,1,0:T(8,128)(2,1)S(1)}, bf16[4,152,128]{2,1,0:T(8,128)(2,1)S(1)}, u32[]{:S(2)}, u32[]{:S(2)}) collective-permute-start(bf16[4,152,128]{2,1,0:T(8,128)(2,1)S(1)} %get-tuple-element.63), channel_id=1, source_target_pairs={{0,8},{1,9},{2,10},{3,11},{4,12},{5,13},{6,14},{7,15},{8,0},{9,1},... | collective-permute-start | bytes 466952 | tf_op jit(solution)/shard_map/ppermute | solution.py:1047
  19.6 11.0 %copy-start = (bf16[8,152,128]{2,1,0:T(8,128)(2,1)}, bf16[8,152,128]{2,1,0:T(8,128)(2,1)S(1)}, u32[]{:S(2)}) copy-start(bf16[8,152,128]{2,1,0:T(8,128)(2,1)S(1)} %pad_maximum_fusion.3.refs_2_) | copy-start | bytes 933892
  21.0 9.0 %copy-start.1 = (bf16[8,152,128]{2,1,0:T(8,128)(2,1)}, bf16[8,152,128]{2,1,0:T(8,128)(2,1)S(1)}, u32[]{:S(2)}) copy-start(bf16[8,152,128]{2,1,0:T(8,128)(2,1)S(1)} %pad_maximum_fusion.2.refs_0_) | copy-start | bytes 933892
  21.0 8.9 %collective-permute-start.5 = (bf16[8,152,128]{2,1,0:T(8,128)(2,1)S(1)}, bf16[8,152,128]{2,1,0:T(8,128)(2,1)S(1)}, u32[]{:S(2)}, u32[]{:S(2)}) collective-permute-start(bf16[8,152,128]{2,1,0:T(8,128)(2,1)S(1)} %pad_maximum_fusion.2.refs_0_), channel_id=1, source_target_pairs={{0,16},{1,17},{2,18},{3,19},{4,20},{5,21},{6,22},{7,23},{8,24},{9,... | collective-permute-start | bytes 933896 | tf_op jit(solution)/shard_map/ppermute | solution.py:1047
  21.6 8.4 %collective-permute-start.6 = (bf16[8,152,128]{2,1,0:T(8,128)(2,1)S(1)}, bf16[8,152,128]{2,1,0:T(8,128)(2,1)S(1)}, u32[]{:S(2)}, u32[]{:S(2)}) collective-permute-start(bf16[8,152,128]{2,1,0:T(8,128)(2,1)S(1)} %pad_maximum_fusion.3.refs_2_), channel_id=1, source_target_pairs={{0,8},{1,9},{2,10},{3,11},{4,12},{5,13},{6,14},{7,15},{8,0},{9,1},... | collective-permute-start | bytes 933896 | tf_op jit(solution)/shard_map/ppermute | solution.py:1047
  23.1 8.0 %copy-start.3 = (s32[1,288]{1,0:T(1,128)S(1)}, s32[1,288]{1,0:T(1,128)}, u32[]{:S(2)}) copy-start(s32[1,288]{1,0:T(1,128)} %param.11) | copy-start | bytes 3460
  30.0 3.6 %copy-start.4 = (bf16[8,152,128]{2,1,0:T(8,128)(2,1)}, bf16[8,152,128]{2,1,0:T(8,128)(2,1)S(1)}, u32[]{:S(2)}) copy-start(bf16[8,152,128]{2,1,0:T(8,128)(2,1)S(1)} %collective-permute-done.5.refs_1_) | copy-start | bytes 933892
  30.0 1.9 %collective-permute-start.7 = (bf16[8,152,128]{2,1,0:T(8,128)(2,1)S(1)}, bf16[8,152,128]{2,1,0:T(8,128)(2,1)S(1)}, u32[]{:S(2)}, u32[]{:S(2)}) collective-permute-start(bf16[8,152,128]{2,1,0:T(8,128)(2,1)S(1)} %pad_maximum_fusion.2.refs_0_), channel_id=1, source_target_pairs={{0,1},{1,0},{2,3},{3,2},{4,5},{5,4},{6,7},{7,6},{8,9},{9,8},{10,11... | collective-permute-start | bytes 933896 | tf_op jit(solution)/shard_map/ppermute | solution.py:1047
  30.1 2.0 %collective-permute-start.8 = (bf16[8,152,128]{2,1,0:T(8,128)(2,1)S(1)}, bf16[8,152,128]{2,1,0:T(8,128)(2,1)S(1)}, u32[]{:S(2)}, u32[]{:S(2)}) collective-permute-start(bf16[8,152,128]{2,1,0:T(8,128)(2,1)S(1)} %collective-permute-done.5.refs_1_), channel_id=1, source_target_pairs={{0,1},{1,0},{2,3},{3,2},{4,5},{5,4},{6,7},{7,6},{8,9},{9,8},{10,11... | collective-permute-start | bytes 933896 | tf_op jit(solution)/shard_map/ppermute | solution.py:1047
  30.6 2.0 %collective-permute-start.9 = (bf16[8,152,128]{2,1,0:T(8,128)(2,1)S(1)}, bf16[8,152,128]{2,1,0:T(8,128)(2,1)S(1)}, u32[]{:S(2)}, u32[]{:S(2)}) collective-permute-start(bf16[8,152,128]{2,1,0:T(8,128)(2,1)S(1)} %pad_maximum_fusion.3.refs_2_), channel_id=1, source_target_pairs={{0,1},{1,0},{2,3},{3,2},{4,5},{5,4},{6,7},{7,6},{8,9},{9,8},{10,11... | collective-permute-start | bytes 933896 | tf_op jit(solution)/shard_map/ppermute | solution.py:1047
  30.7 2.3 %collective-permute-start.10 = (bf16[8,152,128]{2,1,0:T(8,128)(2,1)S(1)}, bf16[8,152,128]{2,1,0:T(8,128)(2,1)S(1)}, u32[]{:S(2)}, u32[]{:S(2)}) collective-permute-start(bf16[8,152,128]{2,1,0:T(8,128)(2,1)S(1)} %collective-permute-done.6.refs_3_), channel_id=1, source_target_pairs={{0,1},{1,0},{2,3},{3,2},{4,5},{5,4},{6,7},{7,6},{8,9},{9,8},{10,11... | collective-permute-start | bytes 933896 | tf_op jit(solution)/shard_map/ppermute | solution.py:1047
  114.6 3.2 %collective-permute-start.11 = (bf16[16,304,128]{2,1,0:T(8,128)(2,1)}, bf16[16,304,128]{2,1,0:T(8,128)(2,1)S(1)}, u32[]{:S(2)}, u32[]{:S(2)}) collective-permute-start(bf16[16,304,128]{2,1,0:T(8,128)(2,1)} %get-tuple-element.51), channel_id=1, source_target_pairs={{0,1},{1,0},{2,3},{3,2},{4,5},{5,4},{6,7},{7,6},{8,9},{9,8},{10,11... | collective-permute-start | bytes 3735560 | tf_op jit(solution)/shard_map/ppermute | solution.py:1047
  119.5 11.9 %collective-permute-start.12 = (bf16[8,152,128]{2,1,0:T(8,128)(2,1)S(1)}, bf16[8,152,128]{2,1,0:T(8,128)(2,1)S(1)}, u32[]{:S(2)}, u32[]{:S(2)}) collective-permute-start(bf16[8,152,128]{2,1,0:T(8,128)(2,1)S(1)} %slice.119), channel_id=1, source_target_pairs={{0,16},{1,17},{2,18},{3,19},{4,20},{5,21},{6,22},{7,23},{8,24},{9,... | collective-permute-start | bytes 933896 | tf_op jit(solution)/shard_map/ppermute | solution.py:1047
  121.1 10.3 %collective-permute-start.13 = (bf16[2,4,152,128]{3,2,1,0:T(8,128)(2,1)S(1)}, bf16[2,4,152,128]{3,2,1,0:T(8,128)(2,1)S(1)}, u32[]{:S(2)}, u32[]{:S(2)}) collective-permute-start(bf16[2,4,152,128]{3,2,1,0:T(8,128)(2,1)S(1)} %fusion.2), channel_id=1, source_target_pairs={{0,8},{1,9},{2,10},{3,11},{4,12},{5,13},{6,14},{7,15},{8,0},{9,1},... | collective-permute-start | bytes 933896 | tf_op jit(solution)/shard_map/ppermute | solution.py:1047
  131.5 5.6 %collective-permute-start.15 = (bf16[4,152,128]{2,1,0:T(8,128)(2,1)S(1)}, bf16[4,152,128]{2,1,0:T(8,128)(2,1)S(1)}, u32[]{:S(2)}, u32[]{:S(2)}) collective-permute-start(bf16[4,152,128]{2,1,0:T(8,128)(2,1)S(1)} %fusion.3), channel_id=1, source_target_pairs={{0,16},{1,17},{2,18},{3,19},{4,20},{5,21},{6,22},{7,23},{8,24},{9,... | collective-permute-start | bytes 466952 | tf_op jit(solution)/shard_map/ppermute | solution.py:1047
  132.1 5.3 %collective-permute-start.14 = (bf16[4,152,128]{2,1,0:T(8,128)(2,1)S(1)}, bf16[4,152,128]{2,1,0:T(8,128)(2,1)S(1)}, u32[]{:S(2)}, u32[]{:S(2)}) collective-permute-start(bf16[4,152,128]{2,1,0:T(8,128)(2,1)S(1)} %slice.120), channel_id=1, source_target_pairs={{0,8},{1,9},{2,10},{3,11},{4,12},{5,13},{6,14},{7,15},{8,0},{9,1},... | collective-permute-start | bytes 466952 | tf_op jit(solution)/shard_map/ppermute | solution.py:1047
  137.5 5.8 %collective-permute-start.16 = (bf16[304,128]{1,0:T(8,128)(2,1)S(1)}, bf16[304,128]{1,0:T(8,128)(2,1)S(1)}, u32[]{:S(2)}, u32[]{:S(2)}) collective-permute-start(bf16[304,128]{1,0:T(8,128)(2,1)S(1)} %get-tuple-element.59), channel_id=1, source_target_pairs={{0,2},{1,3},{2,0},{3,1},{4,6},{5,7},{6,4},{7,5},{8,10},{9,11},{10,... | collective-permute-start | bytes 233480 | tf_op jit(solution)/shard_map/ppermute | solution.py:1047
  138.5 6.2 %collective-permute-start.18 = (bf16[304,128]{1,0:T(8,128)(2,1)S(1)}, bf16[304,128]{1,0:T(8,128)(2,1)S(1)}, u32[]{:S(2)}, u32[]{:S(2)}) collective-permute-start(bf16[304,128]{1,0:T(8,128)(2,1)S(1)} %get-tuple-element.60), channel_id=1, source_target_pairs={{0,6},{1,7},{2,4},{3,5},{4,2},{5,3},{6,0},{7,1},{8,14},{9,15},{10,... | collective-permute-start | bytes 233480 | tf_op jit(solution)/shard_map/ppermute | solution.py:1047
  140.3 6.7 %collective-permute-start.17 = (bf16[304,128]{1,0:T(8,128)(2,1)S(1)}, bf16[304,128]{1,0:T(8,128)(2,1)S(1)}, u32[]{:S(2)}, u32[]{:S(2)}) collective-permute-start(bf16[304,128]{1,0:T(8,128)(2,1)S(1)} %get-tuple-element.61), channel_id=1, source_target_pairs={{0,4},{1,5},{2,6},{3,7},{4,0},{5,1},{6,2},{7,3},{8,12},{9,13},{10,... | collective-permute-start | bytes 233480 | tf_op jit(solution)/shard_map/ppermute | solution.py:1047
  (5 other events, 8.3 us)

commit v5 on v4

--- a/solution.py
+++ b/solution.py
@@ -22,7 +22,6 @@
 LOG2E = math.log2(math.e)
 F32 = jnp.float32
 BF16 = jnp.bfloat16
-VMEM_LIMIT = 58 << 20
 
 norm_eps = 1e-05
 
@@ -281,10 +280,24 @@
     return jnp.where(ids == near, jnp.ones((), BF16), jnp.zeros((), BF16))
 
 
+def spread_windows(rows_t):
+    blank = jnp.zeros((rows_t.shape[0], LANES - WIN), rows_t.dtype)
+    pieces = []
+    for k in range(0, rows_t.shape[1], WIN):
+        pieces += [rows_t[:, k : k + WIN], blank]
+    return jnp.concatenate(pieces, axis=1)
+
+
+def join_windows(rows_t):
+    return jnp.concatenate(
+        [rows_t[:, k : k + WIN] for k in range(0, rows_t.shape[1], LANES)], axis=1
+    )
+
+
 def to_slots(rows_t, slots):
     tokens = rows_t.shape[1]
     pick = jnp.concatenate([chooser(k, slots) for k in range(0, tokens, PICK)], axis=0)
-    return mm(rows_t, pick).astype(BF16)
+    return spread_windows(mm(rows_t, pick)).astype(BF16)
 
 
 def from_slots(slot_rows, slots, first, rows):
@@ -293,7 +306,7 @@
     )
 
 
-def call(kernel, grid, ins, outs, scratch, name, macs, scalars=0):
+def call(kernel, grid, ins, outs, scratch, name, macs, limit, scalars=0):
     in_specs = [s for _, s in ins]
     spec = pltpu.PrefetchScalarGridSpec(
         num_scalar_prefetch=scalars,
@@ -307,7 +320,7 @@
         grid_spec=spec,
         out_shape=[jax.ShapeDtypeStruct(shape, kind) for shape, kind, _ in outs],
         compiler_params=pltpu.CompilerParams(
-            dimension_semantics=("arbitrary",) * len(grid), vmem_limit_bytes=VMEM_LIMIT
+            dimension_semantics=("arbitrary",) * len(grid), vmem_limit_bytes=limit << 20
         ),
         cost_estimate=pl.CostEstimate(
             flops=2 * macs,
@@ -327,8 +340,10 @@
     return pl.BlockSpec(shape, lambda *_: (0,) * len(shape))
 
 
-SLOT_BLOCK = 1024
+SLOT_BLOCK = 2048
+TIGHT_BLOCK = SLOT_BLOCK // LANES * WIN
 TURNS = 12
+RING = 4
 PICK = 256
 TOKEN_BLOCK = 768
 
@@ -342,18 +357,19 @@
 
 
 def shift_call(tokens, slots):
-    count, n = tokens.shape[0], slots.shape[1]
+    count, n = tokens.shape[0], slots.shape[1] // WIN * LANES
     return call(
         shift_kernel,
         (n // SLOT_BLOCK,),
         [
             (tokens, whole_block(tokens.shape)),
-            (slots, pl.BlockSpec((1, SLOT_BLOCK), lambda i: (0, i))),
+            (slots, pl.BlockSpec((1, TIGHT_BLOCK), lambda i: (0, i))),
         ],
         [((D, n), BF16, pl.BlockSpec((D, SLOT_BLOCK), lambda i: (0, i)))],
         [pltpu.VMEM((D, count), BF16)],
         "shift",
         D * count * n,
+        24,
     )[0]
 
 
@@ -473,8 +489,8 @@
         for turn in range(per_step + 2):
             if turn < per_step:
                 lanes = slice(turn * LANES, (turn + 1) * LANES)
-                scatter_heads(spread.at[turn], qkv[:D, lanes])
-                scores[turn] = mm(qkv[D : 2 * D, lanes].T[:KEYS], spread[turn])
+                scatter_heads(spread.at[turn % RING], qkv[:D, lanes])
+                scores[turn] = mm(qkv[D : 2 * D, lanes].T[:KEYS], spread[turn % RING])
             if 1 <= turn <= per_step:
                 w = turn - 1
                 table = band_s if fused else band_ref
@@ -494,11 +510,12 @@
                 mixed.append(blend(qkv[2 * D :, w * LANES : (w + 1) * LANES], tall))
         mixed = jnp.concatenate(mixed, axis=1).astype(BF16)
         mixed_ref[...] = mixed
-        result = (mm(proj_t[...], mixed) + vec[:, 2:3]).astype(BF16)
+        result = mm(proj_t[...], mixed) + vec[:, 2:3]
         if fused:
-            y_all[:, pl.ds(pl.multiple_of(step * SLOT_BLOCK, SLOT_BLOCK), SLOT_BLOCK)] = result
+            spot = pl.ds(pl.multiple_of(step * TIGHT_BLOCK, TIGHT_BLOCK), TIGHT_BLOCK)
+            y_all[:, spot] = join_windows(result).astype(BF16)
         else:
-            out_ref[...] = result
+            out_ref[...] = result.astype(BF16)
 
     if fused:
 
@@ -557,8 +574,8 @@
         pltpu.VMEM((5, D, LANES), F32),
         pltpu.VMEM((3 * D, D), BF16),
         pltpu.VMEM((D, D), BF16),
-        pltpu.VMEM((per_step, D, HEADS * LANES), BF16),
-        pltpu.VMEM((D, n), BF16),
+        pltpu.VMEM((RING, D, HEADS * LANES), BF16),
+        pltpu.VMEM((D, n // LANES * WIN), BF16),
         pltpu.SMEM((max(space, 1), LANES), jnp.int32),
         pltpu.SemaphoreType.DMA,
     ]
@@ -571,7 +588,7 @@
         steps=steps,
         space=space,
     )
-    return call(kernel, (grid,), ins, outs, scratch, "window_forward", 12 * D * D * n, scalars=2)
+    return call(kernel, (grid,), ins, outs, scratch, "window_forward", 12 * D * D * n, 40, scalars=2)
 
 
 COLUMN_BLOCK = 768
@@ -608,14 +625,10 @@
     t_out,
     vec,
     fvec,
-    n2_s,
-    dqkv_s,
-    mixed_s,
-    attn_s,
-    n3_s,
-    dpre_s,
-    act_s,
-    cot_s,
+    grad_qkv,
+    grad_proj,
+    grad_in,
+    grad_out,
     sums,
     fsums,
     spread,
@@ -640,6 +653,8 @@
         fvec[:, 0:1] = read_vector(dense, COL_LO, "mlp_in_bias")
         sums[...] = jnp.zeros_like(sums)
         fsums[...] = jnp.zeros_like(fsums)
+        for grad in (grad_qkv, grad_proj, grad_in, grad_out):
+            grad[...] = jnp.zeros_like(grad)
         spread[...] = jnp.zeros_like(spread)
 
     gain2, shift2, bias2, gain3, shift3, bias_out = [vec[:, k : k + 1] for k in range(6)]
@@ -653,12 +668,9 @@
 
     def part_steps(part):
         here = slice(part * COLUMN_PART, (part + 1) * COLUMN_PART)
-        start = step * COLUMN_BLOCK + part * COLUMN_PART
-        cols = pl.ds(pl.multiple_of(start, COLUMN_PART), COLUMN_PART)
         x = x_ref[:, here]
         unit2, scale2 = norm_parts(x)
         n2 = (unit2 * gain2 + shift2).astype(BF16)
-        n2_s[:, cols] = n2
         yield
         qkv = mm(t_qkv[...], n2).astype(BF16)
         yield
@@ -682,18 +694,15 @@
             blend(qkv[2 * D :, g * LANES : (g + 1) * LANES], tall_probs[g]) for g in range(groups)
         ]
         mixed = jnp.concatenate(mixed, axis=1).astype(BF16)
-        mixed_s[:, cols] = mixed
         projected = mm(t_proj[...], mixed)
         yield
         middle = x + (projected + bias2)
         unit3, scale3 = norm_parts(middle)
         n3 = (unit3 * gain3 + shift3).astype(BF16)
-        n3_s[:, cols] = n3
         yield
         pre = mm(t_in[...], n3)
         cot = cot_ref[here, :].astype(F32).T
         cot_bf = cot.astype(BF16)
-        cot_s[:, cols] = cot_bf
         dact = mm(w_out[...], cot_bf)
         yield
         pre = pre + fvec[:, 0:1]
@@ -703,17 +712,16 @@
         act = pre * share
         slope = share + act * (1.0 - share) * (2.0 * root + (6.0 * root * 0.044715) * square)
         act = act.astype(BF16)
-        act_s[:, cols] = act
         dpre = (dact * slope).astype(BF16)
-        dpre_s[:, cols] = dpre
         yield
         output = middle + (mm(t_out[...], act) + bias_out)
         out_ref[here, :] = output.T.astype(BF16)
         dn3 = mm(w_in[...], dpre)
+        grad_out[...] += mt(act, cot_bf)
+        grad_in[...] += mt(n3, dpre)
         yield
         dmiddle = cot + norm_back(dn3, unit3, scale3, gain3)
         dattn = dmiddle.astype(BF16)
-        attn_s[:, cols] = dattn
         sums[2] += lane_fold(dattn.astype(F32))
         sums[3] += lane_fold(dn3 * unit3)
         sums[4] += lane_fold(dn3)
@@ -721,6 +729,7 @@
         fsums[...] += lane_fold(dpre.astype(F32))
         yield
         dmixed = mm(w_proj[...], dattn).astype(BF16)
+        grad_proj[...] += mt(mixed, dattn)
         dprobs = []
         for g in range(groups):
             lanes = slice(g * LANES, (g + 1) * LANES)
@@ -739,8 +748,8 @@
             dv.append(gather_pairs(spread.at[1, part * groups + g], tall_probs[g]))
         dqkv = [jnp.concatenate(d, axis=1) for d in (dq, dk, dv)]
         dqkv = jnp.concatenate(dqkv, axis=0).astype(BF16)
-        dqkv_s[:, cols] = dqkv
         dn2 = mm(w_qkv[...], dqkv)
+        grad_qkv[...] += mt(n2, dqkv)
         yield
         dafter = dmiddle + norm_back(dn2, unit2, scale2, gain2)
         after_ref[:, here] = dafter
@@ -753,13 +762,13 @@
     @pl.when(step == pl.num_programs(0) - 1)
     def _():
         grad_ref[...] = jnp.zeros_like(grad_ref)
-        split_into(mat, mt(n2_s[...], dqkv_s[...]))
+        split_into(mat, grad_qkv[...])
         write_matrix(grad_ref, COL_LO, "qkv2", mat)
-        split_into(mat, mt(mixed_s[...], attn_s[...]))
+        split_into(mat, grad_proj[...])
         write_matrix(grad_ref, COL_LO, "proj2", mat)
-        split_into(mat, mt(n3_s[...], dpre_s[...]))
+        split_into(mat, grad_in[...])
         write_matrix(grad_ref, COL_LO, "mlp_in", mat)
-        split_into(tall, mt(act_s[...], cot_s[...]))
+        split_into(tall, grad_out[...])
         write_matrix(grad_ref, COL_LO, "mlp_out", tall)
         for k, name in enumerate(COLUMN_VECTORS):
             write_vector(grad_ref, COL_LO, name, sums[k])
@@ -770,7 +779,6 @@
     n = after_t.shape[1]
     feature = lambda r: pl.BlockSpec((r, COLUMN_BLOCK), lambda i: (0, i))
     token = pl.BlockSpec((COLUMN_BLOCK, D), lambda i: (i, 0))
-    keep = lambda r: pltpu.VMEM((r, n), BF16)
     return call(
         column_kernel,
         (n // COLUMN_BLOCK,),
@@ -799,20 +807,17 @@
             pltpu.VMEM((D, FF), BF16),
             pltpu.VMEM((D, LANES), F32),
             pltpu.VMEM((FF, LANES), F32),
-            keep(D),
-            keep(3 * D),
-            keep(D),
-            keep(D),
-            keep(D),
-            keep(FF),
-            keep(FF),
-            keep(D),
+            pltpu.VMEM((D, 3 * D), F32),
+            pltpu.VMEM((D, D), F32),
+            pltpu.VMEM((D, FF), F32),
+            pltpu.VMEM((FF, D), F32),
             pltpu.VMEM((6, D, LANES), F32),
             pltpu.VMEM((FF, LANES), F32),
             pltpu.VMEM((2, COLUMN_BLOCK // LANES, D, HEADS * LANES), BF16),
         ],
         "column",
         40 * D * D * n,
+        44,
     )
 
 
@@ -839,10 +844,8 @@
         mat,
         blocks,
         spread,
-        normed_s,
-        dqkv_s,
-        mixed_s,
-        grad_s,
+        grad_qkv,
+        grad_proj,
         sums,
         sem,
     ) = refs
@@ -853,15 +856,15 @@
     def _():
         total[...] = jnp.zeros_like(total)
         sums[...] = jnp.zeros_like(sums)
+        grad_qkv[...] = jnp.zeros_like(grad_qkv)
+        grad_proj[...] = jnp.zeros_like(grad_proj)
         spread[...] = jnp.zeros_like(spread)
 
-    cols = pl.ds(pl.multiple_of(step * SLOT_BLOCK, SLOT_BLOCK), SLOT_BLOCK)
     if fused:
         grad = to_slots(grad_ref[...], slots_ref[...])
     else:
         grad = grad_ref[...]
-    grad_s[:, cols] = grad
-    mixed_s[:, cols] = mixed_ref[...]
+    grad_proj[...] += mt(mixed_ref[...], grad)
     dmixed = mm(weights_ref[:, 3 * D :], grad).astype(BF16)
     qkv = qkv_ref[...]
     blank = jnp.zeros((LANES - KEYS, HEADS * LANES), BF16)
@@ -869,9 +872,9 @@
     for turn in range(per_step + 2):
         if turn < per_step:
             lanes = slice(turn * LANES, (turn + 1) * LANES)
-            scatter_heads(spread.at[0, turn], qkv[:D, lanes])
-            scatter_heads(spread.at[1, turn], dmixed[:, lanes])
-            dprobs[turn] = mm(qkv[2 * D :, lanes].T[:KEYS], spread[1, turn])
+            scatter_heads(spread.at[0, turn % RING], qkv[:D, lanes])
+            scatter_heads(spread.at[1, turn % RING], dmixed[:, lanes])
+            dprobs[turn] = mm(qkv[2 * D :, lanes].T[:KEYS], spread[1, turn % RING])
         if 1 <= turn <= per_step:
             w = turn - 1
             heads = []
@@ -887,11 +890,10 @@
             w = turn - 2
             tall = jnp.concatenate([dscores[w], blank], axis=0)
             dq.append(blend(qkv[D : 2 * D, w * LANES : (w + 1) * LANES], tall) * SCALE)
-            dk.append(gather_pairs(spread.at[0, w], tall) * SCALE)
+            dk.append(gather_pairs(spread.at[0, w % RING], tall) * SCALE)
             tall = jnp.concatenate([prob_ref[w], blank], axis=0)
-            dv.append(gather_pairs(spread.at[1, w], tall))
+            dv.append(gather_pairs(spread.at[1, w % RING], tall))
     dqkv = jnp.concatenate([jnp.concatenate(d, axis=1) for d in (dq, dk, dv)], axis=0).astype(BF16)
-    dqkv_s[:, cols] = dqkv
 
     def add(w, _):
         band = band_of(band_ref, step * per_step + w, me_ref, space, pl.num_programs(0))
@@ -901,9 +903,10 @@
 
     lax.fori_loop(0, per_step, add, 0)
     unit, scale = norm_parts(shifted_ref[...].astype(F32))
-    normed_s[:, cols] = (unit * vec[:, 0:1] + vec[:, 1:2]).astype(BF16)
+    grad_qkv[...] += mt((unit * vec[:, 0:1] + vec[:, 1:2]).astype(BF16), dqkv)
     dnormed = mm(weights_ref[:, : 3 * D], dqkv)
-    out_ref[...] = norm_back(dnormed, unit, scale, vec[:, 0:1]).astype(BF16)
+    dshifted = norm_back(dnormed, unit, scale, vec[:, 0:1])
+    out_ref[...] = (join_windows(dshifted) if fused else dshifted).astype(BF16)
     for k, value in enumerate((dnormed * unit, dnormed, grad.astype(F32))):
         sums[k] += lane_fold(value)
 
@@ -913,12 +916,13 @@
         wide[WIDE + BIAS_ROWS :, :] = jnp.zeros((wide.shape[0] - WIDE - BIAS_ROWS, LANES), F32)
 
         def turn(k, _):
-            for h in range(HEADS):
-                spot = pl.multiple_of(WIDE + (k * HEADS + h) * WIN, 8)
-                wide[pl.ds(spot, WIN), :KEYS] = total[k, h].T[:WIN]
+            for j in range(2):
+                for h in range(HEADS):
+                    spot = pl.multiple_of(WIDE + ((2 * k + j) * HEADS + h) * WIN, 8)
+                    wide[pl.ds(spot, WIN), :KEYS] = total[2 * k + j, h].T[:WIN]
             return 0
 
-        lax.fori_loop(0, LAT_BANDS, turn, 0)
+        lax.fori_loop(0, LAT_BANDS // 2, turn, 0)
         dense[:COL_LO, :] = jnp.zeros((COL_LO, LANES), F32)
         write_bias(wide, dense, 0)
         covered = BIAS_ROW + DENSE * PERIODS
@@ -929,9 +933,9 @@
         start = rows * LANES + lane < OFFSET["earth_bias"]
         dense[COL_LO : COL_HI - 16, :] = column_ref[: COL_HI - COL_LO - 16, :]
         dense[COL_HI - 16 : COL_HI, :] = jnp.where(start, both, dense[COL_HI - 16 : COL_HI, :])
-        split_into(mat, mt(normed_s[...], dqkv_s[...]))
+        split_into(mat, grad_qkv[...])
         write_matrix(dense, 0, "qkv1", mat)
-        split_into(mat, mt(mixed_s[...], grad_s[...]))
+        split_into(mat, grad_proj[...])
         write_matrix(dense, 0, "proj1", mat)
         for k, name in enumerate(("norm1_gain", "norm1_shift", "proj1_bias")):
             write_vector(dense, 0, name, sums[k])
@@ -959,7 +963,8 @@
     slot_block = lambda r: pl.BlockSpec((r, SLOT_BLOCK), lambda i, *_: (0, i))
     ins = [(me, None), (bands, None)]
     if fused:
-        ins += [(slots, slot_block(1)), (grad, whole_block(grad.shape))]
+        tight = pl.BlockSpec((1, TIGHT_BLOCK), lambda i, *_: (0, i))
+        ins += [(slots, tight), (grad, whole_block(grad.shape))]
     else:
         ins += [(grad, slot_block(D))]
     ins += [
@@ -975,8 +980,13 @@
         ),
     ]
     flat_rows = max(shards * rows, BIAS_ROW + DENSE * PERIODS + 8)
+    if fused:
+        tight = pl.BlockSpec((D, TIGHT_BLOCK), lambda i, *_: (0, i))
+        first = ((D, n // LANES * WIN), BF16, tight)
+    else:
+        first = ((D, n), BF16, slot_block(D))
     outs = [
-        ((D, n), BF16, slot_block(D)),
+        first,
         ((shards // 2, padded, LANES), BF16, pl.BlockSpec(memory_space=pl.ANY)),
         ((shards // 2, padded, LANES), BF16, pl.BlockSpec(memory_space=pl.ANY)),
     ]
@@ -987,18 +997,16 @@
         pltpu.VMEM((flat_rows, LANES), F32),
         pltpu.VMEM((5, D, LANES), F32),
         pltpu.VMEM((shards, padded, LANES), BF16),
-        pltpu.VMEM((2, per_step, D, HEADS * LANES), BF16),
-        pltpu.VMEM((D, n), BF16),
-        pltpu.VMEM((3 * D, n), BF16),
-        pltpu.VMEM((D, n), BF16),
-        pltpu.VMEM((D, n), BF16),
+        pltpu.VMEM((2, RING, D, HEADS * LANES), BF16),
+        pltpu.VMEM((D, 3 * D), F32),
+        pltpu.VMEM((D, D), F32),
         pltpu.VMEM((3, D, LANES), F32),
         pltpu.SemaphoreType.DMA((2,)),
     ]
     kernel = functools.partial(
         window_backward_kernel, order=order, shard_rows=rows, space=space
     )
-    return call(kernel, (n // SLOT_BLOCK,), ins, outs, scratch, "window_backward", 24 * D * D * n, scalars=2)
+    return call(kernel, (n // SLOT_BLOCK,), ins, outs, scratch, "window_backward", 24 * D * D * n, 48, scalars=2)
 
 
 def finish_kernel(shift_ref, slots_ref, after_ref, out_ref):
@@ -1021,6 +1029,7 @@
         [],
         "finish",
         D * n * slots.shape[1],
+        24,
     )[0]
 
 
@@ -1066,9 +1075,7 @@
     flat_in = block_input[0].reshape(rows_dev, model_width)
     routes = send_rows[0, :, 0, :]
     route_flat = routes.reshape(-1)
-    slots = jnp.pad(
-        routes.reshape(-1, WIN), ((0, 0), (0, LANES - WIN)), constant_values=-1
-    ).reshape(1, -1)
+    slots = routes.reshape(1, -1)
     if fused:
         bands = jnp.zeros((1, LANES), jnp.int32)
     else:

time: 148 us -> 134 us (0.905)
  Pallas kernels: 97.3 us -> 77.9 us
  waiting for transfers between devices: 22.6 us -> 26.4 us
  local copies, waits for them, and re-layouts: 2.57 us -> 4.43 us
    pallas_call x5, Pallas kernels: 97.3 us -> 77.9 us  [call(): pl.pallas_call(kernel, grid_spec=spec, out_shape=[jax.ShapeDtypeStruct(sh...]
    ppermute x19, waiting for transfers between devices: 22.6 us -> 26.4 us  [swap(): lax.ppermute(value, ('dp', 'space'), [(k, k ^ flip) for k in range(device...]
    unnamed x20 -> x16, local copies, waits for them, and re-layouts: 0.19 us -> 3.77 us
  transfers between devices with their start and end apart: 19 -> 19, of which waited for: 13 -> 18; matrix products, arithmetic and copies ran while one was open for 1% -> 0% of each run, Pallas kernels for 11% -> 6%
where the time goes in v5:
time: 134 us
  Pallas kernels  77.9 us (58%)
  waiting for transfers between devices  26.4 us (20%)
  starting transfers between devices  21 us (16%)
  local copies, waits for them, and re-layouts  4.43 us (3%)
  other arithmetic  3.15 us (2%)
    pallas_call x5, Pallas kernels, call(): pl.pallas_call(kernel, grid_spec=spec, out_shape=[jax.ShapeDtypeStruct(sh...  77.9 us
    ppermute x19, waiting for transfers between devices, swap(): lax.ppermute(value, ('dp', 'space'), [(k, k ^ flip) for k in range(device...  26.4 us
    ppermute x19, starting transfers between devices, swap(): lax.ppermute(value, ('dp', 'space'), [(k, k ^ flip) for k in range(device...  21 us
    unnamed x16, local copies, waits for them, and re-layouts  3.77 us
  transfers between devices with their start and end apart: 19, of which 18 were waited for; matrix products, arithmetic and copies ran while one was open for 0% of the time, Pallas kernels for 6%

profile of v5, /device:TPU:0, one launch (start us, length us, event | category | flops | bytes accessed | tf_op | source)
XLA Modules:
  0.0 133.6 jit_solution(3455881647758076284)
XLA Ops:
  2.5 5.1 %collective-permute-start.2 = (bf16[1,304,128]{2,1,0:T(8,128)(2,1)S(1)}, bf16[1,304,128]{2,1,0:T(8,128)(2,1)S(1)}, u32[]{:S(2)}, u32[]{:S(2)}) collective-permute-start(bf16[1,304,128]{2,1,0:T(8,128)(2,1)S(1)} %maximum_bitcast_fusion), channel_id=1, source_target_pairs={{0,6},{1,7},{2,4},{3,5},{4,2},{5,3},{6,0},{7,1},{8,14},{9,15},{10,... | collective-permute-start | bytes 233480 | tf_op jit(solution)/shard_map/ppermute | solution.py:1056
  8.3 2.2 %collective-permute-done.2 = bf16[1,304,128]{2,1,0:T(8,128)(2,1)S(1)} collective-permute-done((bf16[1,304,128]{2,1,0:T(8,128)(2,1)S(1)}, bf16[1,304,128]{2,1,0:T(8,128)(2,1)S(1)}, u32[]{:S(2)}, u32[]{:S(2)}) %collective-permute-start.2) | collective-permute-done | bytes 77856 | tf_op jit(solution)/shard_map/ppermute | solution.py:1056
  10.5 3.7 %collective-permute-done.1 = bf16[1,304,128]{2,1,0:T(8,128)(2,1)S(1)} collective-permute-done((bf16[1,304,128]{2,1,0:T(8,128)(2,1)S(1)}, bf16[1,304,128]{2,1,0:T(8,128)(2,1)S(1)}, u32[]{:S(2)}, u32[]{:S(2)}) %collective-permute-start.1) | collective-permute-done | bytes 77856 | tf_op jit(solution)/shard_map/ppermute | solution.py:1056
  14.3 1.6 %collective-permute-start.4 = (bf16[4,152,128]{2,1,0:T(8,128)(2,1)S(1)}, bf16[4,152,128]{2,1,0:T(8,128)(2,1)S(1)}, u32[]{:S(2)}, u32[]{:S(2)}) collective-permute-start(bf16[4,152,128]{2,1,0:T(8,128)(2,1)S(1)} %get-tuple-element.62), channel_id=1, source_target_pairs={{0,16},{1,17},{2,18},{3,19},{4,20},{5,21},{6,22},{7,23},{8,24},{9,... | collective-permute-start | bytes 466952 | tf_op jit(solution)/shard_map/ppermute | solution.py:1056
  15.8 1.5 %collective-permute-start.3 = (bf16[4,152,128]{2,1,0:T(8,128)(2,1)S(1)}, bf16[4,152,128]{2,1,0:T(8,128)(2,1)S(1)}, u32[]{:S(2)}, u32[]{:S(2)}) collective-permute-start(bf16[4,152,128]{2,1,0:T(8,128)(2,1)S(1)} %get-tuple-element.63), channel_id=1, source_target_pairs={{0,8},{1,9},{2,10},{3,11},{4,12},{5,13},{6,14},{7,15},{8,0},{9,1},... | collective-permute-start | bytes 466952 | tf_op jit(solution)/shard_map/ppermute | solution.py:1056
  17.5 2.2 %collective-permute-done.4 = bf16[4,152,128]{2,1,0:T(8,128)(2,1)S(1)} collective-permute-done((bf16[4,152,128]{2,1,0:T(8,128)(2,1)S(1)}, bf16[4,152,128]{2,1,0:T(8,128)(2,1)S(1)}, u32[]{:S(2)}, u32[]{:S(2)}) %collective-permute-start.4) | collective-permute-done | bytes 155680 | tf_op jit(solution)/shard_map/ppermute | solution.py:1056
  19.7 1.4 %collective-permute-done.3 = bf16[4,152,128]{2,1,0:T(8,128)(2,1)S(1)} collective-permute-done((bf16[4,152,128]{2,1,0:T(8,128)(2,1)S(1)}, bf16[4,152,128]{2,1,0:T(8,128)(2,1)S(1)}, u32[]{:S(2)}, u32[]{:S(2)}) %collective-permute-start.3) | collective-permute-done | bytes 155680 | tf_op jit(solution)/shard_map/ppermute | solution.py:1056
  21.7 1.5 %collective-permute-start.6 = (bf16[8,152,128]{2,1,0:T(8,128)(2,1)S(1)}, bf16[8,152,128]{2,1,0:T(8,128)(2,1)S(1)}, u32[]{:S(2)}, u32[]{:S(2)}) collective-permute-start(bf16[8,152,128]{2,1,0:T(8,128)(2,1)S(1)} %pad_maximum_fusion.3.refs_2_), channel_id=1, source_target_pairs={{0,8},{1,9},{2,10},{3,11},{4,12},{5,13},{6,14},{7,15},{8,0},{9,1},... | collective-permute-start | bytes 933896 | tf_op jit(solution)/shard_map/ppermute | solution.py:1056
  23.2 3.3 %shift.1.refs_8_.refs_5_ = bf16[192,4096]{1,0:T(8,128)(2,1)S(1)} custom-call(bf16[2304,192]{1,0:T(8,128)(2,1)S(1)} %bitcast.34, s32[1,2304]{1,0:T(1,128)S(1)} %reshape_squeeze.9.slots_ref.refs_9_.refs_0_), custom_call_target="tpu_custom_call" | custom-call | flops 3623878656 | bytes 2466816 | tf_op jit(solution)/shard_map/shift/pallas_call | solution.py:318
  32.2 1.4 %copy-done.3 = bf16[192,4096]{1,0:T(8,128)(2,1)S(1)} copy-done((bf16[192,4096]{1,0:T(8,128)(2,1)S(1)}, bf16[192,4096]{1,0:T(8,128)(2,1)}, u32[]{:S(2)}) %copy-start.3) | copy-done | bytes 1572888
  33.6 20.7 %window_forward.1 = (f32[192,2304]{1,0:T(8,128)S(1)}, bf16[576,4096]{1,0:T(8,128)(2,1)}, bf16[192,4096]{1,0:T(8,128)(2,1)S(1)}, bf16[32,80,768]{2,1,0:T(8,128)(2...) custom-call(s32[1]{0:T(128)} %bitcast.me_ref, ...), custom_call_target="tpu_custom_call" | custom-call | flops 3623878656 | bytes 19133956 | tf_op jit(solution)/shard_map/window_forward/pallas_call | solution.py:318
  54.3 22.3 %column.1 = (bf16[2304,192]{1,0:T(8,128)(2,1)}, f32[192,2304]{1,0:T(8,128)S(1)}, bf16[192,2304]{1,0:T(8,128)(2,1)S(1)}, f32[3488,128]{1,0:T(8,128)S(1)}) custom-call(f32[3488,128]{1,0:T(8,128)S(1)} %get-tuple-element.39.dense, f32[192,2304]{1,0:T(8,128)S(1)} %get-tuple-element.40.x_ref, bf16[2304,192]{1,0:T(8,128)(2,1)S(1)} %bitcast.36, ...), custom_call_target="tpu_custom_call" | custom-call | flops 6794772480 | bytes 9774080 | tf_op jit(solution)/shard_map/column/pallas_call | solution.py:318
  77.9 26.2 %window_backward.1 = (bf16[192,2304]{1,0:T(8,128)(2,1)S(1)}, bf16[16,304,128]{2,1,0:T(8,128)(2,1)S(1)}, bf16[16,304,128]{2,1,0:T(8,128)(2,1)S(1)}) custom-call(s32[1]{0:T(128)} %bitcast.me_ref, s32[8,128]{1,0:T(8,128)S(1)} %get-tuple-element.42.band_ref, s32[1,2304]{1,0:T(1,128)S(1)} %reshape_squeeze.9.slots_ref.refs_9_.refs_0_, ...), custom_call_target="tpu_custom_call" | custom-call | flops 7247757312 | bytes 18248708 | tf_op jit(solution)/shard_map/window_backward/pallas_call | solution.py:318
  104.3 2.8 %collective-permute-done.11 = bf16[16,304,128]{2,1,0:T(8,128)(2,1)S(1)} collective-permute-done((bf16[16,304,128]{2,1,0:T(8,128)(2,1)S(1)}, bf16[16,304,128]{2,1,0:T(8,128)(2,1)S(1)}, u32[]{:S(2)}, u32[]{:S(2)}) %collective-permute-start.11) | collective-permute-done | bytes 1245216 | tf_op jit(solution)/shard_map/ppermute | solution.py:1056
  107.5 1.6 %collective-permute-start.12 = (bf16[8,152,128]{2,1,0:T(8,128)(2,1)S(1)}, bf16[8,152,128]{2,1,0:T(8,128)(2,1)S(1)}, u32[]{:S(2)}, u32[]{:S(2)}) collective-permute-start(bf16[8,152,128]{2,1,0:T(8,128)(2,1)S(1)} %slice.119), channel_id=1, source_target_pairs={{0,16},{1,17},{2,18},{3,19},{4,20},{5,21},{6,22},{7,23},{8,24},{9,... | collective-permute-start | bytes 933896 | tf_op jit(solution)/shard_map/ppermute | solution.py:1056
  109.2 1.5 %collective-permute-start.13 = (bf16[2,4,152,128]{3,2,1,0:T(8,128)(2,1)S(1)}, bf16[2,4,152,128]{3,2,1,0:T(8,128)(2,1)S(1)}, u32[]{:S(2)}, u32[]{:S(2)}) collective-permute-start(bf16[2,4,152,128]{3,2,1,0:T(8,128)(2,1)S(1)} %fusion.2), channel_id=1, source_target_pairs={{0,8},{1,9},{2,10},{3,11},{4,12},{5,13},{6,14},{7,15},{8,0},{9,1},... | collective-permute-start | bytes 933896 | tf_op jit(solution)/shard_map/ppermute | solution.py:1056
  110.7 5.4 %finish.1 = f32[2304,192]{1,0:T(8,128)} custom-call(bf16[192,2304]{1,0:T(8,128)(2,1)S(1)} %get-tuple-element.54.shift_ref, s32[1,2304]{1,0:T(1,128)S(1)} %reshape_squeeze.9.slots_ref.refs_9_.refs_0_, f32[192,2304]{1,0:T(8,128)S(1)} %get-tuple-element.55.after_ref), custom_call_target="tpu_custom_call" | custom-call | flops 2038431744 | bytes 4432896 | tf_op jit(solution)/shard_map/finish/pallas_call | solution.py:318
  117.1 1.3 collective-permute-done.13
  119.0 1.6 %collective-permute-start.14 = (bf16[4,152,128]{2,1,0:T(8,128)(2,1)S(1)}, bf16[4,152,128]{2,1,0:T(8,128)(2,1)S(1)}, u32[]{:S(2)}, u32[]{:S(2)}) collective-permute-start(bf16[4,152,128]{2,1,0:T(8,128)(2,1)S(1)} %slice.120), channel_id=1, source_target_pairs={{0,8},{1,9},{2,10},{3,11},{4,12},{5,13},{6,14},{7,15},{8,0},{9,1},... | collective-permute-start | bytes 466952 | tf_op jit(solution)/shard_map/ppermute | solution.py:1056
  120.6 3.1 %collective-permute-done.15 = bf16[4,152,128]{2,1,0:T(8,128)(2,1)S(1)} collective-permute-done((bf16[4,152,128]{2,1,0:T(8,128)(2,1)S(1)}, bf16[4,152,128]{2,1,0:T(8,128)(2,1)S(1)}, u32[]{:S(2)}, u32[]{:S(2)}) %collective-permute-start.15) | collective-permute-done | bytes 155680 | tf_op jit(solution)/shard_map/ppermute | solution.py:1056
  124.9 1.8 %collective-permute-start.18 = (bf16[304,128]{1,0:T(8,128)(2,1)S(1)}, bf16[304,128]{1,0:T(8,128)(2,1)S(1)}, u32[]{:S(2)}, u32[]{:S(2)}) collective-permute-start(bf16[304,128]{1,0:T(8,128)(2,1)S(1)} %get-tuple-element.60), channel_id=1, source_target_pairs={{0,6},{1,7},{2,4},{3,5},{4,2},{5,3},{6,0},{7,1},{8,14},{9,15},{10,... | collective-permute-start | bytes 233480 | tf_op jit(solution)/shard_map/ppermute | solution.py:1056
  128.0 1.6 %collective-permute-done.16 = bf16[304,128]{1,0:T(8,128)(2,1)S(1)} collective-permute-done((bf16[304,128]{1,0:T(8,128)(2,1)S(1)}, bf16[304,128]{1,0:T(8,128)(2,1)S(1)}, u32[]{:S(2)}, u32[]{:S(2)}) %collective-permute-start.16) | collective-permute-done | bytes 77856 | tf_op jit(solution)/shard_map/ppermute | solution.py:1056
  129.6 1.7 %collective-permute-done.18 = bf16[304,128]{1,0:T(8,128)(2,1)S(1)} collective-permute-done((bf16[304,128]{1,0:T(8,128)(2,1)S(1)}, bf16[304,128]{1,0:T(8,128)(2,1)S(1)}, u32[]{:S(2)}, u32[]{:S(2)}) %collective-permute-start.18) | collective-permute-done | bytes 77856 | tf_op jit(solution)/shard_map/ppermute | solution.py:1056
  131.2 1.7 %collective-permute-done.17 = bf16[304,128]{1,0:T(8,128)(2,1)S(1)} collective-permute-done((bf16[304,128]{1,0:T(8,128)(2,1)S(1)}, bf16[304,128]{1,0:T(8,128)(2,1)S(1)}, u32[]{:S(2)}, u32[]{:S(2)}) %collective-permute-start.17) | collective-permute-done | bytes 77856 | tf_op jit(solution)/shard_map/ppermute | solution.py:1056
  (65 shorter events, 15.7 us)
Async XLA Ops:
  0.6 16.7 %copy-start.6 = (s32[1,8,1,288]{3,2,1,0:T(1,128)S(1)}, s32[1,8,1,288]{3,2,1,0:T(1,128)}, u32[]{:S(2)}) copy-start(s32[1,8,1,288]{3,2,1,0:T(1,128)} %param.9) | copy-start | bytes 27652
  0.6 22.5 %copy-start = (bf16[1,288,8,192]{3,2,1,0:T(8,128)(2,1)S(1)}, bf16[1,288,8,192]{3,2,1,0:T(8,128)(2,1)}, u32[]{:S(2)}) copy-start(bf16[1,288,8,192]{3,2,1,0:T(8,128)(2,1)} %param.6) | copy-start | bytes 2654212
  2.5 8.0 %collective-permute-start.2 = (bf16[1,304,128]{2,1,0:T(8,128)(2,1)S(1)}, bf16[1,304,128]{2,1,0:T(8,128)(2,1)S(1)}, u32[]{:S(2)}, u32[]{:S(2)}) collective-permute-start(bf16[1,304,128]{2,1,0:T(8,128)(2,1)S(1)} %maximum_bitcast_fusion), channel_id=1, source_target_pairs={{0,6},{1,7},{2,4},{3,5},{4,2},{5,3},{6,0},{7,1},{8,14},{9,15},{10,... | collective-permute-start | bytes 233480 | tf_op jit(solution)/shard_map/ppermute | solution.py:1056
  7.7 6.5 %collective-permute-start.1 = (bf16[1,304,128]{2,1,0:T(8,128)(2,1)S(1)}, bf16[1,304,128]{2,1,0:T(8,128)(2,1)S(1)}, u32[]{:S(2)}, u32[]{:S(2)}) collective-permute-start(bf16[1,304,128]{2,1,0:T(8,128)(2,1)S(1)} %maximum_bitcast_fusion), channel_id=1, source_target_pairs={{0,4},{1,5},{2,6},{3,7},{4,0},{5,1},{6,2},{7,3},{8,12},{9,13},{10,... | collective-permute-start | bytes 233480 | tf_op jit(solution)/shard_map/ppermute | solution.py:1056
  7.7 6.5 %collective-permute-start = (bf16[1,304,128]{2,1,0:T(8,128)(2,1)S(1)}, bf16[1,304,128]{2,1,0:T(8,128)(2,1)S(1)}, u32[]{:S(2)}, u32[]{:S(2)}) collective-permute-start(bf16[1,304,128]{2,1,0:T(8,128)(2,1)S(1)} %maximum_bitcast_fusion), channel_id=1, source_target_pairs={{0,2},{1,3},{2,0},{3,1},{4,6},{5,7},{6,4},{7,5},{8,10},{9,11},{10,... | collective-permute-start | bytes 233480 | tf_op jit(solution)/shard_map/ppermute | solution.py:1056
  14.3 5.4 %collective-permute-start.4 = (bf16[4,152,128]{2,1,0:T(8,128)(2,1)S(1)}, bf16[4,152,128]{2,1,0:T(8,128)(2,1)S(1)}, u32[]{:S(2)}, u32[]{:S(2)}) collective-permute-start(bf16[4,152,128]{2,1,0:T(8,128)(2,1)S(1)} %get-tuple-element.62), channel_id=1, source_target_pairs={{0,16},{1,17},{2,18},{3,19},{4,20},{5,21},{6,22},{7,23},{8,24},{9,... | collective-permute-start | bytes 466952 | tf_op jit(solution)/shard_map/ppermute | solution.py:1056
  15.8 5.2 %collective-permute-start.3 = (bf16[4,152,128]{2,1,0:T(8,128)(2,1)S(1)}, bf16[4,152,128]{2,1,0:T(8,128)(2,1)S(1)}, u32[]{:S(2)}, u32[]{:S(2)}) collective-permute-start(bf16[4,152,128]{2,1,0:T(8,128)(2,1)S(1)} %get-tuple-element.63), channel_id=1, source_target_pairs={{0,8},{1,9},{2,10},{3,11},{4,12},{5,13},{6,14},{7,15},{8,0},{9,1},... | collective-permute-start | bytes 466952 | tf_op jit(solution)/shard_map/ppermute | solution.py:1056
  21.1 7.8 %collective-permute-start.5 = (bf16[8,152,128]{2,1,0:T(8,128)(2,1)S(1)}, bf16[8,152,128]{2,1,0:T(8,128)(2,1)S(1)}, u32[]{:S(2)}, u32[]{:S(2)}) collective-permute-start(bf16[8,152,128]{2,1,0:T(8,128)(2,1)S(1)} %pad_maximum_fusion.2.refs_0_), channel_id=1, source_target_pairs={{0,16},{1,17},{2,18},{3,19},{4,20},{5,21},{6,22},{7,23},{8,24},{9,... | collective-permute-start | bytes 933896 | tf_op jit(solution)/shard_map/ppermute | solution.py:1056
  21.7 7.4 %collective-permute-start.6 = (bf16[8,152,128]{2,1,0:T(8,128)(2,1)S(1)}, bf16[8,152,128]{2,1,0:T(8,128)(2,1)S(1)}, u32[]{:S(2)}, u32[]{:S(2)}) collective-permute-start(bf16[8,152,128]{2,1,0:T(8,128)(2,1)S(1)} %pad_maximum_fusion.3.refs_2_), channel_id=1, source_target_pairs={{0,8},{1,9},{2,10},{3,11},{4,12},{5,13},{6,14},{7,15},{8,0},{9,1},... | collective-permute-start | bytes 933896 | tf_op jit(solution)/shard_map/ppermute | solution.py:1056
  23.2 7.0 %copy-start.7 = (s32[1,288]{1,0:T(1,128)S(1)}, s32[1,288]{1,0:T(1,128)}, u32[]{:S(2)}) copy-start(s32[1,288]{1,0:T(1,128)} %param.11) | copy-start | bytes 3460
  29.1 1.6 %collective-permute-start.7 = (bf16[8,152,128]{2,1,0:T(8,128)(2,1)S(1)}, bf16[8,152,128]{2,1,0:T(8,128)(2,1)S(1)}, u32[]{:S(2)}, u32[]{:S(2)}) collective-permute-start(bf16[8,152,128]{2,1,0:T(8,128)(2,1)S(1)} %pad_maximum_fusion.2.refs_0_), channel_id=1, source_target_pairs={{0,1},{1,0},{2,3},{3,2},{4,5},{5,4},{6,7},{7,6},{8,9},{9,8},{10,11... | collective-permute-start | bytes 933896 | tf_op jit(solution)/shard_map/ppermute | solution.py:1056
  29.1 2.0 %collective-permute-start.8 = (bf16[8,152,128]{2,1,0:T(8,128)(2,1)S(1)}, bf16[8,152,128]{2,1,0:T(8,128)(2,1)S(1)}, u32[]{:S(2)}, u32[]{:S(2)}) collective-permute-start(bf16[8,152,128]{2,1,0:T(8,128)(2,1)S(1)} %collective-permute-done.5.refs_1_), channel_id=1, source_target_pairs={{0,1},{1,0},{2,3},{3,2},{4,5},{5,4},{6,7},{7,6},{8,9},{9,8},{10,11... | collective-permute-start | bytes 933896 | tf_op jit(solution)/shard_map/ppermute | solution.py:1056
  29.6 2.4 %collective-permute-start.9 = (bf16[8,152,128]{2,1,0:T(8,128)(2,1)S(1)}, bf16[8,152,128]{2,1,0:T(8,128)(2,1)S(1)}, u32[]{:S(2)}, u32[]{:S(2)}) collective-permute-start(bf16[8,152,128]{2,1,0:T(8,128)(2,1)S(1)} %pad_maximum_fusion.3.refs_2_), channel_id=1, source_target_pairs={{0,1},{1,0},{2,3},{3,2},{4,5},{5,4},{6,7},{7,6},{8,9},{9,8},{10,11... | collective-permute-start | bytes 933896 | tf_op jit(solution)/shard_map/ppermute | solution.py:1056
  29.6 2.6 %collective-permute-start.10 = (bf16[8,152,128]{2,1,0:T(8,128)(2,1)S(1)}, bf16[8,152,128]{2,1,0:T(8,128)(2,1)}, u32[]{:S(2)}, u32[]{:S(2)}) collective-permute-start(bf16[8,152,128]{2,1,0:T(8,128)(2,1)S(1)} %collective-permute-done.6.refs_3_), channel_id=1, source_target_pairs={{0,1},{1,0},{2,3},{3,2},{4,5},{5,4},{6,7},{7,6},{8,9},{9,8},{10,11... | collective-permute-start | bytes 933896 | tf_op jit(solution)/shard_map/ppermute | solution.py:1056
  33.6 20.7 %copy-start.1 = (bf16[1,288,8,192]{3,2,1,0:T(8,128)(2,1)S(1)}, bf16[1,288,8,192]{3,2,1,0:T(8,128)(2,1)}, u32[]{:S(2)}) copy-start(bf16[1,288,8,192]{3,2,1,0:T(8,128)(2,1)} %param.7) | copy-start | bytes 2654212
  54.3 22.4 %copy-start.4 = (bf16[192,4096]{1,0:T(8,128)(2,1)}, bf16[192,4096]{1,0:T(8,128)(2,1)S(1)}, u32[]{:S(2)}) copy-start(bf16[192,4096]{1,0:T(8,128)(2,1)S(1)} %get-tuple-element.48.refs_7_) | copy-start | bytes 4718596
  104.1 3.0 %collective-permute-start.11 = (bf16[16,304,128]{2,1,0:T(8,128)(2,1)S(1)}, bf16[16,304,128]{2,1,0:T(8,128)(2,1)S(1)}, u32[]{:S(2)}, u32[]{:S(2)}) collective-permute-start(bf16[16,304,128]{2,1,0:T(8,128)(2,1)S(1)} %get-tuple-element.51), channel_id=1, source_target_pairs={{0,1},{1,0},{2,3},{3,2},{4,5},{5,4},{6,7},{7,6},{8,9},{9,8},{10,11... | collective-permute-start | bytes 3735560 | tf_op jit(solution)/shard_map/ppermute | solution.py:1056
  107.5 9.5 %collective-permute-start.12 = (bf16[8,152,128]{2,1,0:T(8,128)(2,1)S(1)}, bf16[8,152,128]{2,1,0:T(8,128)(2,1)S(1)}, u32[]{:S(2)}, u32[]{:S(2)}) collective-permute-start(bf16[8,152,128]{2,1,0:T(8,128)(2,1)S(1)} %slice.119), channel_id=1, source_target_pairs={{0,16},{1,17},{2,18},{3,19},{4,20},{5,21},{6,22},{7,23},{8,24},{9,... | collective-permute-start | bytes 933896 | tf_op jit(solution)/shard_map/ppermute | solution.py:1056
  109.2 9.2 %collective-permute-start.13 = (bf16[2,4,152,128]{3,2,1,0:T(8,128)(2,1)S(1)}, bf16[2,4,152,128]{3,2,1,0:T(8,128)(2,1)S(1)}, u32[]{:S(2)}, u32[]{:S(2)}) collective-permute-start(bf16[2,4,152,128]{3,2,1,0:T(8,128)(2,1)S(1)} %fusion.2), channel_id=1, source_target_pairs={{0,8},{1,9},{2,10},{3,11},{4,12},{5,13},{6,14},{7,15},{8,0},{9,1},... | collective-permute-start | bytes 933896 | tf_op jit(solution)/shard_map/ppermute | solution.py:1056
  118.5 5.3 %collective-permute-start.15 = (bf16[4,152,128]{2,1,0:T(8,128)(2,1)S(1)}, bf16[4,152,128]{2,1,0:T(8,128)(2,1)S(1)}, u32[]{:S(2)}, u32[]{:S(2)}) collective-permute-start(bf16[4,152,128]{2,1,0:T(8,128)(2,1)S(1)} %fusion.3), channel_id=1, source_target_pairs={{0,16},{1,17},{2,18},{3,19},{4,20},{5,21},{6,22},{7,23},{8,24},{9,... | collective-permute-start | bytes 466952 | tf_op jit(solution)/shard_map/ppermute | solution.py:1056
  119.0 5.3 %collective-permute-start.14 = (bf16[4,152,128]{2,1,0:T(8,128)(2,1)S(1)}, bf16[4,152,128]{2,1,0:T(8,128)(2,1)S(1)}, u32[]{:S(2)}, u32[]{:S(2)}) collective-permute-start(bf16[4,152,128]{2,1,0:T(8,128)(2,1)S(1)} %slice.120), channel_id=1, source_target_pairs={{0,8},{1,9},{2,10},{3,11},{4,12},{5,13},{6,14},{7,15},{8,0},{9,1},... | collective-permute-start | bytes 466952 | tf_op jit(solution)/shard_map/ppermute | solution.py:1056
  124.4 5.1 %collective-permute-start.16 = (bf16[304,128]{1,0:T(8,128)(2,1)S(1)}, bf16[304,128]{1,0:T(8,128)(2,1)S(1)}, u32[]{:S(2)}, u32[]{:S(2)}) collective-permute-start(bf16[304,128]{1,0:T(8,128)(2,1)S(1)} %get-tuple-element.59), channel_id=1, source_target_pairs={{0,2},{1,3},{2,0},{3,1},{4,6},{5,7},{6,4},{7,5},{8,10},{9,11},{10,... | collective-permute-start | bytes 233480 | tf_op jit(solution)/shard_map/ppermute | solution.py:1056
  124.9 6.3 %collective-permute-start.18 = (bf16[304,128]{1,0:T(8,128)(2,1)S(1)}, bf16[304,128]{1,0:T(8,128)(2,1)S(1)}, u32[]{:S(2)}, u32[]{:S(2)}) collective-permute-start(bf16[304,128]{1,0:T(8,128)(2,1)S(1)} %get-tuple-element.60), channel_id=1, source_target_pairs={{0,6},{1,7},{2,4},{3,5},{4,2},{5,3},{6,0},{7,1},{8,14},{9,15},{10,... | collective-permute-start | bytes 233480 | tf_op jit(solution)/shard_map/ppermute | solution.py:1056
  126.8 6.2 %collective-permute-start.17 = (bf16[304,128]{1,0:T(8,128)(2,1)S(1)}, bf16[304,128]{1,0:T(8,128)(2,1)S(1)}, u32[]{:S(2)}, u32[]{:S(2)}) collective-permute-start(bf16[304,128]{1,0:T(8,128)(2,1)S(1)} %get-tuple-element.61), channel_id=1, source_target_pairs={{0,4},{1,5},{2,6},{3,7},{4,0},{5,1},{6,2},{7,3},{8,12},{9,13},{10,... | collective-permute-start | bytes 233480 | tf_op jit(solution)/shard_map/ppermute | solution.py:1056
  (3 other events, 3.8 us)

commit v6 on v5

--- a/solution.py
+++ b/solution.py
@@ -63,6 +63,8 @@
 WIDE = LANES // math.gcd(WIN, LANES)
 DENSE = WIN // math.gcd(WIN, LANES)
 PERIODS = -(-(BIAS_ROWS // WIDE + 1) // 8) * 8
+PITCH = PERIODS + 1
+USED = BIAS_ROWS // WIDE
 COL_LO = (OFFSET["norm2_gain"] // LANES) // 8 * 8
 COL_HI = -(-BIAS_ROW // 8) * 8 + 8
 BIAS_LO = BIAS_ROW // 8 * 8
@@ -177,7 +179,12 @@
             value = jnp.where(lane < first, after, value)
         if first:
             value = pltpu.roll(value, LANES - first, 1)
-        wide[pl.ds(j, PERIODS, stride=WIDE), :] = value
+        wide[pl.ds(j * PITCH, PERIODS), :] = value
+
+
+def wide_rows(pair, part, tile):
+    line = part * WIN + tile * 8
+    return pl.ds(line % WIDE * PITCH + WIN * 2 // WIDE * pair + line // WIDE, 8, stride=PITCH)
 
 
 def write_bias(wide, dense, first_row):
@@ -188,7 +195,7 @@
         value = None
         while line * WIN < begin + LANES:
             shift = line * WIN - begin
-            piece = wide[pl.ds(WIDE + line, PERIODS, stride=WIDE), :]
+            piece = wide[pl.ds(line % WIDE * PITCH + line // WIDE, PERIODS), :]
             if shift % LANES:
                 piece = pltpu.roll(piece, shift % LANES, 1)
             value = piece if value is None else jnp.where(lane >= shift, piece, value)
@@ -340,6 +347,12 @@
     return pl.BlockSpec(shape, lambda *_: (0,) * len(shape))
 
 
+def fixed_block(array):
+    return pl.BlockSpec(
+        array.shape, lambda *_: (0,) * array.ndim, pipeline_mode=pl.Buffered(buffer_count=1)
+    )
+
+
 SLOT_BLOCK = 2048
 TIGHT_BLOCK = SLOT_BLOCK // LANES * WIN
 TURNS = 12
@@ -348,12 +361,14 @@
 TOKEN_BLOCK = 768
 
 
-def shift_kernel(x_ref, slots_ref, out_ref, x_t):
+def shift_kernel(x_ref, slots_ref, out_ref, again_ref, x_t):
     @pl.when(pl.program_id(0) == 0)
     def _():
         x_t[...] = x_ref[...].astype(F32).T.astype(BF16)
 
-    out_ref[...] = to_slots(x_t[...], slots_ref[...])
+    result = to_slots(x_t[...], slots_ref[...])
+    out_ref[...] = result
+    again_ref[...] = result
 
 
 def shift_call(tokens, slots):
@@ -362,15 +377,15 @@
         shift_kernel,
         (n // SLOT_BLOCK,),
         [
-            (tokens, whole_block(tokens.shape)),
+            (tokens, fixed_block(tokens)),
             (slots, pl.BlockSpec((1, TIGHT_BLOCK), lambda i: (0, i))),
         ],
-        [((D, n), BF16, pl.BlockSpec((D, SLOT_BLOCK), lambda i: (0, i)))],
+        [((D, n), BF16, pl.BlockSpec((D, SLOT_BLOCK), lambda i: (0, i)))] * 2,
         [pltpu.VMEM((D, count), BF16)],
         "shift",
         D * count * n,
         24,
-    )[0]
+    )
 
 
 def load_dense(me_ref, parts, plan, blocks, dense, sem, order, rows):
@@ -465,12 +480,14 @@
         vec[:, 1:2] = read_vector(dense, 0, "norm1_shift")
         vec[:, 2:3] = read_vector(dense, 0, "proj1_bias")
         read_bias(dense, wide)
-        wide[BIAS_ROWS:, :] = jnp.zeros((wide.shape[0] - BIAS_ROWS, LANES), F32)
+        blank = jnp.zeros((LANES - WIN, LANES), F32)
 
         def turn(k, _):
             for j in range(TURNS):
-                spot = pl.multiple_of((k * TURNS + j) * WIN, 8)
-                bias[k * TURNS + j, :WIN, :] = wide[pl.ds(spot, LANES), :].T[:WIN].astype(BF16)
+                pair, part = k * (TURNS // 2) + j // 2, j % 2
+                tiles = [wide[wide_rows(pair, part, tile), :] for tile in range(WIN // 8)]
+                block = jnp.concatenate(tiles + [blank], axis=0).T
+                bias[k * TURNS + j, :WIN, :] = block[:WIN].astype(BF16)
             return 0
 
         lax.fori_loop(0, LAT_BANDS * HEADS // TURNS, turn, 0)
@@ -542,7 +559,7 @@
         count = tokens.shape[0]
         late = lambda i: jnp.maximum(i - steps, 0)
         ins += [
-            (slots, whole_block(slots.shape)),
+            (slots, fixed_block(slots)),
             (tokens, pl.BlockSpec((TOKEN_BLOCK, D), lambda i, *_: (late(i), 0))),
         ]
         first = ((D, count), F32, pl.BlockSpec((D, TOKEN_BLOCK), lambda i, *_: (0, late(i))))
@@ -569,7 +586,7 @@
     scratch = [
         pltpu.VMEM((shards, padded, LANES), BF16),
         pltpu.VMEM((flat_rows, LANES), F32),
-        pltpu.VMEM((WIDE * PERIODS + LANES, LANES), F32),
+        pltpu.VMEM((WIDE * PITCH, LANES), F32),
         pltpu.VMEM((LAT_BANDS * HEADS, KEYS, LANES), BF16),
         pltpu.VMEM((5, D, LANES), F32),
         pltpu.VMEM((3 * D, D), BF16),
@@ -588,7 +605,7 @@
         steps=steps,
         space=space,
     )
-    return call(kernel, (grid,), ins, outs, scratch, "window_forward", 12 * D * D * n, 40, scalars=2)
+    return call(kernel, (grid,), ins, outs, scratch, "window_forward", 12 * D * D * n, 36, scalars=2)
 
 
 COLUMN_BLOCK = 768
@@ -783,7 +800,7 @@
         column_kernel,
         (n // COLUMN_BLOCK,),
         [
-            (dense, whole_block(dense.shape)),
+            (dense, fixed_block(dense)),
             (after_t, feature(D)),
             (cotangent, token),
             (counts, feature(1)),
@@ -817,7 +834,7 @@
         ],
         "column",
         40 * D * D * n,
-        44,
+        40,
     )
 
 
@@ -838,7 +855,6 @@
         keep_ref,
         send_ref,
         total,
-        kept,
         wide,
         dense,
         mat,
@@ -885,7 +901,10 @@
                     (prob * (dprob - jnp.sum(prob * dprob, axis=0, keepdims=True))).astype(BF16)
                 )
             dscores[w] = jnp.concatenate(heads, axis=1)
-            kept[w] = dscores[w]
+            band = band_of(band_ref, step * per_step + w, me_ref, space, pl.num_programs(0))
+            for h in range(HEADS):
+                spot = pl.ds(pl.multiple_of((band * HEADS + h) * KEYS, 8), KEYS)
+                total[spot, :] += heads[h].astype(F32)
         if turn >= 2:
             w = turn - 2
             tall = jnp.concatenate([dscores[w], blank], axis=0)
@@ -894,14 +913,6 @@
             tall = jnp.concatenate([prob_ref[w], blank], axis=0)
             dv.append(gather_pairs(spread.at[1, w % RING], tall))
     dqkv = jnp.concatenate([jnp.concatenate(d, axis=1) for d in (dq, dk, dv)], axis=0).astype(BF16)
-
-    def add(w, _):
-        band = band_of(band_ref, step * per_step + w, me_ref, space, pl.num_programs(0))
-        for h in range(HEADS):
-            total[band, h] += kept[w, :, head_lanes(h)].astype(F32)
-        return 0
-
-    lax.fori_loop(0, per_step, add, 0)
     unit, scale = norm_parts(shifted_ref[...].astype(F32))
     grad_qkv[...] += mt((unit * vec[:, 0:1] + vec[:, 1:2]).astype(BF16), dqkv)
     dnormed = mm(weights_ref[:, : 3 * D], dqkv)
@@ -912,17 +923,20 @@
 
     @pl.when(step == pl.num_programs(0) - 1)
     def _():
-        wide[:WIDE, :] = jnp.zeros((WIDE, LANES), F32)
-        wide[WIDE + BIAS_ROWS :, :] = jnp.zeros((wide.shape[0] - WIDE - BIAS_ROWS, LANES), F32)
+        for j in range(WIDE):
+            wide[j * PITCH + USED : (j + 1) * PITCH, :] = jnp.zeros((PITCH - USED, LANES), F32)
+        blank = jnp.zeros((WIN, LANES - KEYS), F32)
 
         def turn(k, _):
-            for j in range(2):
-                for h in range(HEADS):
-                    spot = pl.multiple_of(WIDE + ((2 * k + j) * HEADS + h) * WIN, 8)
-                    wide[pl.ds(spot, WIN), :KEYS] = total[2 * k + j, h].T[:WIN]
+            for j in range(TURNS):
+                pair, part = k * (TURNS // 2) + j // 2, j % 2
+                spot = pl.ds(pl.multiple_of((k * TURNS + j) * KEYS, 8), KEYS)
+                block = jnp.concatenate([total[spot, :].T[:WIN], blank], axis=1)
+                for tile in range(WIN // 8):
+                    wide[wide_rows(pair, part, tile), :] = block[tile * 8 : tile * 8 + 8]
             return 0
 
-        lax.fori_loop(0, LAT_BANDS // 2, turn, 0)
+        lax.fori_loop(0, LAT_BANDS * HEADS // TURNS, turn, 0)
         dense[:COL_LO, :] = jnp.zeros((COL_LO, LANES), F32)
         write_bias(wide, dense, 0)
         covered = BIAS_ROW + DENSE * PERIODS
@@ -964,13 +978,13 @@
     ins = [(me, None), (bands, None)]
     if fused:
         tight = pl.BlockSpec((1, TIGHT_BLOCK), lambda i, *_: (0, i))
-        ins += [(slots, tight), (grad, whole_block(grad.shape))]
+        ins += [(slots, tight), (grad, fixed_block(grad))]
     else:
         ins += [(grad, slot_block(D))]
     ins += [
-        (weights, whole_block(weights.shape)),
-        (vec, whole_block(vec.shape)),
-        (column_grad, whole_block(column_grad.shape)),
+        (weights, fixed_block(weights)),
+        (vec, fixed_block(vec)),
+        (column_grad, fixed_block(column_grad)),
         (shifted, slot_block(D)),
         (qkv, slot_block(3 * D)),
         (mixed, slot_block(D)),
@@ -991,9 +1005,8 @@
         ((shards // 2, padded, LANES), BF16, pl.BlockSpec(memory_space=pl.ANY)),
     ]
     scratch = [
-        pltpu.VMEM((LAT_BANDS, HEADS, KEYS, LANES), F32),
-        pltpu.VMEM((per_step, KEYS, HEADS * LANES), BF16),
-        pltpu.VMEM((WIDE * (PERIODS + 2), LANES), F32),
+        pltpu.VMEM((LAT_BANDS * HEADS * KEYS, LANES), F32),
+        pltpu.VMEM((WIDE * PITCH, LANES), F32),
         pltpu.VMEM((flat_rows, LANES), F32),
         pltpu.VMEM((5, D, LANES), F32),
         pltpu.VMEM((shards, padded, LANES), BF16),
@@ -1006,7 +1019,7 @@
     kernel = functools.partial(
         window_backward_kernel, order=order, shard_rows=rows, space=space
     )
-    return call(kernel, (n // SLOT_BLOCK,), ins, outs, scratch, "window_backward", 24 * D * D * n, 48, scalars=2)
+    return call(kernel, (n // SLOT_BLOCK,), ins, outs, scratch, "window_backward", 24 * D * D * n, 44, scalars=2)
 
 
 def finish_kernel(shift_ref, slots_ref, after_ref, out_ref):
@@ -1021,8 +1034,8 @@
         finish_kernel,
         (n // TOKEN_BLOCK,),
         [
-            (grad_shifted, whole_block(grad_shifted.shape)),
-            (slots, whole_block(slots.shape)),
+            (grad_shifted, fixed_block(grad_shifted)),
+            (slots, fixed_block(slots)),
             (after_t, pl.BlockSpec((D, TOKEN_BLOCK), lambda i: (0, i))),
         ],
         [((n, D), F32, pl.BlockSpec((TOKEN_BLOCK, D), lambda i: (i, 0)))],
@@ -1083,19 +1096,14 @@
         bands = lax.dynamic_slice(
             all_bands, ((place % group) * dest, (place // group) * per_dest), (dest, per_dest)
         ).reshape(1, -1)
-        shifted = to_windows(flat_in)
+        shifted = shifted_again = to_windows(flat_in)
 
     shard_rows = params.shape[0] // LANES
     padded = padded_rows(shard_rows)
-    band_row = jnp.pad(window_band[0].astype(BF16), (0, LANES - window_band.shape[1]))
-    held = jnp.concatenate(
-        [
-            params.astype(BF16).reshape(shard_rows, LANES),
-            band_row.reshape(1, LANES),
-            jnp.zeros((padded - shard_rows - 1, LANES), BF16),
-        ],
-        axis=0,
-    ).reshape(1, padded, LANES)
+    band_row = jnp.pad(window_band[0], (0, LANES - window_band.shape[1])).astype(BF16)
+    own_rows = jnp.pad(params.reshape(shard_rows, LANES), ((0, padded - shard_rows), (0, 0)))
+    row_id = lax.broadcasted_iota(jnp.int32, (padded, 1), 0)
+    held = jnp.where(row_id == shard_rows, band_row[None, :], own_rows.astype(BF16))[None]
     near, far = order[-1], order[-2]
     direct = [swap(held, near), swap(held, far), swap(held, near, far)]
     held = jnp.concatenate([held] + direct, axis=0)
@@ -1108,10 +1116,10 @@
     lower = jnp.concatenate([lower, swap(lower, top)], axis=0)
     if fused:
         upper, lower, slots = lax.optimization_barrier((upper, lower, slots))
-        shifted = shift_call(flat_in, slots)
+        shifted, shifted_again = shift_call(flat_in, slots)
     parts = [upper, swap(upper, top), lower, swap(lower, next_top)]
     if fused:
-        parts, shifted = lax.optimization_barrier((parts, shifted))
+        parts, shifted, shifted_again = lax.optimization_barrier((parts, shifted, shifted_again))
     parts = parts + [swap(part, order[0]) for part in parts]
     few = devices // 8
     plan = []
@@ -1141,7 +1149,7 @@
         grad_branch = to_windows(grad_branch.T)
     grad_shifted, keep, send = window_backward_call(
         me, bands, order, devices, shard_rows, slots, grad_branch, weights, vec, column_grad,
-        shifted, qkv, mixed, prob, space
+        shifted_again, qkv, mixed, prob, space
     )
     total = keep.astype(F32) + swap(send, order[0]).astype(F32)
     total, grad_shifted = lax.optimization_barrier((total, grad_shifted))

time: 134 us -> 129 us (0.963)
  Pallas kernels: 77.9 us -> 71.8 us
  local copies, waits for them, and re-layouts: 4.43 us -> 6.24 us
    pallas_call x5, Pallas kernels: 77.9 us -> 71.8 us  [call(): pl.pallas_call(kernel, grid_spec=spec, out_shape=[jax.ShapeDtypeStruct(sh...]
    unnamed x16 -> x18, local copies, waits for them, and re-layouts: 3.77 us -> 5.67 us
  transfers between devices with their start and end apart: 19 -> 19, of which waited for: 18 -> 17; matrix products, arithmetic and copies ran while one was open for 0% -> 0% of each run, Pallas kernels for 6% -> 7%
where the time goes in v6:
time: 129 us; the launch traced here: 128 us
  Pallas kernels  71.8 us (56%)
  waiting for transfers between devices  25.4 us (20%)
  starting transfers between devices  20.9 us (16%)
  local copies, waits for them, and re-layouts  6.24 us (5%)
  other arithmetic  3.12 us (2%)
    pallas_call x5, Pallas kernels, call(): pl.pallas_call(kernel, grid_spec=spec, out_shape=[jax.ShapeDtypeStruct(sh...  71.8 us
    ppermute x19, waiting for transfers between devices, swap(): lax.ppermute(value, ('dp', 'space'), [(k, k ^ flip) for k in range(device...  25.4 us
    ppermute x19, starting transfers between devices, swap(): lax.ppermute(value, ('dp', 'space'), [(k, k ^ flip) for k in range(device...  20.9 us
    unnamed x18, local copies, waits for them, and re-layouts  5.67 us
  transfers between devices with their start and end apart: 19, of which 17 were waited for; matrix products, arithmetic and copies ran while one was open for 0% of the time, Pallas kernels for 7%

profile of v6, /device:TPU:0, one launch (start us, length us, event | category | flops | bytes accessed | tf_op | source)
XLA Modules:
  0.0 128.3 jit_solution(5147740264118142242)
XLA Ops:
  2.5 5.1 %collective-permute-start.2 = (bf16[1,304,128]{2,1,0:T(8,128)(2,1)S(1)}, bf16[1,304,128]{2,1,0:T(8,128)(2,1)S(1)}, u32[]{:S(2)}, u32[]{:S(2)}) collective-permute-start(bf16[1,304,128]{2,1,0:T(8,128)(2,1)S(1)} %select_bitcast_fusion), channel_id=1, source_target_pairs={{0,6},{1,7},{2,4},{3,5},{4,2},{5,3},{6,0},{7,1},{8,14},{9,15},{10,... | collective-permute-start | bytes 233480 | tf_op jit(solution)/shard_map/ppermute | solution.py:1069
  8.2 2.2 %collective-permute-done.2 = bf16[1,304,128]{2,1,0:T(8,128)(2,1)S(1)} collective-permute-done((bf16[1,304,128]{2,1,0:T(8,128)(2,1)S(1)}, bf16[1,304,128]{2,1,0:T(8,128)(2,1)S(1)}, u32[]{:S(2)}, u32[]{:S(2)}) %collective-permute-start.2) | collective-permute-done | bytes 77856 | tf_op jit(solution)/shard_map/ppermute | solution.py:1069
  10.5 3.7 %collective-permute-done.1 = bf16[1,304,128]{2,1,0:T(8,128)(2,1)S(1)} collective-permute-done((bf16[1,304,128]{2,1,0:T(8,128)(2,1)S(1)}, bf16[1,304,128]{2,1,0:T(8,128)(2,1)S(1)}, u32[]{:S(2)}, u32[]{:S(2)}) %collective-permute-start.1) | collective-permute-done | bytes 77856 | tf_op jit(solution)/shard_map/ppermute | solution.py:1069
  14.2 1.6 %collective-permute-start.4 = (bf16[4,152,128]{2,1,0:T(8,128)(2,1)S(1)}, bf16[4,152,128]{2,1,0:T(8,128)(2,1)S(1)}, u32[]{:S(2)}, u32[]{:S(2)}) collective-permute-start(bf16[4,152,128]{2,1,0:T(8,128)(2,1)S(1)} %get-tuple-element.68), channel_id=1, source_target_pairs={{0,16},{1,17},{2,18},{3,19},{4,20},{5,21},{6,22},{7,23},{8,24},{9,... | collective-permute-start | bytes 466952 | tf_op jit(solution)/shard_map/ppermute | solution.py:1069
  15.8 1.5 %collective-permute-start.3 = (bf16[4,152,128]{2,1,0:T(8,128)(2,1)S(1)}, bf16[4,152,128]{2,1,0:T(8,128)(2,1)S(1)}, u32[]{:S(2)}, u32[]{:S(2)}) collective-permute-start(bf16[4,152,128]{2,1,0:T(8,128)(2,1)S(1)} %get-tuple-element.69), channel_id=1, source_target_pairs={{0,8},{1,9},{2,10},{3,11},{4,12},{5,13},{6,14},{7,15},{8,0},{9,1},... | collective-permute-start | bytes 466952 | tf_op jit(solution)/shard_map/ppermute | solution.py:1069
  17.4 2.2 %collective-permute-done.4 = bf16[4,152,128]{2,1,0:T(8,128)(2,1)S(1)} collective-permute-done((bf16[4,152,128]{2,1,0:T(8,128)(2,1)S(1)}, bf16[4,152,128]{2,1,0:T(8,128)(2,1)S(1)}, u32[]{:S(2)}, u32[]{:S(2)}) %collective-permute-start.4) | collective-permute-done | bytes 155680 | tf_op jit(solution)/shard_map/ppermute | solution.py:1069
  19.6 1.4 %collective-permute-done.3 = bf16[4,152,128]{2,1,0:T(8,128)(2,1)S(1)} collective-permute-done((bf16[4,152,128]{2,1,0:T(8,128)(2,1)S(1)}, bf16[4,152,128]{2,1,0:T(8,128)(2,1)S(1)}, u32[]{:S(2)}, u32[]{:S(2)}) %collective-permute-start.3) | collective-permute-done | bytes 155680 | tf_op jit(solution)/shard_map/ppermute | solution.py:1069
  21.6 1.5 %collective-permute-start.6 = (bf16[8,152,128]{2,1,0:T(8,128)(2,1)S(1)}, bf16[8,152,128]{2,1,0:T(8,128)(2,1)S(1)}, u32[]{:S(2)}, u32[]{:S(2)}) collective-permute-start(bf16[8,152,128]{2,1,0:T(8,128)(2,1)S(1)} %pad_maximum_fusion.3.refs_2_), channel_id=1, source_target_pairs={{0,8},{1,9},{2,10},{3,11},{4,12},{5,13},{6,14},{7,15},{8,0},{9,1},... | collective-permute-start | bytes 933896 | tf_op jit(solution)/shard_map/ppermute | solution.py:1069
  23.1 3.4 %shift.1 = (bf16[192,4096]{1,0:T(8,128)(2,1)S(1)}, bf16[192,4096]{1,0:T(8,128)(2,1)S(1)}) custom-call(bf16[2304,192]{1,0:T(8,128)(2,1)S(1)} %bitcast.32, s32[1,2304]{1,0:T(1,128)S(1)} %reshape_squeeze.9.slots_ref.refs_9_.refs_0_), custom_call_target="tpu_custom_call" | custom-call | flops 3623878656 | bytes 4039680 | tf_op jit(solution)/shard_map/shift/pallas_call | solution.py:325
  32.1 1.4 %copy-done.4 = bf16[192,4096]{1,0:T(8,128)(2,1)S(1)} copy-done((bf16[192,4096]{1,0:T(8,128)(2,1)S(1)}, bf16[192,4096]{1,0:T(8,128)(2,1)}, u32[]{:S(2)}) %copy-start.4) | copy-done | bytes 1572888
  33.5 19.0 %window_forward.1 = (f32[192,2304]{1,0:T(8,128)S(1)}, bf16[576,4096]{1,0:T(8,128)(2,1)}, bf16[192,4096]{1,0:T(8,128)(2,1)S(1)}, bf16[32,80,768]{2,1,0:T(8,128)(2...) custom-call(s32[1]{0:T(128)} %bitcast.me_ref, ...), custom_call_target="tpu_custom_call" | custom-call | flops 3623878656 | bytes 19133956 | tf_op jit(solution)/shard_map/window_forward/pallas_call | solution.py:325
  52.5 1.9 %copy-done.2 = bf16[32,80,768]{2,1,0:T(8,128)(2,1)} copy-done((bf16[32,80,768]{2,1,0:T(8,128)(2,1)}, bf16[32,80,768]{2,1,0:T(8,128)(2,1)S(1)}, u32[]{:S(2)}) %copy-start.2) | copy-done | bytes 3932184
  54.5 22.2 %column.1 = (bf16[2304,192]{1,0:T(8,128)(2,1)}, f32[192,2304]{1,0:T(8,128)S(1)}, bf16[192,2304]{1,0:T(8,128)(2,1)S(1)}, f32[3488,128]{1,0:T(8,128)S(1)}) custom-call(f32[3488,128]{1,0:T(8,128)S(1)} %get-tuple-element.44.dense, f32[192,2304]{1,0:T(8,128)S(1)} %get-tuple-element.45.x_ref, bf16[2304,192]{1,0:T(8,128)(2,1)S(1)} %bitcast.34, ...), custom_call_target="tpu_custom_call" | custom-call | flops 6794772480 | bytes 9774080 | tf_op jit(solution)/shard_map/column/pallas_call | solution.py:325
  76.7 21.8 %window_backward.1 = (bf16[192,2304]{1,0:T(8,128)(2,1)S(1)}, bf16[16,304,128]{2,1,0:T(8,128)(2,1)S(1)}, bf16[16,304,128]{2,1,0:T(8,128)(2,1)S(1)}) custom-call(s32[1]{0:T(128)} %bitcast.me_ref, s32[8,128]{1,0:T(8,128)S(1)} %get-tuple-element.47.band_ref, s32[1,2304]{1,0:T(1,128)S(1)} %reshape_squeeze.9.slots_ref.refs_9_.refs_0_, ...), custom_call_target="tpu_custom_call" | custom-call | flops 7247757312 | bytes 18248708 | tf_op jit(solution)/shard_map/window_backward/pallas_call | solution.py:325
  98.7 2.8 %collective-permute-done.11 = bf16[16,304,128]{2,1,0:T(8,128)(2,1)S(1)} collective-permute-done((bf16[16,304,128]{2,1,0:T(8,128)(2,1)S(1)}, bf16[16,304,128]{2,1,0:T(8,128)(2,1)S(1)}, u32[]{:S(2)}, u32[]{:S(2)}) %collective-permute-start.11) | collective-permute-done | bytes 1245216 | tf_op jit(solution)/shard_map/ppermute | solution.py:1069
  101.9 1.6 %collective-permute-start.12 = (bf16[8,152,128]{2,1,0:T(8,128)(2,1)S(1)}, bf16[8,152,128]{2,1,0:T(8,128)(2,1)S(1)}, u32[]{:S(2)}, u32[]{:S(2)}) collective-permute-start(bf16[8,152,128]{2,1,0:T(8,128)(2,1)S(1)} %slice.119), channel_id=1, source_target_pairs={{0,16},{1,17},{2,18},{3,19},{4,20},{5,21},{6,22},{7,23},{8,24},{9,... | collective-permute-start | bytes 933896 | tf_op jit(solution)/shard_map/ppermute | solution.py:1069
  103.5 1.5 %collective-permute-start.13 = (bf16[2,4,152,128]{3,2,1,0:T(8,128)(2,1)S(1)}, bf16[2,4,152,128]{3,2,1,0:T(8,128)(2,1)S(1)}, u32[]{:S(2)}, u32[]{:S(2)}) collective-permute-start(bf16[2,4,152,128]{3,2,1,0:T(8,128)(2,1)S(1)} %fusion.2), channel_id=1, source_target_pairs={{0,8},{1,9},{2,10},{3,11},{4,12},{5,13},{6,14},{7,15},{8,0},{9,1},... | collective-permute-start | bytes 933896 | tf_op jit(solution)/shard_map/ppermute | solution.py:1069
  105.1 5.4 %finish.1 = f32[2304,192]{1,0:T(8,128)} custom-call(bf16[192,2304]{1,0:T(8,128)(2,1)S(1)} %get-tuple-element.60.shift_ref, s32[1,2304]{1,0:T(1,128)S(1)} %reshape_squeeze.9.slots_ref.refs_9_.refs_0_, f32[192,2304]{1,0:T(8,128)S(1)} %get-tuple-element.61.after_ref), custom_call_target="tpu_custom_call" | custom-call | flops 2038431744 | bytes 4432896 | tf_op jit(solution)/shard_map/finish/pallas_call | solution.py:325
  113.4 1.6 %collective-permute-start.14 = (bf16[4,152,128]{2,1,0:T(8,128)(2,1)S(1)}, bf16[4,152,128]{2,1,0:T(8,128)(2,1)S(1)}, u32[]{:S(2)}, u32[]{:S(2)}) collective-permute-start(bf16[4,152,128]{2,1,0:T(8,128)(2,1)S(1)} %slice.120), channel_id=1, source_target_pairs={{0,8},{1,9},{2,10},{3,11},{4,12},{5,13},{6,14},{7,15},{8,0},{9,1},... | collective-permute-start | bytes 466952 | tf_op jit(solution)/shard_map/ppermute | solution.py:1069
  115.0 3.1 %collective-permute-done.15 = bf16[4,152,128]{2,1,0:T(8,128)(2,1)S(1)} collective-permute-done((bf16[4,152,128]{2,1,0:T(8,128)(2,1)S(1)}, bf16[4,152,128]{2,1,0:T(8,128)(2,1)S(1)}, u32[]{:S(2)}, u32[]{:S(2)}) %collective-permute-start.15) | collective-permute-done | bytes 155680 | tf_op jit(solution)/shard_map/ppermute | solution.py:1069
  119.6 1.8 %collective-permute-start.18 = (bf16[304,128]{1,0:T(8,128)(2,1)S(1)}, bf16[304,128]{1,0:T(8,128)(2,1)S(1)}, u32[]{:S(2)}, u32[]{:S(2)}) collective-permute-start(bf16[304,128]{1,0:T(8,128)(2,1)S(1)} %get-tuple-element.66), channel_id=1, source_target_pairs={{0,6},{1,7},{2,4},{3,5},{4,2},{5,3},{6,0},{7,1},{8,14},{9,15},{10,... | collective-permute-start | bytes 233480 | tf_op jit(solution)/shard_map/ppermute | solution.py:1069
  122.4 1.7 %collective-permute-done.16 = bf16[304,128]{1,0:T(8,128)(2,1)S(1)} collective-permute-done((bf16[304,128]{1,0:T(8,128)(2,1)S(1)}, bf16[304,128]{1,0:T(8,128)(2,1)S(1)}, u32[]{:S(2)}, u32[]{:S(2)}) %collective-permute-start.16) | collective-permute-done | bytes 77856 | tf_op jit(solution)/shard_map/ppermute | solution.py:1069
  124.1 1.8 %collective-permute-done.18 = bf16[304,128]{1,0:T(8,128)(2,1)S(1)} collective-permute-done((bf16[304,128]{1,0:T(8,128)(2,1)S(1)}, bf16[304,128]{1,0:T(8,128)(2,1)S(1)}, u32[]{:S(2)}, u32[]{:S(2)}) %collective-permute-start.18) | collective-permute-done | bytes 77856 | tf_op jit(solution)/shard_map/ppermute | solution.py:1069
  125.9 1.7 %collective-permute-done.17 = bf16[304,128]{1,0:T(8,128)(2,1)S(1)} collective-permute-done((bf16[304,128]{1,0:T(8,128)(2,1)S(1)}, bf16[304,128]{1,0:T(8,128)(2,1)S(1)}, u32[]{:S(2)}, u32[]{:S(2)}) %collective-permute-start.17) | collective-permute-done | bytes 77856 | tf_op jit(solution)/shard_map/ppermute | solution.py:1069
  (66 shorter events, 15.6 us)
Async XLA Ops:
  0.6 16.6 %copy-start.7 = (s32[1,8,1,288]{3,2,1,0:T(1,128)S(1)}, s32[1,8,1,288]{3,2,1,0:T(1,128)}, u32[]{:S(2)}) copy-start(s32[1,8,1,288]{3,2,1,0:T(1,128)} %param.9) | copy-start | bytes 27652
  0.6 22.5 %copy-start = (bf16[1,288,8,192]{3,2,1,0:T(8,128)(2,1)S(1)}, bf16[1,288,8,192]{3,2,1,0:T(8,128)(2,1)}, u32[]{:S(2)}) copy-start(bf16[1,288,8,192]{3,2,1,0:T(8,128)(2,1)} %param.6) | copy-start | bytes 2654212
  2.5 8.0 %collective-permute-start.2 = (bf16[1,304,128]{2,1,0:T(8,128)(2,1)S(1)}, bf16[1,304,128]{2,1,0:T(8,128)(2,1)S(1)}, u32[]{:S(2)}, u32[]{:S(2)}) collective-permute-start(bf16[1,304,128]{2,1,0:T(8,128)(2,1)S(1)} %select_bitcast_fusion), channel_id=1, source_target_pairs={{0,6},{1,7},{2,4},{3,5},{4,2},{5,3},{6,0},{7,1},{8,14},{9,15},{10,... | collective-permute-start | bytes 233480 | tf_op jit(solution)/shard_map/ppermute | solution.py:1069
  7.6 6.5 %collective-permute-start.1 = (bf16[1,304,128]{2,1,0:T(8,128)(2,1)S(1)}, bf16[1,304,128]{2,1,0:T(8,128)(2,1)S(1)}, u32[]{:S(2)}, u32[]{:S(2)}) collective-permute-start(bf16[1,304,128]{2,1,0:T(8,128)(2,1)S(1)} %select_bitcast_fusion), channel_id=1, source_target_pairs={{0,4},{1,5},{2,6},{3,7},{4,0},{5,1},{6,2},{7,3},{8,12},{9,13},{10,... | collective-permute-start | bytes 233480 | tf_op jit(solution)/shard_map/ppermute | solution.py:1069
  7.6 6.5 %collective-permute-start = (bf16[1,304,128]{2,1,0:T(8,128)(2,1)S(1)}, bf16[1,304,128]{2,1,0:T(8,128)(2,1)S(1)}, u32[]{:S(2)}, u32[]{:S(2)}) collective-permute-start(bf16[1,304,128]{2,1,0:T(8,128)(2,1)S(1)} %select_bitcast_fusion), channel_id=1, source_target_pairs={{0,2},{1,3},{2,0},{3,1},{4,6},{5,7},{6,4},{7,5},{8,10},{9,11},{10,... | collective-permute-start | bytes 233480 | tf_op jit(solution)/shard_map/ppermute | solution.py:1069
  14.2 5.4 %collective-permute-start.4 = (bf16[4,152,128]{2,1,0:T(8,128)(2,1)S(1)}, bf16[4,152,128]{2,1,0:T(8,128)(2,1)S(1)}, u32[]{:S(2)}, u32[]{:S(2)}) collective-permute-start(bf16[4,152,128]{2,1,0:T(8,128)(2,1)S(1)} %get-tuple-element.68), channel_id=1, source_target_pairs={{0,16},{1,17},{2,18},{3,19},{4,20},{5,21},{6,22},{7,23},{8,24},{9,... | collective-permute-start | bytes 466952 | tf_op jit(solution)/shard_map/ppermute | solution.py:1069
  15.8 5.2 %collective-permute-start.3 = (bf16[4,152,128]{2,1,0:T(8,128)(2,1)S(1)}, bf16[4,152,128]{2,1,0:T(8,128)(2,1)S(1)}, u32[]{:S(2)}, u32[]{:S(2)}) collective-permute-start(bf16[4,152,128]{2,1,0:T(8,128)(2,1)S(1)} %get-tuple-element.69), channel_id=1, source_target_pairs={{0,8},{1,9},{2,10},{3,11},{4,12},{5,13},{6,14},{7,15},{8,0},{9,1},... | collective-permute-start | bytes 466952 | tf_op jit(solution)/shard_map/ppermute | solution.py:1069
  21.0 7.8 %collective-permute-start.5 = (bf16[8,152,128]{2,1,0:T(8,128)(2,1)S(1)}, bf16[8,152,128]{2,1,0:T(8,128)(2,1)S(1)}, u32[]{:S(2)}, u32[]{:S(2)}) collective-permute-start(bf16[8,152,128]{2,1,0:T(8,128)(2,1)S(1)} %pad_maximum_fusion.2.refs_0_), channel_id=1, source_target_pairs={{0,16},{1,17},{2,18},{3,19},{4,20},{5,21},{6,22},{7,23},{8,24},{9,... | collective-permute-start | bytes 933896 | tf_op jit(solution)/shard_map/ppermute | solution.py:1069
  21.6 7.4 %collective-permute-start.6 = (bf16[8,152,128]{2,1,0:T(8,128)(2,1)S(1)}, bf16[8,152,128]{2,1,0:T(8,128)(2,1)S(1)}, u32[]{:S(2)}, u32[]{:S(2)}) collective-permute-start(bf16[8,152,128]{2,1,0:T(8,128)(2,1)S(1)} %pad_maximum_fusion.3.refs_2_), channel_id=1, source_target_pairs={{0,8},{1,9},{2,10},{3,11},{4,12},{5,13},{6,14},{7,15},{8,0},{9,1},... | collective-permute-start | bytes 933896 | tf_op jit(solution)/shard_map/ppermute | solution.py:1069
  23.1 7.0 %copy-start.8 = (s32[1,288]{1,0:T(1,128)S(1)}, s32[1,288]{1,0:T(1,128)}, u32[]{:S(2)}) copy-start(s32[1,288]{1,0:T(1,128)} %param.11) | copy-start | bytes 3460
  29.1 1.6 %collective-permute-start.7 = (bf16[8,152,128]{2,1,0:T(8,128)(2,1)S(1)}, bf16[8,152,128]{2,1,0:T(8,128)(2,1)S(1)}, u32[]{:S(2)}, u32[]{:S(2)}) collective-permute-start(bf16[8,152,128]{2,1,0:T(8,128)(2,1)S(1)} %pad_maximum_fusion.2.refs_0_), channel_id=1, source_target_pairs={{0,1},{1,0},{2,3},{3,2},{4,5},{5,4},{6,7},{7,6},{8,9},{9,8},{10,11... | collective-permute-start | bytes 933896 | tf_op jit(solution)/shard_map/ppermute | solution.py:1069
  29.1 2.0 %collective-permute-start.8 = (bf16[8,152,128]{2,1,0:T(8,128)(2,1)S(1)}, bf16[8,152,128]{2,1,0:T(8,128)(2,1)S(1)}, u32[]{:S(2)}, u32[]{:S(2)}) collective-permute-start(bf16[8,152,128]{2,1,0:T(8,128)(2,1)S(1)} %collective-permute-done.5.refs_1_), channel_id=1, source_target_pairs={{0,1},{1,0},{2,3},{3,2},{4,5},{5,4},{6,7},{7,6},{8,9},{9,8},{10,11... | collective-permute-start | bytes 933896 | tf_op jit(solution)/shard_map/ppermute | solution.py:1069
  29.6 2.4 %collective-permute-start.9 = (bf16[8,152,128]{2,1,0:T(8,128)(2,1)S(1)}, bf16[8,152,128]{2,1,0:T(8,128)(2,1)S(1)}, u32[]{:S(2)}, u32[]{:S(2)}) collective-permute-start(bf16[8,152,128]{2,1,0:T(8,128)(2,1)S(1)} %pad_maximum_fusion.3.refs_2_), channel_id=1, source_target_pairs={{0,1},{1,0},{2,3},{3,2},{4,5},{5,4},{6,7},{7,6},{8,9},{9,8},{10,11... | collective-permute-start | bytes 933896 | tf_op jit(solution)/shard_map/ppermute | solution.py:1069
  29.6 2.6 %collective-permute-start.10 = (bf16[8,152,128]{2,1,0:T(8,128)(2,1)S(1)}, bf16[8,152,128]{2,1,0:T(8,128)(2,1)}, u32[]{:S(2)}, u32[]{:S(2)}) collective-permute-start(bf16[8,152,128]{2,1,0:T(8,128)(2,1)S(1)} %collective-permute-done.6.refs_3_), channel_id=1, source_target_pairs={{0,1},{1,0},{2,3},{3,2},{4,5},{5,4},{6,7},{7,6},{8,9},{9,8},{10,11... | collective-permute-start | bytes 933896 | tf_op jit(solution)/shard_map/ppermute | solution.py:1069
  33.5 20.9 %copy-start.1 = (bf16[1,288,8,192]{3,2,1,0:T(8,128)(2,1)S(1)}, bf16[1,288,8,192]{3,2,1,0:T(8,128)(2,1)}, u32[]{:S(2)}) copy-start(bf16[1,288,8,192]{3,2,1,0:T(8,128)(2,1)} %param.7) | copy-start | bytes 2654212
  54.5 22.2 %copy-start.6 = (bf16[192,4096]{1,0:T(8,128)(2,1)S(1)}, bf16[192,4096]{1,0:T(8,128)(2,1)}, u32[]{:S(2)}) copy-start(bf16[192,4096]{1,0:T(8,128)(2,1)} %copy-done.5) | copy-start | bytes 4718596
  98.5 3.0 %collective-permute-start.11 = (bf16[16,304,128]{2,1,0:T(8,128)(2,1)S(1)}, bf16[16,304,128]{2,1,0:T(8,128)(2,1)S(1)}, u32[]{:S(2)}, u32[]{:S(2)}) collective-permute-start(bf16[16,304,128]{2,1,0:T(8,128)(2,1)S(1)} %get-tuple-element.57), channel_id=1, source_target_pairs={{0,1},{1,0},{2,3},{3,2},{4,5},{5,4},{6,7},{7,6},{8,9},{9,8},{10,11... | collective-permute-start | bytes 3735560 | tf_op jit(solution)/shard_map/ppermute | solution.py:1069
  101.9 9.5 %collective-permute-start.12 = (bf16[8,152,128]{2,1,0:T(8,128)(2,1)S(1)}, bf16[8,152,128]{2,1,0:T(8,128)(2,1)S(1)}, u32[]{:S(2)}, u32[]{:S(2)}) collective-permute-start(bf16[8,152,128]{2,1,0:T(8,128)(2,1)S(1)} %slice.119), channel_id=1, source_target_pairs={{0,16},{1,17},{2,18},{3,19},{4,20},{5,21},{6,22},{7,23},{8,24},{9,... | collective-permute-start | bytes 933896 | tf_op jit(solution)/shard_map/ppermute | solution.py:1069
  103.5 9.2 %collective-permute-start.13 = (bf16[2,4,152,128]{3,2,1,0:T(8,128)(2,1)S(1)}, bf16[2,4,152,128]{3,2,1,0:T(8,128)(2,1)S(1)}, u32[]{:S(2)}, u32[]{:S(2)}) collective-permute-start(bf16[2,4,152,128]{3,2,1,0:T(8,128)(2,1)S(1)} %fusion.2), channel_id=1, source_target_pairs={{0,8},{1,9},{2,10},{3,11},{4,12},{5,13},{6,14},{7,15},{8,0},{9,1},... | collective-permute-start | bytes 933896 | tf_op jit(solution)/shard_map/ppermute | solution.py:1069
  112.8 5.3 %collective-permute-start.15 = (bf16[4,152,128]{2,1,0:T(8,128)(2,1)S(1)}, bf16[4,152,128]{2,1,0:T(8,128)(2,1)S(1)}, u32[]{:S(2)}, u32[]{:S(2)}) collective-permute-start(bf16[4,152,128]{2,1,0:T(8,128)(2,1)S(1)} %fusion.3), channel_id=1, source_target_pairs={{0,16},{1,17},{2,18},{3,19},{4,20},{5,21},{6,22},{7,23},{8,24},{9,... | collective-permute-start | bytes 466952 | tf_op jit(solution)/shard_map/ppermute | solution.py:1069
  113.4 5.3 %collective-permute-start.14 = (bf16[4,152,128]{2,1,0:T(8,128)(2,1)S(1)}, bf16[4,152,128]{2,1,0:T(8,128)(2,1)S(1)}, u32[]{:S(2)}, u32[]{:S(2)}) collective-permute-start(bf16[4,152,128]{2,1,0:T(8,128)(2,1)S(1)} %slice.120), channel_id=1, source_target_pairs={{0,8},{1,9},{2,10},{3,11},{4,12},{5,13},{6,14},{7,15},{8,0},{9,1},... | collective-permute-start | bytes 466952 | tf_op jit(solution)/shard_map/ppermute | solution.py:1069
  118.8 5.3 %collective-permute-start.16 = (bf16[304,128]{1,0:T(8,128)(2,1)S(1)}, bf16[304,128]{1,0:T(8,128)(2,1)S(1)}, u32[]{:S(2)}, u32[]{:S(2)}) collective-permute-start(bf16[304,128]{1,0:T(8,128)(2,1)S(1)} %get-tuple-element.65), channel_id=1, source_target_pairs={{0,2},{1,3},{2,0},{3,1},{4,6},{5,7},{6,4},{7,5},{8,10},{9,11},{10,... | collective-permute-start | bytes 233480 | tf_op jit(solution)/shard_map/ppermute | solution.py:1069
  119.6 6.3 %collective-permute-start.18 = (bf16[304,128]{1,0:T(8,128)(2,1)S(1)}, bf16[304,128]{1,0:T(8,128)(2,1)S(1)}, u32[]{:S(2)}, u32[]{:S(2)}) collective-permute-start(bf16[304,128]{1,0:T(8,128)(2,1)S(1)} %get-tuple-element.66), channel_id=1, source_target_pairs={{0,6},{1,7},{2,4},{3,5},{4,2},{5,3},{6,0},{7,1},{8,14},{9,15},{10,... | collective-permute-start | bytes 233480 | tf_op jit(solution)/shard_map/ppermute | solution.py:1069
  121.5 6.1 %collective-permute-start.17 = (bf16[304,128]{1,0:T(8,128)(2,1)S(1)}, bf16[304,128]{1,0:T(8,128)(2,1)S(1)}, u32[]{:S(2)}, u32[]{:S(2)}) collective-permute-start(bf16[304,128]{1,0:T(8,128)(2,1)S(1)} %get-tuple-element.67), channel_id=1, source_target_pairs={{0,4},{1,5},{2,6},{3,7},{4,0},{5,1},{6,2},{7,3},{8,12},{9,13},{10,... | collective-permute-start | bytes 233480 | tf_op jit(solution)/shard_map/ppermute | solution.py:1069
  (4 other events, 5.7 us)

commit v7 on v6

--- a/solution.py
+++ b/solution.py
@@ -550,7 +550,7 @@
     steps = n // SLOT_BLOCK
     per_step = SLOT_BLOCK // LANES
     padded = padded_rows(rows)
-    flat_rows = max(shards * rows, BIAS_ROW + DENSE * PERIODS + 8)
+    flat_rows = max(shards * rows, BIAS_ROW + DENSE * PERIODS + 16)
     slot_block = lambda r: pl.BlockSpec((r, SLOT_BLOCK), lambda i, *_: (0, jnp.minimum(i, steps - 1)))
     ins = [(me, None), (bands, None)]
     ins += [(p, pl.BlockSpec(memory_space=pl.ANY)) for p in parts]
@@ -993,7 +993,7 @@
             pl.BlockSpec((per_step, KEYS, HEADS * LANES), lambda i, *_: (i, 0, 0)),
         ),
     ]
-    flat_rows = max(shards * rows, BIAS_ROW + DENSE * PERIODS + 8)
+    flat_rows = max(shards * rows, BIAS_ROW + DENSE * PERIODS + 16)
     if fused:
         tight = pl.BlockSpec((D, TIGHT_BLOCK), lambda i, *_: (0, i))
         first = ((D, n // LANES * WIN), BF16, tight)
@@ -1019,7 +1019,7 @@
     kernel = functools.partial(
         window_backward_kernel, order=order, shard_rows=rows, space=space
     )
-    return call(kernel, (n // SLOT_BLOCK,), ins, outs, scratch, "window_backward", 24 * D * D * n, 44, scalars=2)
+    return call(kernel, (n // SLOT_BLOCK,), ins, outs, scratch, "window_backward", 24 * D * D * n, 40, scalars=2)
 
 
 def finish_kernel(shift_ref, slots_ref, after_ref, out_ref):

time: 129 us -> 127 us (0.984)
  local copies, waits for them, and re-layouts: 6.24 us -> 4.33 us
    unnamed x18 -> x16, local copies, waits for them, and re-layouts: 5.67 us -> 3.76 us
where the time goes in v7:
time: 127 us; the launch traced here: 126 us
  Pallas kernels  71.7 us (56%)
  waiting for transfers between devices  25.3 us (20%)
  starting transfers between devices  21 us (17%)
  local copies, waits for them, and re-layouts  4.33 us (3%)
  other arithmetic  3.12 us (2%)
    pallas_call x5, Pallas kernels, call(): pl.pallas_call(kernel, grid_spec=spec, out_shape=[jax.ShapeDtypeStruct(sh...  71.7 us
    ppermute x19, waiting for transfers between devices, swap(): lax.ppermute(value, ('dp', 'space'), [(k, k ^ flip) for k in range(device...  25.3 us
    ppermute x19, starting transfers between devices, swap(): lax.ppermute(value, ('dp', 'space'), [(k, k ^ flip) for k in range(device...  21 us
    unnamed x16, local copies, waits for them, and re-layouts  3.76 us
  transfers between devices with their start and end apart: 19, of which 17 were waited for; matrix products, arithmetic and copies ran while one was open for 0% of the time, Pallas kernels for 7%

profile of v7, /device:TPU:0, one launch (start us, length us, event | category | flops | bytes accessed | tf_op | source)
XLA Modules:
  0.0 126.3 jit_solution(889047955320313836)
XLA Ops:
  2.5 5.1 %collective-permute-start.2 = (bf16[1,304,128]{2,1,0:T(8,128)(2,1)S(1)}, bf16[1,304,128]{2,1,0:T(8,128)(2,1)S(1)}, u32[]{:S(2)}, u32[]{:S(2)}) collective-permute-start(bf16[1,304,128]{2,1,0:T(8,128)(2,1)S(1)} %select_bitcast_fusion), channel_id=1, source_target_pairs={{0,6},{1,7},{2,4},{3,5},{4,2},{5,3},{6,0},{7,1},{8,14},{9,15},{10,... | collective-permute-start | bytes 233480 | tf_op jit(solution)/shard_map/ppermute | solution.py:1069
  8.2 2.2 %collective-permute-done.2 = bf16[1,304,128]{2,1,0:T(8,128)(2,1)S(1)} collective-permute-done((bf16[1,304,128]{2,1,0:T(8,128)(2,1)S(1)}, bf16[1,304,128]{2,1,0:T(8,128)(2,1)S(1)}, u32[]{:S(2)}, u32[]{:S(2)}) %collective-permute-start.2) | collective-permute-done | bytes 77856 | tf_op jit(solution)/shard_map/ppermute | solution.py:1069
  10.5 3.7 %collective-permute-done.1 = bf16[1,304,128]{2,1,0:T(8,128)(2,1)S(1)} collective-permute-done((bf16[1,304,128]{2,1,0:T(8,128)(2,1)S(1)}, bf16[1,304,128]{2,1,0:T(8,128)(2,1)S(1)}, u32[]{:S(2)}, u32[]{:S(2)}) %collective-permute-start.1) | collective-permute-done | bytes 77856 | tf_op jit(solution)/shard_map/ppermute | solution.py:1069
  14.2 1.6 %collective-permute-start.4 = (bf16[4,152,128]{2,1,0:T(8,128)(2,1)S(1)}, bf16[4,152,128]{2,1,0:T(8,128)(2,1)S(1)}, u32[]{:S(2)}, u32[]{:S(2)}) collective-permute-start(bf16[4,152,128]{2,1,0:T(8,128)(2,1)S(1)} %get-tuple-element.68), channel_id=1, source_target_pairs={{0,16},{1,17},{2,18},{3,19},{4,20},{5,21},{6,22},{7,23},{8,24},{9,... | collective-permute-start | bytes 466952 | tf_op jit(solution)/shard_map/ppermute | solution.py:1069
  15.8 1.5 %collective-permute-start.3 = (bf16[4,152,128]{2,1,0:T(8,128)(2,1)S(1)}, bf16[4,152,128]{2,1,0:T(8,128)(2,1)S(1)}, u32[]{:S(2)}, u32[]{:S(2)}) collective-permute-start(bf16[4,152,128]{2,1,0:T(8,128)(2,1)S(1)} %get-tuple-element.69), channel_id=1, source_target_pairs={{0,8},{1,9},{2,10},{3,11},{4,12},{5,13},{6,14},{7,15},{8,0},{9,1},... | collective-permute-start | bytes 466952 | tf_op jit(solution)/shard_map/ppermute | solution.py:1069
  17.4 2.2 %collective-permute-done.4 = bf16[4,152,128]{2,1,0:T(8,128)(2,1)S(1)} collective-permute-done((bf16[4,152,128]{2,1,0:T(8,128)(2,1)S(1)}, bf16[4,152,128]{2,1,0:T(8,128)(2,1)S(1)}, u32[]{:S(2)}, u32[]{:S(2)}) %collective-permute-start.4) | collective-permute-done | bytes 155680 | tf_op jit(solution)/shard_map/ppermute | solution.py:1069
  19.6 1.4 %collective-permute-done.3 = bf16[4,152,128]{2,1,0:T(8,128)(2,1)S(1)} collective-permute-done((bf16[4,152,128]{2,1,0:T(8,128)(2,1)S(1)}, bf16[4,152,128]{2,1,0:T(8,128)(2,1)S(1)}, u32[]{:S(2)}, u32[]{:S(2)}) %collective-permute-start.3) | collective-permute-done | bytes 155680 | tf_op jit(solution)/shard_map/ppermute | solution.py:1069
  21.6 1.5 %collective-permute-start.6 = (bf16[8,152,128]{2,1,0:T(8,128)(2,1)S(1)}, bf16[8,152,128]{2,1,0:T(8,128)(2,1)S(1)}, u32[]{:S(2)}, u32[]{:S(2)}) collective-permute-start(bf16[8,152,128]{2,1,0:T(8,128)(2,1)S(1)} %pad_maximum_fusion.3.refs_2_), channel_id=1, source_target_pairs={{0,8},{1,9},{2,10},{3,11},{4,12},{5,13},{6,14},{7,15},{8,0},{9,1},... | collective-permute-start | bytes 933896 | tf_op jit(solution)/shard_map/ppermute | solution.py:1069
  23.1 3.4 %shift.1 = (bf16[192,4096]{1,0:T(8,128)(2,1)S(1)}, bf16[192,4096]{1,0:T(8,128)(2,1)S(1)}) custom-call(bf16[2304,192]{1,0:T(8,128)(2,1)S(1)} %bitcast.32, s32[1,2304]{1,0:T(1,128)S(1)} %reshape_squeeze.9.slots_ref.refs_9_.refs_0_), custom_call_target="tpu_custom_call" | custom-call | flops 3623878656 | bytes 4039680 | tf_op jit(solution)/shard_map/shift/pallas_call | solution.py:325
  32.1 1.4 %copy-done.3 = bf16[192,4096]{1,0:T(8,128)(2,1)S(1)} copy-done((bf16[192,4096]{1,0:T(8,128)(2,1)S(1)}, bf16[192,4096]{1,0:T(8,128)(2,1)}, u32[]{:S(2)}) %copy-start.3) | copy-done | bytes 1572888
  33.5 19.0 %window_forward.1 = (f32[192,2304]{1,0:T(8,128)S(1)}, bf16[576,4096]{1,0:T(8,128)(2,1)}, bf16[192,4096]{1,0:T(8,128)(2,1)S(1)}, bf16[32,80,768]{2,1,0:T(8,128)(2...) custom-call(s32[1]{0:T(128)} %bitcast.me_ref, ...), custom_call_target="tpu_custom_call" | custom-call | flops 3623878656 | bytes 19133956 | tf_op jit(solution)/shard_map/window_forward/pallas_call | solution.py:325
  52.6 22.4 %column.1 = (bf16[2304,192]{1,0:T(8,128)(2,1)}, f32[192,2304]{1,0:T(8,128)S(1)}, bf16[192,2304]{1,0:T(8,128)(2,1)S(1)}, f32[3488,128]{1,0:T(8,128)S(1)}) custom-call(f32[3488,128]{1,0:T(8,128)S(1)} %get-tuple-element.44.dense, f32[192,2304]{1,0:T(8,128)S(1)} %get-tuple-element.45.x_ref, bf16[2304,192]{1,0:T(8,128)(2,1)S(1)} %bitcast.34, ...), custom_call_target="tpu_custom_call" | custom-call | flops 6794772480 | bytes 9774080 | tf_op jit(solution)/shard_map/column/pallas_call | solution.py:325
  75.0 21.5 %window_backward.1 = (bf16[192,2304]{1,0:T(8,128)(2,1)S(1)}, bf16[16,304,128]{2,1,0:T(8,128)(2,1)S(1)}, bf16[16,304,128]{2,1,0:T(8,128)(2,1)S(1)}) custom-call(s32[1]{0:T(128)} %bitcast.me_ref, s32[8,128]{1,0:T(8,128)S(1)} %get-tuple-element.47.band_ref, s32[1,2304]{1,0:T(1,128)S(1)} %reshape_squeeze.9.slots_ref.refs_9_.refs_0_, ...), custom_call_target="tpu_custom_call" | custom-call | flops 7247757312 | bytes 18248708 | tf_op jit(solution)/shard_map/window_backward/pallas_call | solution.py:325
  96.7 2.8 %collective-permute-done.11 = bf16[16,304,128]{2,1,0:T(8,128)(2,1)S(1)} collective-permute-done((bf16[16,304,128]{2,1,0:T(8,128)(2,1)S(1)}, bf16[16,304,128]{2,1,0:T(8,128)(2,1)S(1)}, u32[]{:S(2)}, u32[]{:S(2)}) %collective-permute-start.11) | collective-permute-done | bytes 1245216 | tf_op jit(solution)/shard_map/ppermute | solution.py:1069
  99.9 1.6 %collective-permute-start.12 = (bf16[8,152,128]{2,1,0:T(8,128)(2,1)S(1)}, bf16[8,152,128]{2,1,0:T(8,128)(2,1)S(1)}, u32[]{:S(2)}, u32[]{:S(2)}) collective-permute-start(bf16[8,152,128]{2,1,0:T(8,128)(2,1)S(1)} %slice.119), channel_id=1, source_target_pairs={{0,16},{1,17},{2,18},{3,19},{4,20},{5,21},{6,22},{7,23},{8,24},{9,... | collective-permute-start | bytes 933896 | tf_op jit(solution)/shard_map/ppermute | solution.py:1069
  101.5 1.6 %collective-permute-start.13 = (bf16[2,4,152,128]{3,2,1,0:T(8,128)(2,1)S(1)}, bf16[2,4,152,128]{3,2,1,0:T(8,128)(2,1)S(1)}, u32[]{:S(2)}, u32[]{:S(2)}) collective-permute-start(bf16[2,4,152,128]{3,2,1,0:T(8,128)(2,1)S(1)} %fusion.2), channel_id=1, source_target_pairs={{0,8},{1,9},{2,10},{3,11},{4,12},{5,13},{6,14},{7,15},{8,0},{9,1},... | collective-permute-start | bytes 933896 | tf_op jit(solution)/shard_map/ppermute | solution.py:1069
  103.1 5.4 %finish.1 = f32[2304,192]{1,0:T(8,128)} custom-call(bf16[192,2304]{1,0:T(8,128)(2,1)S(1)} %get-tuple-element.60.shift_ref, s32[1,2304]{1,0:T(1,128)S(1)} %reshape_squeeze.9.slots_ref.refs_9_.refs_0_, f32[192,2304]{1,0:T(8,128)S(1)} %get-tuple-element.61.after_ref), custom_call_target="tpu_custom_call" | custom-call | flops 2038431744 | bytes 4432896 | tf_op jit(solution)/shard_map/finish/pallas_call | solution.py:325
  109.5 1.2 collective-permute-done.13
  111.4 1.5 %collective-permute-start.14 = (bf16[4,152,128]{2,1,0:T(8,128)(2,1)S(1)}, bf16[4,152,128]{2,1,0:T(8,128)(2,1)S(1)}, u32[]{:S(2)}, u32[]{:S(2)}) collective-permute-start(bf16[4,152,128]{2,1,0:T(8,128)(2,1)S(1)} %slice.120), channel_id=1, source_target_pairs={{0,8},{1,9},{2,10},{3,11},{4,12},{5,13},{6,14},{7,15},{8,0},{9,1},... | collective-permute-start | bytes 466952 | tf_op jit(solution)/shard_map/ppermute | solution.py:1069
  113.0 3.1 %collective-permute-done.15 = bf16[4,152,128]{2,1,0:T(8,128)(2,1)S(1)} collective-permute-done((bf16[4,152,128]{2,1,0:T(8,128)(2,1)S(1)}, bf16[4,152,128]{2,1,0:T(8,128)(2,1)S(1)}, u32[]{:S(2)}, u32[]{:S(2)}) %collective-permute-start.15) | collective-permute-done | bytes 155680 | tf_op jit(solution)/shard_map/ppermute | solution.py:1069
  117.7 1.8 %collective-permute-start.18 = (bf16[304,128]{1,0:T(8,128)(2,1)S(1)}, bf16[304,128]{1,0:T(8,128)(2,1)S(1)}, u32[]{:S(2)}, u32[]{:S(2)}) collective-permute-start(bf16[304,128]{1,0:T(8,128)(2,1)S(1)} %get-tuple-element.66), channel_id=1, source_target_pairs={{0,6},{1,7},{2,4},{3,5},{4,2},{5,3},{6,0},{7,1},{8,14},{9,15},{10,... | collective-permute-start | bytes 233480 | tf_op jit(solution)/shard_map/ppermute | solution.py:1069
  120.4 1.7 %collective-permute-done.16 = bf16[304,128]{1,0:T(8,128)(2,1)S(1)} collective-permute-done((bf16[304,128]{1,0:T(8,128)(2,1)S(1)}, bf16[304,128]{1,0:T(8,128)(2,1)S(1)}, u32[]{:S(2)}, u32[]{:S(2)}) %collective-permute-start.16) | collective-permute-done | bytes 77856 | tf_op jit(solution)/shard_map/ppermute | solution.py:1069
  122.1 1.9 %collective-permute-done.18 = bf16[304,128]{1,0:T(8,128)(2,1)S(1)} collective-permute-done((bf16[304,128]{1,0:T(8,128)(2,1)S(1)}, bf16[304,128]{1,0:T(8,128)(2,1)S(1)}, u32[]{:S(2)}, u32[]{:S(2)}) %collective-permute-start.18) | collective-permute-done | bytes 77856 | tf_op jit(solution)/shard_map/ppermute | solution.py:1069
  124.0 1.7 %collective-permute-done.17 = bf16[304,128]{1,0:T(8,128)(2,1)S(1)} collective-permute-done((bf16[304,128]{1,0:T(8,128)(2,1)S(1)}, bf16[304,128]{1,0:T(8,128)(2,1)S(1)}, u32[]{:S(2)}, u32[]{:S(2)}) %collective-permute-start.17) | collective-permute-done | bytes 77856 | tf_op jit(solution)/shard_map/ppermute | solution.py:1069
  (64 shorter events, 14.4 us)
Async XLA Ops:
  0.6 16.6 %copy-start.6 = (s32[1,8,1,288]{3,2,1,0:T(1,128)S(1)}, s32[1,8,1,288]{3,2,1,0:T(1,128)}, u32[]{:S(2)}) copy-start(s32[1,8,1,288]{3,2,1,0:T(1,128)} %param.9) | copy-start | bytes 27652
  0.6 22.5 %copy-start = (bf16[1,288,8,192]{3,2,1,0:T(8,128)(2,1)S(1)}, bf16[1,288,8,192]{3,2,1,0:T(8,128)(2,1)}, u32[]{:S(2)}) copy-start(bf16[1,288,8,192]{3,2,1,0:T(8,128)(2,1)} %param.6) | copy-start | bytes 2654212
  2.5 8.0 %collective-permute-start.2 = (bf16[1,304,128]{2,1,0:T(8,128)(2,1)S(1)}, bf16[1,304,128]{2,1,0:T(8,128)(2,1)S(1)}, u32[]{:S(2)}, u32[]{:S(2)}) collective-permute-start(bf16[1,304,128]{2,1,0:T(8,128)(2,1)S(1)} %select_bitcast_fusion), channel_id=1, source_target_pairs={{0,6},{1,7},{2,4},{3,5},{4,2},{5,3},{6,0},{7,1},{8,14},{9,15},{10,... | collective-permute-start | bytes 233480 | tf_op jit(solution)/shard_map/ppermute | solution.py:1069
  7.6 6.5 %collective-permute-start.1 = (bf16[1,304,128]{2,1,0:T(8,128)(2,1)S(1)}, bf16[1,304,128]{2,1,0:T(8,128)(2,1)S(1)}, u32[]{:S(2)}, u32[]{:S(2)}) collective-permute-start(bf16[1,304,128]{2,1,0:T(8,128)(2,1)S(1)} %select_bitcast_fusion), channel_id=1, source_target_pairs={{0,4},{1,5},{2,6},{3,7},{4,0},{5,1},{6,2},{7,3},{8,12},{9,13},{10,... | collective-permute-start | bytes 233480 | tf_op jit(solution)/shard_map/ppermute | solution.py:1069
  7.6 6.5 %collective-permute-start = (bf16[1,304,128]{2,1,0:T(8,128)(2,1)S(1)}, bf16[1,304,128]{2,1,0:T(8,128)(2,1)S(1)}, u32[]{:S(2)}, u32[]{:S(2)}) collective-permute-start(bf16[1,304,128]{2,1,0:T(8,128)(2,1)S(1)} %select_bitcast_fusion), channel_id=1, source_target_pairs={{0,2},{1,3},{2,0},{3,1},{4,6},{5,7},{6,4},{7,5},{8,10},{9,11},{10,... | collective-permute-start | bytes 233480 | tf_op jit(solution)/shard_map/ppermute | solution.py:1069
  14.2 5.4 %collective-permute-start.4 = (bf16[4,152,128]{2,1,0:T(8,128)(2,1)S(1)}, bf16[4,152,128]{2,1,0:T(8,128)(2,1)S(1)}, u32[]{:S(2)}, u32[]{:S(2)}) collective-permute-start(bf16[4,152,128]{2,1,0:T(8,128)(2,1)S(1)} %get-tuple-element.68), channel_id=1, source_target_pairs={{0,16},{1,17},{2,18},{3,19},{4,20},{5,21},{6,22},{7,23},{8,24},{9,... | collective-permute-start | bytes 466952 | tf_op jit(solution)/shard_map/ppermute | solution.py:1069
  15.8 5.2 %collective-permute-start.3 = (bf16[4,152,128]{2,1,0:T(8,128)(2,1)S(1)}, bf16[4,152,128]{2,1,0:T(8,128)(2,1)S(1)}, u32[]{:S(2)}, u32[]{:S(2)}) collective-permute-start(bf16[4,152,128]{2,1,0:T(8,128)(2,1)S(1)} %get-tuple-element.69), channel_id=1, source_target_pairs={{0,8},{1,9},{2,10},{3,11},{4,12},{5,13},{6,14},{7,15},{8,0},{9,1},... | collective-permute-start | bytes 466952 | tf_op jit(solution)/shard_map/ppermute | solution.py:1069
  21.0 7.8 %collective-permute-start.5 = (bf16[8,152,128]{2,1,0:T(8,128)(2,1)S(1)}, bf16[8,152,128]{2,1,0:T(8,128)(2,1)S(1)}, u32[]{:S(2)}, u32[]{:S(2)}) collective-permute-start(bf16[8,152,128]{2,1,0:T(8,128)(2,1)S(1)} %pad_maximum_fusion.2.refs_0_), channel_id=1, source_target_pairs={{0,16},{1,17},{2,18},{3,19},{4,20},{5,21},{6,22},{7,23},{8,24},{9,... | collective-permute-start | bytes 933896 | tf_op jit(solution)/shard_map/ppermute | solution.py:1069
  21.6 7.4 %collective-permute-start.6 = (bf16[8,152,128]{2,1,0:T(8,128)(2,1)S(1)}, bf16[8,152,128]{2,1,0:T(8,128)(2,1)S(1)}, u32[]{:S(2)}, u32[]{:S(2)}) collective-permute-start(bf16[8,152,128]{2,1,0:T(8,128)(2,1)S(1)} %pad_maximum_fusion.3.refs_2_), channel_id=1, source_target_pairs={{0,8},{1,9},{2,10},{3,11},{4,12},{5,13},{6,14},{7,15},{8,0},{9,1},... | collective-permute-start | bytes 933896 | tf_op jit(solution)/shard_map/ppermute | solution.py:1069
  23.1 7.0 %copy-start.7 = (s32[1,288]{1,0:T(1,128)S(1)}, s32[1,288]{1,0:T(1,128)}, u32[]{:S(2)}) copy-start(s32[1,288]{1,0:T(1,128)} %param.11) | copy-start | bytes 3460
  29.1 1.6 %collective-permute-start.7 = (bf16[8,152,128]{2,1,0:T(8,128)(2,1)S(1)}, bf16[8,152,128]{2,1,0:T(8,128)(2,1)S(1)}, u32[]{:S(2)}, u32[]{:S(2)}) collective-permute-start(bf16[8,152,128]{2,1,0:T(8,128)(2,1)S(1)} %pad_maximum_fusion.2.refs_0_), channel_id=1, source_target_pairs={{0,1},{1,0},{2,3},{3,2},{4,5},{5,4},{6,7},{7,6},{8,9},{9,8},{10,11... | collective-permute-start | bytes 933896 | tf_op jit(solution)/shard_map/ppermute | solution.py:1069
  29.1 2.0 %collective-permute-start.8 = (bf16[8,152,128]{2,1,0:T(8,128)(2,1)S(1)}, bf16[8,152,128]{2,1,0:T(8,128)(2,1)S(1)}, u32[]{:S(2)}, u32[]{:S(2)}) collective-permute-start(bf16[8,152,128]{2,1,0:T(8,128)(2,1)S(1)} %collective-permute-done.5.refs_1_), channel_id=1, source_target_pairs={{0,1},{1,0},{2,3},{3,2},{4,5},{5,4},{6,7},{7,6},{8,9},{9,8},{10,11... | collective-permute-start | bytes 933896 | tf_op jit(solution)/shard_map/ppermute | solution.py:1069
  29.6 2.4 %collective-permute-start.9 = (bf16[8,152,128]{2,1,0:T(8,128)(2,1)S(1)}, bf16[8,152,128]{2,1,0:T(8,128)(2,1)S(1)}, u32[]{:S(2)}, u32[]{:S(2)}) collective-permute-start(bf16[8,152,128]{2,1,0:T(8,128)(2,1)S(1)} %pad_maximum_fusion.3.refs_2_), channel_id=1, source_target_pairs={{0,1},{1,0},{2,3},{3,2},{4,5},{5,4},{6,7},{7,6},{8,9},{9,8},{10,11... | collective-permute-start | bytes 933896 | tf_op jit(solution)/shard_map/ppermute | solution.py:1069
  29.6 2.6 %collective-permute-start.10 = (bf16[8,152,128]{2,1,0:T(8,128)(2,1)S(1)}, bf16[8,152,128]{2,1,0:T(8,128)(2,1)}, u32[]{:S(2)}, u32[]{:S(2)}) collective-permute-start(bf16[8,152,128]{2,1,0:T(8,128)(2,1)S(1)} %collective-permute-done.6.refs_3_), channel_id=1, source_target_pairs={{0,1},{1,0},{2,3},{3,2},{4,5},{5,4},{6,7},{7,6},{8,9},{9,8},{10,11... | collective-permute-start | bytes 933896 | tf_op jit(solution)/shard_map/ppermute | solution.py:1069
  33.5 19.0 %copy-start.1 = (bf16[1,288,8,192]{3,2,1,0:T(8,128)(2,1)S(1)}, bf16[1,288,8,192]{3,2,1,0:T(8,128)(2,1)}, u32[]{:S(2)}) copy-start(bf16[1,288,8,192]{3,2,1,0:T(8,128)(2,1)} %param.7) | copy-start | bytes 2654212
  52.6 22.4 %copy-start.5 = (bf16[192,4096]{1,0:T(8,128)(2,1)S(1)}, bf16[192,4096]{1,0:T(8,128)(2,1)}, u32[]{:S(2)}) copy-start(bf16[192,4096]{1,0:T(8,128)(2,1)} %copy-done.4) | copy-start | bytes 4718596
  96.5 3.0 %collective-permute-start.11 = (bf16[16,304,128]{2,1,0:T(8,128)(2,1)S(1)}, bf16[16,304,128]{2,1,0:T(8,128)(2,1)S(1)}, u32[]{:S(2)}, u32[]{:S(2)}) collective-permute-start(bf16[16,304,128]{2,1,0:T(8,128)(2,1)S(1)} %get-tuple-element.57), channel_id=1, source_target_pairs={{0,1},{1,0},{2,3},{3,2},{4,5},{5,4},{6,7},{7,6},{8,9},{9,8},{10,11... | collective-permute-start | bytes 3735560 | tf_op jit(solution)/shard_map/ppermute | solution.py:1069
  99.9 9.5 %collective-permute-start.12 = (bf16[8,152,128]{2,1,0:T(8,128)(2,1)S(1)}, bf16[8,152,128]{2,1,0:T(8,128)(2,1)S(1)}, u32[]{:S(2)}, u32[]{:S(2)}) collective-permute-start(bf16[8,152,128]{2,1,0:T(8,128)(2,1)S(1)} %slice.119), channel_id=1, source_target_pairs={{0,16},{1,17},{2,18},{3,19},{4,20},{5,21},{6,22},{7,23},{8,24},{9,... | collective-permute-start | bytes 933896 | tf_op jit(solution)/shard_map/ppermute | solution.py:1069
  101.5 9.2 %collective-permute-start.13 = (bf16[2,4,152,128]{3,2,1,0:T(8,128)(2,1)S(1)}, bf16[2,4,152,128]{3,2,1,0:T(8,128)(2,1)S(1)}, u32[]{:S(2)}, u32[]{:S(2)}) collective-permute-start(bf16[2,4,152,128]{3,2,1,0:T(8,128)(2,1)S(1)} %fusion.2), channel_id=1, source_target_pairs={{0,8},{1,9},{2,10},{3,11},{4,12},{5,13},{6,14},{7,15},{8,0},{9,1},... | collective-permute-start | bytes 933896 | tf_op jit(solution)/shard_map/ppermute | solution.py:1069
  110.8 5.3 %collective-permute-start.15 = (bf16[4,152,128]{2,1,0:T(8,128)(2,1)S(1)}, bf16[4,152,128]{2,1,0:T(8,128)(2,1)S(1)}, u32[]{:S(2)}, u32[]{:S(2)}) collective-permute-start(bf16[4,152,128]{2,1,0:T(8,128)(2,1)S(1)} %fusion.3), channel_id=1, source_target_pairs={{0,16},{1,17},{2,18},{3,19},{4,20},{5,21},{6,22},{7,23},{8,24},{9,... | collective-permute-start | bytes 466952 | tf_op jit(solution)/shard_map/ppermute | solution.py:1069
  111.4 5.3 %collective-permute-start.14 = (bf16[4,152,128]{2,1,0:T(8,128)(2,1)S(1)}, bf16[4,152,128]{2,1,0:T(8,128)(2,1)S(1)}, u32[]{:S(2)}, u32[]{:S(2)}) collective-permute-start(bf16[4,152,128]{2,1,0:T(8,128)(2,1)S(1)} %slice.120), channel_id=1, source_target_pairs={{0,8},{1,9},{2,10},{3,11},{4,12},{5,13},{6,14},{7,15},{8,0},{9,1},... | collective-permute-start | bytes 466952 | tf_op jit(solution)/shard_map/ppermute | solution.py:1069
  116.8 5.3 %collective-permute-start.16 = (bf16[304,128]{1,0:T(8,128)(2,1)S(1)}, bf16[304,128]{1,0:T(8,128)(2,1)S(1)}, u32[]{:S(2)}, u32[]{:S(2)}) collective-permute-start(bf16[304,128]{1,0:T(8,128)(2,1)S(1)} %get-tuple-element.65), channel_id=1, source_target_pairs={{0,2},{1,3},{2,0},{3,1},{4,6},{5,7},{6,4},{7,5},{8,10},{9,11},{10,... | collective-permute-start | bytes 233480 | tf_op jit(solution)/shard_map/ppermute | solution.py:1069
  117.7 6.3 %collective-permute-start.18 = (bf16[304,128]{1,0:T(8,128)(2,1)S(1)}, bf16[304,128]{1,0:T(8,128)(2,1)S(1)}, u32[]{:S(2)}, u32[]{:S(2)}) collective-permute-start(bf16[304,128]{1,0:T(8,128)(2,1)S(1)} %get-tuple-element.66), channel_id=1, source_target_pairs={{0,6},{1,7},{2,4},{3,5},{4,2},{5,3},{6,0},{7,1},{8,14},{9,15},{10,... | collective-permute-start | bytes 233480 | tf_op jit(solution)/shard_map/ppermute | solution.py:1069
  119.5 6.1 %collective-permute-start.17 = (bf16[304,128]{1,0:T(8,128)(2,1)S(1)}, bf16[304,128]{1,0:T(8,128)(2,1)S(1)}, u32[]{:S(2)}, u32[]{:S(2)}) collective-permute-start(bf16[304,128]{1,0:T(8,128)(2,1)S(1)} %get-tuple-element.67), channel_id=1, source_target_pairs={{0,4},{1,5},{2,6},{3,7},{4,0},{5,1},{6,2},{7,3},{8,12},{9,13},{10,... | collective-permute-start | bytes 233480 | tf_op jit(solution)/shard_map/ppermute | solution.py:1069
  (3 other events, 3.8 us)

commit v8 on v7

--- a/solution.py
+++ b/solution.py
@@ -1114,12 +1114,10 @@
     upper, lower = held[:, :cut], held[:, cut:]
     upper = jnp.concatenate([upper, swap(upper, next_top)], axis=0)
     lower = jnp.concatenate([lower, swap(lower, top)], axis=0)
-    if fused:
-        upper, lower, slots = lax.optimization_barrier((upper, lower, slots))
-        shifted, shifted_again = shift_call(flat_in, slots)
     parts = [upper, swap(upper, top), lower, swap(lower, next_top)]
     if fused:
-        parts, shifted, shifted_again = lax.optimization_barrier((parts, shifted, shifted_again))
+        _, slots = lax.optimization_barrier((parts, slots))
+        shifted, shifted_again = shift_call(flat_in, slots)
     parts = parts + [swap(part, order[0]) for part in parts]
     few = devices // 8
     plan = []

time: 127 us -> 126 us (level)
  local copies, waits for them, and re-layouts: 4.33 us -> 0.59 us
  waiting for transfers between devices: 25.3 us -> 28.5 us
    unnamed x16 -> x8, local copies, waits for them, and re-layouts: 3.76 us -> 0.02 us
    ppermute x19, waiting for transfers between devices: 25.3 us -> 28.5 us  [swap(): lax.ppermute(value, ('dp', 'space'), [(k, k ^ flip) for k in range(device...]
  transfers between devices with their start and end apart: 19 -> 19, of which waited for: 17 -> 13; matrix products, arithmetic and copies ran while one was open for 0% -> 0% of each run, Pallas kernels for 7% -> 7%
where the time goes in v8:
time: 126 us; the launch traced here: 125 us
  Pallas kernels  70.8 us (56%)
  waiting for transfers between devices  28.5 us (23%)
  starting transfers between devices  21.5 us (17%)
  other arithmetic  3.12 us (2%)
    pallas_call x5, Pallas kernels, call(): pl.pallas_call(kernel, grid_spec=spec, out_shape=[jax.ShapeDtypeStruct(sh...  70.8 us
    ppermute x19, waiting for transfers between devices, swap(): lax.ppermute(value, ('dp', 'space'), [(k, k ^ flip) for k in range(device...  28.5 us
    ppermute x19, starting transfers between devices, swap(): lax.ppermute(value, ('dp', 'space'), [(k, k ^ flip) for k in range(device...  21.5 us
  transfers between devices with their start and end apart: 19, of which 13 were waited for; matrix products, arithmetic and copies ran while one was open for 0% of the time, Pallas kernels for 7%

profile of v8, /device:TPU:0, one launch (start us, length us, event | category | flops | bytes accessed | tf_op | source)
XLA Modules:
  0.0 125.4 jit_solution(6057583239823238335)
XLA Ops:
  2.5 5.1 %collective-permute-start.2 = (bf16[1,304,128]{2,1,0:T(8,128)(2,1)S(1)}, bf16[1,304,128]{2,1,0:T(8,128)(2,1)S(1)}, u32[]{:S(2)}, u32[]{:S(2)}) collective-permute-start(bf16[1,304,128]{2,1,0:T(8,128)(2,1)S(1)} %select_bitcast_fusion), channel_id=1, source_target_pairs={{0,6},{1,7},{2,4},{3,5},{4,2},{5,3},{6,0},{7,1},{8,14},{9,15},{10,... | collective-permute-start | bytes 233480 | tf_op jit(solution)/shard_map/ppermute | solution.py:1069
  8.2 2.2 %collective-permute-done.2 = bf16[1,304,128]{2,1,0:T(8,128)(2,1)S(1)} collective-permute-done((bf16[1,304,128]{2,1,0:T(8,128)(2,1)S(1)}, bf16[1,304,128]{2,1,0:T(8,128)(2,1)S(1)}, u32[]{:S(2)}, u32[]{:S(2)}) %collective-permute-start.2) | collective-permute-done | bytes 77856 | tf_op jit(solution)/shard_map/ppermute | solution.py:1069
  10.5 3.7 %collective-permute-done.1 = bf16[1,304,128]{2,1,0:T(8,128)(2,1)S(1)} collective-permute-done((bf16[1,304,128]{2,1,0:T(8,128)(2,1)S(1)}, bf16[1,304,128]{2,1,0:T(8,128)(2,1)S(1)}, u32[]{:S(2)}, u32[]{:S(2)}) %collective-permute-start.1) | collective-permute-done | bytes 77856 | tf_op jit(solution)/shard_map/ppermute | solution.py:1069
  14.2 1.6 %collective-permute-start.3 = (bf16[4,152,128]{2,1,0:T(8,128)(2,1)S(1)}, bf16[4,152,128]{2,1,0:T(8,128)(2,1)S(1)}, u32[]{:S(2)}, u32[]{:S(2)}) collective-permute-start(bf16[4,152,128]{2,1,0:T(8,128)(2,1)S(1)} %get-tuple-element.53), channel_id=1, source_target_pairs={{0,8},{1,9},{2,10},{3,11},{4,12},{5,13},{6,14},{7,15},{8,0},{9,1},... | collective-permute-start | bytes 466952 | tf_op jit(solution)/shard_map/ppermute | solution.py:1069
  15.8 1.5 %collective-permute-start.5 = (bf16[4,152,128]{2,1,0:T(8,128)(2,1)S(1)}, bf16[4,152,128]{2,1,0:T(8,128)(2,1)S(1)}, u32[]{:S(2)}, u32[]{:S(2)}) collective-permute-start(bf16[4,152,128]{2,1,0:T(8,128)(2,1)S(1)} %get-tuple-element.52), channel_id=1, source_target_pairs={{0,16},{1,17},{2,18},{3,19},{4,20},{5,21},{6,22},{7,23},{8,24},{9,... | collective-permute-start | bytes 466952 | tf_op jit(solution)/shard_map/ppermute | solution.py:1069
  17.3 2.3 %collective-permute-done.3 = bf16[4,152,128]{2,1,0:T(8,128)(2,1)S(1)} collective-permute-done((bf16[4,152,128]{2,1,0:T(8,128)(2,1)S(1)}, bf16[4,152,128]{2,1,0:T(8,128)(2,1)S(1)}, u32[]{:S(2)}, u32[]{:S(2)}) %collective-permute-start.3) | collective-permute-done | bytes 155680 | tf_op jit(solution)/shard_map/ppermute | solution.py:1069
  19.6 1.8 %collective-permute-start.4 = (bf16[8,152,128]{2,1,0:T(8,128)(2,1)S(1)}, bf16[8,152,128]{2,1,0:T(8,128)(2,1)S(1)}, u32[]{:S(2)}, u32[]{:S(2)}) collective-permute-start(bf16[8,152,128]{2,1,0:T(8,128)(2,1)S(1)} %pad_maximum_fusion.2.refs_0_), channel_id=1, source_target_pairs={{0,16},{1,17},{2,18},{3,19},{4,20},{5,21},{6,22},{7,23},{8,24},{9,... | collective-permute-start | bytes 933896 | tf_op jit(solution)/shard_map/ppermute | solution.py:1069
  21.4 1.6 %collective-permute-start.6 = (bf16[8,152,128]{2,1,0:T(8,128)(2,1)S(1)}, bf16[8,152,128]{2,1,0:T(8,128)(2,1)S(1)}, u32[]{:S(2)}, u32[]{:S(2)}) collective-permute-start(bf16[8,152,128]{2,1,0:T(8,128)(2,1)S(1)} %pad_maximum_fusion.3.refs_2_), channel_id=1, source_target_pairs={{0,8},{1,9},{2,10},{3,11},{4,12},{5,13},{6,14},{7,15},{8,0},{9,1},... | collective-permute-start | bytes 933896 | tf_op jit(solution)/shard_map/ppermute | solution.py:1069
  23.9 3.7 %collective-permute-done.4.refs_1_ = bf16[8,152,128]{2,1,0:T(8,128)(2,1)S(1)} collective-permute-done((bf16[8,152,128]{2,1,0:T(8,128)(2,1)S(1)}, bf16[8,152,128]{2,1,0:T(8,128)(2,1)S(1)}, u32[]{:S(2)}, u32[]{:S(2)}) %collective-permute-start.4) | collective-permute-done | bytes 311328 | tf_op jit(solution)/shard_map/ppermute | solution.py:1069
  27.7 1.5 %collective-permute-done.6.refs_3_ = bf16[8,152,128]{2,1,0:T(8,128)(2,1)S(1)} collective-permute-done((bf16[8,152,128]{2,1,0:T(8,128)(2,1)S(1)}, bf16[8,152,128]{2,1,0:T(8,128)(2,1)S(1)}, u32[]{:S(2)}, u32[]{:S(2)}) %collective-permute-start.6) | collective-permute-done | bytes 311328 | tf_op jit(solution)/shard_map/ppermute | solution.py:1069
  29.6 3.4 %shift.1 = (bf16[192,4096]{1,0:T(8,128)(2,1)S(1)}, bf16[192,4096]{1,0:T(8,128)(2,1)S(1)}) custom-call(bf16[2304,192]{1,0:T(8,128)(2,1)S(1)} %bitcast.32, s32[1,2304]{1,0:T(1,128)S(1)} %reshape_squeeze.10.slots_ref.refs_9_.refs_0_), custom_call_target="tpu_custom_call" | custom-call | flops 3623878656 | bytes 4039680 | tf_op jit(solution)/shard_map/shift/pallas_call | solution.py:325
  33.1 18.2 %window_forward.1 = (f32[192,2304]{1,0:T(8,128)S(1)}, bf16[576,4096]{1,0:T(8,128)(2,1)}, bf16[192,4096]{1,0:T(8,128)(2,1)S(1)}, bf16[32,80,768]{2,1,0:T(8,128)(2...) custom-call(s32[1]{0:T(128)} %bitcast.me_ref, ...), custom_call_target="tpu_custom_call" | custom-call | flops 3623878656 | bytes 19133956 | tf_op jit(solution)/shard_map/window_forward/pallas_call | solution.py:325
  51.3 22.4 %column.1 = (bf16[2304,192]{1,0:T(8,128)(2,1)}, f32[192,2304]{1,0:T(8,128)S(1)}, bf16[192,2304]{1,0:T(8,128)(2,1)S(1)}, f32[3488,128]{1,0:T(8,128)S(1)}) custom-call(f32[3488,128]{1,0:T(8,128)S(1)} %get-tuple-element.28.dense, f32[192,2304]{1,0:T(8,128)S(1)} %get-tuple-element.29.x_ref, bf16[2304,192]{1,0:T(8,128)(2,1)S(1)} %bitcast.34, ...), custom_call_target="tpu_custom_call" | custom-call | flops 6794772480 | bytes 9774080 | tf_op jit(solution)/shard_map/column/pallas_call | solution.py:325
  73.7 21.5 %window_backward.1 = (bf16[192,2304]{1,0:T(8,128)(2,1)S(1)}, bf16[16,304,128]{2,1,0:T(8,128)(2,1)S(1)}, bf16[16,304,128]{2,1,0:T(8,128)(2,1)S(1)}) custom-call(s32[1]{0:T(128)} %bitcast.me_ref, s32[8,128]{1,0:T(8,128)S(1)} %get-tuple-element.31.band_ref, s32[1,2304]{1,0:T(1,128)S(1)} %reshape_squeeze.10.slots_ref.refs_9_.refs_0_, ...), custom_call_target="tpu_custom_call" | custom-call | flops 7247757312 | bytes 18248708 | tf_op jit(solution)/shard_map/window_backward/pallas_call | solution.py:325
  95.3 2.9 %collective-permute-done.11 = bf16[16,304,128]{2,1,0:T(8,128)(2,1)S(1)} collective-permute-done((bf16[16,304,128]{2,1,0:T(8,128)(2,1)S(1)}, bf16[16,304,128]{2,1,0:T(8,128)(2,1)S(1)}, u32[]{:S(2)}, u32[]{:S(2)}) %collective-permute-start.11) | collective-permute-done | bytes 1245216 | tf_op jit(solution)/shard_map/ppermute | solution.py:1069
  98.6 1.3 collective-permute-start.12
  100.7 5.4 %finish.1 = f32[2304,192]{1,0:T(8,128)} custom-call(bf16[192,2304]{1,0:T(8,128)(2,1)S(1)} %get-tuple-element.44.shift_ref, s32[1,2304]{1,0:T(1,128)S(1)} %reshape_squeeze.10.slots_ref.refs_9_.refs_0_, f32[192,2304]{1,0:T(8,128)S(1)} %get-tuple-element.45.after_ref), custom_call_target="tpu_custom_call" | custom-call | flops 2038431744 | bytes 4432896 | tf_op jit(solution)/shard_map/finish/pallas_call | solution.py:325
  106.1 2.0 %collective-permute-done.12 = bf16[8,152,128]{2,1,0:T(8,128)(2,1)S(1)} collective-permute-done((bf16[8,152,128]{2,1,0:T(8,128)(2,1)S(1)}, bf16[8,152,128]{2,1,0:T(8,128)(2,1)S(1)}, u32[]{:S(2)}, u32[]{:S(2)}) %collective-permute-start.12) | collective-permute-done | bytes 311328 | tf_op jit(solution)/shard_map/ppermute | solution.py:1069
  110.1 1.6 %collective-permute-start.14 = (bf16[4,152,128]{2,1,0:T(8,128)(2,1)S(1)}, bf16[4,152,128]{2,1,0:T(8,128)(2,1)S(1)}, u32[]{:S(2)}, u32[]{:S(2)}) collective-permute-start(bf16[4,152,128]{2,1,0:T(8,128)(2,1)S(1)} %slice.120), channel_id=1, source_target_pairs={{0,8},{1,9},{2,10},{3,11},{4,12},{5,13},{6,14},{7,15},{8,0},{9,1},... | collective-permute-start | bytes 466952 | tf_op jit(solution)/shard_map/ppermute | solution.py:1069
  111.6 2.8 %collective-permute-done.15 = bf16[4,152,128]{2,1,0:T(8,128)(2,1)S(1)} collective-permute-done((bf16[4,152,128]{2,1,0:T(8,128)(2,1)S(1)}, bf16[4,152,128]{2,1,0:T(8,128)(2,1)S(1)}, u32[]{:S(2)}, u32[]{:S(2)}) %collective-permute-start.15) | collective-permute-done | bytes 155680 | tf_op jit(solution)/shard_map/ppermute | solution.py:1069
  116.6 2.0 %collective-permute-start.18 = (bf16[304,128]{1,0:T(8,128)(2,1)S(1)}, bf16[304,128]{1,0:T(8,128)(2,1)S(1)}, u32[]{:S(2)}, u32[]{:S(2)}) collective-permute-start(bf16[304,128]{1,0:T(8,128)(2,1)S(1)} %get-tuple-element.50), channel_id=1, source_target_pairs={{0,6},{1,7},{2,4},{3,5},{4,2},{5,3},{6,0},{7,1},{8,14},{9,15},{10,... | collective-permute-start | bytes 233480 | tf_op jit(solution)/shard_map/ppermute | solution.py:1069
  119.1 1.8 %collective-permute-done.16 = bf16[304,128]{1,0:T(8,128)(2,1)S(1)} collective-permute-done((bf16[304,128]{1,0:T(8,128)(2,1)S(1)}, bf16[304,128]{1,0:T(8,128)(2,1)S(1)}, u32[]{:S(2)}, u32[]{:S(2)}) %collective-permute-start.16) | collective-permute-done | bytes 77856 | tf_op jit(solution)/shard_map/ppermute | solution.py:1069
  120.9 2.0 %collective-permute-done.18 = bf16[304,128]{1,0:T(8,128)(2,1)S(1)} collective-permute-done((bf16[304,128]{1,0:T(8,128)(2,1)S(1)}, bf16[304,128]{1,0:T(8,128)(2,1)S(1)}, u32[]{:S(2)}, u32[]{:S(2)}) %collective-permute-start.18) | collective-permute-done | bytes 77856 | tf_op jit(solution)/shard_map/ppermute | solution.py:1069
  122.9 1.8 %collective-permute-done.17 = bf16[304,128]{1,0:T(8,128)(2,1)S(1)} collective-permute-done((bf16[304,128]{1,0:T(8,128)(2,1)S(1)}, bf16[304,128]{1,0:T(8,128)(2,1)S(1)}, u32[]{:S(2)}, u32[]{:S(2)}) %collective-permute-start.17) | collective-permute-done | bytes 77856 | tf_op jit(solution)/shard_map/ppermute | solution.py:1069
  (56 shorter events, 10.7 us)
Async XLA Ops:
  0.6 22.3 %copy-start.3 = (s32[1,288]{1,0:T(1,128)S(1)}, s32[1,288]{1,0:T(1,128)}, u32[]{:S(2)}) copy-start(s32[1,288]{1,0:T(1,128)} %param.11) | copy-start | bytes 3460
  0.6 22.4 %copy-start.2 = (s32[1,8,1,288]{3,2,1,0:T(1,128)S(1)}, s32[1,8,1,288]{3,2,1,0:T(1,128)}, u32[]{:S(2)}) copy-start(s32[1,8,1,288]{3,2,1,0:T(1,128)} %param.9) | copy-start | bytes 27652
  1.3 28.3 %copy-start = (bf16[1,288,8,192]{3,2,1,0:T(8,128)(2,1)S(1)}, bf16[1,288,8,192]{3,2,1,0:T(8,128)(2,1)}, u32[]{:S(2)}) copy-start(bf16[1,288,8,192]{3,2,1,0:T(8,128)(2,1)} %param.6) | copy-start | bytes 2654212
  2.5 8.0 %collective-permute-start.2 = (bf16[1,304,128]{2,1,0:T(8,128)(2,1)S(1)}, bf16[1,304,128]{2,1,0:T(8,128)(2,1)S(1)}, u32[]{:S(2)}, u32[]{:S(2)}) collective-permute-start(bf16[1,304,128]{2,1,0:T(8,128)(2,1)S(1)} %select_bitcast_fusion), channel_id=1, source_target_pairs={{0,6},{1,7},{2,4},{3,5},{4,2},{5,3},{6,0},{7,1},{8,14},{9,15},{10,... | collective-permute-start | bytes 233480 | tf_op jit(solution)/shard_map/ppermute | solution.py:1069
  7.6 6.5 %collective-permute-start.1 = (bf16[1,304,128]{2,1,0:T(8,128)(2,1)S(1)}, bf16[1,304,128]{2,1,0:T(8,128)(2,1)S(1)}, u32[]{:S(2)}, u32[]{:S(2)}) collective-permute-start(bf16[1,304,128]{2,1,0:T(8,128)(2,1)S(1)} %select_bitcast_fusion), channel_id=1, source_target_pairs={{0,4},{1,5},{2,6},{3,7},{4,0},{5,1},{6,2},{7,3},{8,12},{9,13},{10,... | collective-permute-start | bytes 233480 | tf_op jit(solution)/shard_map/ppermute | solution.py:1069
  7.6 6.5 %collective-permute-start = (bf16[1,304,128]{2,1,0:T(8,128)(2,1)S(1)}, bf16[1,304,128]{2,1,0:T(8,128)(2,1)S(1)}, u32[]{:S(2)}, u32[]{:S(2)}) collective-permute-start(bf16[1,304,128]{2,1,0:T(8,128)(2,1)S(1)} %select_bitcast_fusion), channel_id=1, source_target_pairs={{0,2},{1,3},{2,0},{3,1},{4,6},{5,7},{6,4},{7,5},{8,10},{9,11},{10,... | collective-permute-start | bytes 233480 | tf_op jit(solution)/shard_map/ppermute | solution.py:1069
  14.2 5.4 %collective-permute-start.3 = (bf16[4,152,128]{2,1,0:T(8,128)(2,1)S(1)}, bf16[4,152,128]{2,1,0:T(8,128)(2,1)S(1)}, u32[]{:S(2)}, u32[]{:S(2)}) collective-permute-start(bf16[4,152,128]{2,1,0:T(8,128)(2,1)S(1)} %get-tuple-element.53), channel_id=1, source_target_pairs={{0,8},{1,9},{2,10},{3,11},{4,12},{5,13},{6,14},{7,15},{8,0},{9,1},... | collective-permute-start | bytes 466952 | tf_op jit(solution)/shard_map/ppermute | solution.py:1069
  15.8 5.6 %collective-permute-start.5 = (bf16[4,152,128]{2,1,0:T(8,128)(2,1)S(1)}, bf16[4,152,128]{2,1,0:T(8,128)(2,1)S(1)}, u32[]{:S(2)}, u32[]{:S(2)}) collective-permute-start(bf16[4,152,128]{2,1,0:T(8,128)(2,1)S(1)} %get-tuple-element.52), channel_id=1, source_target_pairs={{0,16},{1,17},{2,18},{3,19},{4,20},{5,21},{6,22},{7,23},{8,24},{9,... | collective-permute-start | bytes 466952 | tf_op jit(solution)/shard_map/ppermute | solution.py:1069
  19.6 8.1 %collective-permute-start.4 = (bf16[8,152,128]{2,1,0:T(8,128)(2,1)S(1)}, bf16[8,152,128]{2,1,0:T(8,128)(2,1)S(1)}, u32[]{:S(2)}, u32[]{:S(2)}) collective-permute-start(bf16[8,152,128]{2,1,0:T(8,128)(2,1)S(1)} %pad_maximum_fusion.2.refs_0_), channel_id=1, source_target_pairs={{0,16},{1,17},{2,18},{3,19},{4,20},{5,21},{6,22},{7,23},{8,24},{9,... | collective-permute-start | bytes 933896 | tf_op jit(solution)/shard_map/ppermute | solution.py:1069
  21.4 7.7 %collective-permute-start.6 = (bf16[8,152,128]{2,1,0:T(8,128)(2,1)S(1)}, bf16[8,152,128]{2,1,0:T(8,128)(2,1)S(1)}, u32[]{:S(2)}, u32[]{:S(2)}) collective-permute-start(bf16[8,152,128]{2,1,0:T(8,128)(2,1)S(1)} %pad_maximum_fusion.3.refs_2_), channel_id=1, source_target_pairs={{0,8},{1,9},{2,10},{3,11},{4,12},{5,13},{6,14},{7,15},{8,0},{9,1},... | collective-permute-start | bytes 933896 | tf_op jit(solution)/shard_map/ppermute | solution.py:1069
  23.4 9.7 %collective-permute-start.7 = (bf16[8,152,128]{2,1,0:T(8,128)(2,1)S(1)}, bf16[8,152,128]{2,1,0:T(8,128)(2,1)S(1)}, u32[]{:S(2)}, u32[]{:S(2)}) collective-permute-start(bf16[8,152,128]{2,1,0:T(8,128)(2,1)S(1)} %pad_maximum_fusion.2.refs_0_), channel_id=1, source_target_pairs={{0,1},{1,0},{2,3},{3,2},{4,5},{5,4},{6,7},{7,6},{8,9},{9,8},{10,11... | collective-permute-start | bytes 933896 | tf_op jit(solution)/shard_map/ppermute | solution.py:1069
  23.4 9.6 %collective-permute-start.9 = (bf16[8,152,128]{2,1,0:T(8,128)(2,1)S(1)}, bf16[8,152,128]{2,1,0:T(8,128)(2,1)S(1)}, u32[]{:S(2)}, u32[]{:S(2)}) collective-permute-start(bf16[8,152,128]{2,1,0:T(8,128)(2,1)S(1)} %pad_maximum_fusion.3.refs_2_), channel_id=1, source_target_pairs={{0,1},{1,0},{2,3},{3,2},{4,5},{5,4},{6,7},{7,6},{8,9},{9,8},{10,11... | collective-permute-start | bytes 933896 | tf_op jit(solution)/shard_map/ppermute | solution.py:1069
  29.1 4.0 %collective-permute-start.8 = (bf16[8,152,128]{2,1,0:T(8,128)(2,1)S(1)}, bf16[8,152,128]{2,1,0:T(8,128)(2,1)S(1)}, u32[]{:S(2)}, u32[]{:S(2)}) collective-permute-start(bf16[8,152,128]{2,1,0:T(8,128)(2,1)S(1)} %collective-permute-done.4.refs_1_), channel_id=1, source_target_pairs={{0,1},{1,0},{2,3},{3,2},{4,5},{5,4},{6,7},{7,6},{8,9},{9,8},{10,11... | collective-permute-start | bytes 933896 | tf_op jit(solution)/shard_map/ppermute | solution.py:1069
  29.1 4.0 %collective-permute-start.10 = (bf16[8,152,128]{2,1,0:T(8,128)(2,1)S(1)}, bf16[8,152,128]{2,1,0:T(8,128)(2,1)S(1)}, u32[]{:S(2)}, u32[]{:S(2)}) collective-permute-start(bf16[8,152,128]{2,1,0:T(8,128)(2,1)S(1)} %collective-permute-done.6.refs_3_), channel_id=1, source_target_pairs={{0,1},{1,0},{2,3},{3,2},{4,5},{5,4},{6,7},{7,6},{8,9},{9,8},{10,11... | collective-permute-start | bytes 933896 | tf_op jit(solution)/shard_map/ppermute | solution.py:1069
  33.1 18.2 %copy-start.1 = (bf16[1,288,8,192]{3,2,1,0:T(8,128)(2,1)S(1)}, bf16[1,288,8,192]{3,2,1,0:T(8,128)(2,1)}, u32[]{:S(2)}) copy-start(bf16[1,288,8,192]{3,2,1,0:T(8,128)(2,1)} %param.7) | copy-start | bytes 2654212
  95.2 3.0 %collective-permute-start.11 = (bf16[16,304,128]{2,1,0:T(8,128)(2,1)S(1)}, bf16[16,304,128]{2,1,0:T(8,128)(2,1)S(1)}, u32[]{:S(2)}, u32[]{:S(2)}) collective-permute-start(bf16[16,304,128]{2,1,0:T(8,128)(2,1)S(1)} %get-tuple-element.41), channel_id=1, source_target_pairs={{0,1},{1,0},{2,3},{3,2},{4,5},{5,4},{6,7},{7,6},{8,9},{9,8},{10,11... | collective-permute-start | bytes 3735560 | tf_op jit(solution)/shard_map/ppermute | solution.py:1069
  98.6 9.5 %collective-permute-start.12 = (bf16[8,152,128]{2,1,0:T(8,128)(2,1)S(1)}, bf16[8,152,128]{2,1,0:T(8,128)(2,1)S(1)}, u32[]{:S(2)}, u32[]{:S(2)}) collective-permute-start(bf16[8,152,128]{2,1,0:T(8,128)(2,1)S(1)} %slice.119), channel_id=1, source_target_pairs={{0,16},{1,17},{2,18},{3,19},{4,20},{5,21},{6,22},{7,23},{8,24},{9,... | collective-permute-start | bytes 933896 | tf_op jit(solution)/shard_map/ppermute | solution.py:1069
  99.9 9.2 %collective-permute-start.13 = (bf16[2,4,152,128]{3,2,1,0:T(8,128)(2,1)S(1)}, bf16[2,4,152,128]{3,2,1,0:T(8,128)(2,1)S(1)}, u32[]{:S(2)}, u32[]{:S(2)}) collective-permute-start(bf16[2,4,152,128]{3,2,1,0:T(8,128)(2,1)S(1)} %fusion.2), channel_id=1, source_target_pairs={{0,8},{1,9},{2,10},{3,11},{4,12},{5,13},{6,14},{7,15},{8,0},{9,1},... | collective-permute-start | bytes 933896 | tf_op jit(solution)/shard_map/ppermute | solution.py:1069
  109.2 5.3 %collective-permute-start.15 = (bf16[4,152,128]{2,1,0:T(8,128)(2,1)S(1)}, bf16[4,152,128]{2,1,0:T(8,128)(2,1)S(1)}, u32[]{:S(2)}, u32[]{:S(2)}) collective-permute-start(bf16[4,152,128]{2,1,0:T(8,128)(2,1)S(1)} %fusion.3), channel_id=1, source_target_pairs={{0,16},{1,17},{2,18},{3,19},{4,20},{5,21},{6,22},{7,23},{8,24},{9,... | collective-permute-start | bytes 466952 | tf_op jit(solution)/shard_map/ppermute | solution.py:1069
  110.1 5.3 %collective-permute-start.14 = (bf16[4,152,128]{2,1,0:T(8,128)(2,1)S(1)}, bf16[4,152,128]{2,1,0:T(8,128)(2,1)S(1)}, u32[]{:S(2)}, u32[]{:S(2)}) collective-permute-start(bf16[4,152,128]{2,1,0:T(8,128)(2,1)S(1)} %slice.120), channel_id=1, source_target_pairs={{0,8},{1,9},{2,10},{3,11},{4,12},{5,13},{6,14},{7,15},{8,0},{9,1},... | collective-permute-start | bytes 466952 | tf_op jit(solution)/shard_map/ppermute | solution.py:1069
  115.5 5.4 %collective-permute-start.16 = (bf16[304,128]{1,0:T(8,128)(2,1)S(1)}, bf16[304,128]{1,0:T(8,128)(2,1)S(1)}, u32[]{:S(2)}, u32[]{:S(2)}) collective-permute-start(bf16[304,128]{1,0:T(8,128)(2,1)S(1)} %get-tuple-element.49), channel_id=1, source_target_pairs={{0,2},{1,3},{2,0},{3,1},{4,6},{5,7},{6,4},{7,5},{8,10},{9,11},{10,... | collective-permute-start | bytes 233480 | tf_op jit(solution)/shard_map/ppermute | solution.py:1069
  116.6 6.3 %collective-permute-start.18 = (bf16[304,128]{1,0:T(8,128)(2,1)S(1)}, bf16[304,128]{1,0:T(8,128)(2,1)S(1)}, u32[]{:S(2)}, u32[]{:S(2)}) collective-permute-start(bf16[304,128]{1,0:T(8,128)(2,1)S(1)} %get-tuple-element.50), channel_id=1, source_target_pairs={{0,6},{1,7},{2,4},{3,5},{4,2},{5,3},{6,0},{7,1},{8,14},{9,15},{10,... | collective-permute-start | bytes 233480 | tf_op jit(solution)/shard_map/ppermute | solution.py:1069
  118.6 6.1 %collective-permute-start.17 = (bf16[304,128]{1,0:T(8,128)(2,1)S(1)}, bf16[304,128]{1,0:T(8,128)(2,1)S(1)}, u32[]{:S(2)}, u32[]{:S(2)}) collective-permute-start(bf16[304,128]{1,0:T(8,128)(2,1)S(1)} %get-tuple-element.51), channel_id=1, source_target_pairs={{0,4},{1,5},{2,6},{3,7},{4,0},{5,1},{6,2},{7,3},{8,12},{9,13},{10,... | collective-permute-start | bytes 233480 | tf_op jit(solution)/shard_map/ppermute | solution.py:1069
